TPU v7x, 32 devices: a whole 2x2x4 slice. The times are simulated.
32 devices in a mesh: ctx: 16 (over z, y, x), vid: 2 (over core).
Axes of the slice: x: 2, y: 2, z: 4, core: 2. Of those that a mesh axis runs over, the one named last changes fastest.
Arguments:
- features: bfloat16 [2, 32, 8, 32, 256], P('vid', 'ctx'), may hold values from -6 to 6
- grad_out: bfloat16 [2, 32, 8, 32, 128], P('vid', 'ctx'), may hold values from -6 to 6
- mean_saved: float32 [2, 32], P('vid'), may hold values from -3 to 3
- rstd_saved: float32 [2, 32], P('vid'), may hold values from 0.5 to 2
- latent: float32 [2, 8, 16, 16], P('vid'), may hold values from -6 to 6
- gamma: float32 [256], replicated, may hold values from 0.5 to 1.5
- beta: float32 [256], replicated, may hold values from -3 to 3
- w_scale: float32 [16, 256], replicated, may hold values from -1.5 to 1.5
- b_scale: float32 [256], replicated, may hold values from -3 to 3
- w_shift: float32 [16, 256], replicated, may hold values from -1.5 to 1.5
- b_shift: float32 [256], replicated, may hold values from -3 to 3
- kernel: bfloat16 [6912, 128], replicated, may hold values from -0.078125 to 0.078125
Outputs:
- features_grad: bfloat16 [2, 32, 8, 32, 256], P('vid', 'ctx')
- kernel_grad: float32 [6912, 128], P('ctx', 'vid')
- mod_grads: float32 [2, 16, 256], replicated
- vector_grads: float32 [4, 256], replicated
- latent_grad: float32 [2, 16, 16, 8], P('vid', 'ctx')
All inputs are finite; a program needn't handle non-finite values.
Results may differ from a plain program's by a relative error of at most 0.0029.
Values may be sent and summed in bfloat16 or wider, within the bound.
No kernel may reach another device: no remote copies, remote signals or barrier semaphores. Data moves between devices by JAX's collectives and lax.ppermute only.
A program may use at most 64 MiB of HBM per device.

v0:
```python
import functools
import math

import jax
import jax.numpy as jnp
from jax import lax
from jax.experimental import pallas as pl
from jax.experimental.pallas import tpu as pltpu
from jax.sharding import PartitionSpec as P

NEAR = 4
CELL = 4
TAPS = 3
TILE = 16

f32 = jnp.float32
bf16 = jnp.bfloat16
dot = functools.partial(lax.dot_general, preferred_element_type=f32)
exact = functools.partial(dot, precision=lax.Precision.HIGHEST)
ROWS_COLS = (((1,), (0,)), ((), ()))
ROWS_ROWS = (((1,), (1,)), ((), ()))
COLS_COLS = (((0,), (0,)), ((), ()))


def call(body, outs, scratch=(), name=None, far_args=(), keep=(), aliases=None, work=1000):
    outs = list(outs)
    lost = [k for k in far_args if k not in keep]

    def run(*args):
        args = [pltpu.with_memory_space_constraint(arg, pltpu.HBM) if k in far_args else arg
                for k, arg in enumerate(args)]

        def full(*refs):
            refs = list(refs)
            sems = refs.pop()
            buffers = {k: refs.pop() for k in lost[::-1]}
            first = len(args) + len(outs)
            buffers.update({k: refs.pop(first) for k in keep})
            moves = [pltpu.make_async_copy(refs[k], buffers[k], sems.at[at]) for at, k in enumerate(far_args)]
            for move in moves:
                move.start()
            for k in far_args:
                refs[k] = buffers[k]
            for move in moves:
                move.wait()
            body(*refs)

        return pl.pallas_call(
            full if far_args else body,
            out_shape=outs + [shaped(args[k].shape, args[k].dtype) for k in keep],
            in_specs=[pl.BlockSpec(memory_space=pltpu.HBM if k in far_args else pltpu.VMEM) for k in range(len(args))],
            scratch_shapes=list(scratch) + [pltpu.VMEM(args[k].shape, args[k].dtype) for k in lost]
            + ([pltpu.SemaphoreType.DMA((len(far_args),))] if far_args else []),
            input_output_aliases=aliases or {},
            name=name,
            cost_estimate=pl.CostEstimate(flops=work, bytes_accessed=work, transcendentals=0),
            compiler_params=pltpu.CompilerParams(vmem_limit_bytes=50 * 2**20),
        )(*args)

    return run


def halves(value):
    top = value.astype(bf16)
    return top, (value - top.astype(f32)).astype(bf16)


def shaped(shape, kind=f32):
    return jax.ShapeDtypeStruct(shape, kind)


def cell_matrix(height, width, cells):
    pixel = lax.broadcasted_iota(jnp.int32, (height * width, cells), 0)
    cell = lax.broadcasted_iota(jnp.int32, (height * width, cells), 1)
    place = (pixel // width) // CELL * (width // CELL) + pixel % width // CELL
    return jnp.where(place == cell, 1.0, 0.0).astype(f32)


def modulate_body(frames, height, width, feats, mean, rstd, latent, gamma, beta, ws, bs, wt, bt, grads, weights, *refs):
    acts, (slope, normed_out, gain_out, tab_out, partial, shifted) = refs[:frames], refs[frames:]
    chans = feats.shape[1]
    groups = mean.shape[1]
    pixels = height * width
    lat = latent[0, lax.axis_index("ctx") * frames // CELL]
    group = lax.broadcasted_iota(jnp.int32, (groups, chans), 0)
    chan = lax.broadcasted_iota(jnp.int32, (groups, chans), 1)
    member = jnp.where(chan // (chans // groups) == group, 1.0, 0.0).astype(f32)
    mean_chan = exact(mean[...], member, ROWS_COLS)
    rstd_chan = exact(rstd[...], member, ROWS_COLS)
    scale_tab = exact(lat, ws[...], COLS_COLS) + bs[...]
    shift_tab = exact(lat, wt[...], COLS_COLS) + bt[...]
    tab_out[...] = scale_tab
    cells = cell_matrix(height, width, lat.shape[1])
    scale_map = exact(cells, scale_tab, ROWS_COLS)
    shift_map = exact(cells, shift_tab, ROWS_COLS)
    gain_out[...] = scale_map * (gamma[...] * rstd_chan)
    for frame in range(frames):
        at = pl.ds(frame * pixels, pixels)
        normed = (feats[at, :].astype(f32) - mean_chan) * rstd_chan
        modulated = (normed * gamma[...] + beta[...]) * scale_map + shift_map
        squashed = jax.nn.sigmoid(modulated)
        normed_out[at, :] = normed
        slope[at, :] = squashed * (1.0 + modulated * (1.0 - squashed))
        acts[frame][...] = (modulated * squashed).T.astype(bf16)
    conv_own_body(frames, height, width, grads, weights, partial, shifted)


def column_shifts(value, width):
    column = lax.broadcasted_iota(jnp.int32, value.shape, 0) % width
    rows = value.shape[0]
    return (
        jnp.where(column == width - 1, 0.0, pltpu.roll(value, rows - 1, 0)),
        value,
        jnp.where(column == 0, 0.0, pltpu.roll(value, 1, 0)),
    )


def clear_borders(padded, width):
    lead = padded.shape[:-2]
    length, lanes = padded.shape[-2:]
    edge = jnp.zeros(lead + (width, lanes), padded.dtype)
    every = (slice(None),) * len(lead)
    padded[every + (slice(0, width),)] = edge
    padded[every + (slice(length - width, length),)] = edge


def put_shifts(shifted, source, frames, pixels, width):
    clear_borders(shifted, width)
    for col, value in enumerate(column_shifts(source[...].astype(f32), width)):
        for frame in range(frames):
            shifted[col, frame, width:width + pixels] = value[frame * pixels:(frame + 1) * pixels].astype(bf16)


def taps_of(weights, step, chans):
    return jnp.concatenate(
        [weights[(step * TAPS * TAPS + k) * chans:(step * TAPS * TAPS + k + 1) * chans, :]
         for k in range(TAPS * TAPS)], axis=1)


def shifted_rows(shifted, frame_list, pixels, width):
    def window(frame, row, col):
        start = (TAPS - 1 - row) * width
        return shifted[col, frame, start:start + pixels]

    return jnp.concatenate(
        [jnp.concatenate([window(frame, k // TAPS, k % TAPS) for k in range(TAPS * TAPS)], axis=1)
         for frame in frame_list], axis=0)


def add_rows(total, term, first):
    if first == 0 and term.shape[0] == total.shape[0]:
        total[...] += term
    else:
        total[first:first + term.shape[0]] += term


def conv_own_body(frames, height, width, grads, weights, total, shifted):
    pixels = height * width
    chans = total.shape[1]
    put_shifts(shifted, grads, frames, pixels, width)
    total[...] = jnp.zeros_like(total)
    for step in range(TAPS):
        pairs = [(t, t + TAPS - 1 - step) for t in range(frames) if t + TAPS - 1 - step < frames]
        if pairs:
            rows = shifted_rows(shifted, [frame for _, frame in pairs], pixels, width)
            add_rows(total, dot(rows, taps_of(weights, step, chans), ROWS_ROWS), pairs[0][0] * pixels)

    @pl.when(lax.axis_index("ctx") == 0)
    def _():
        for step in range(TAPS - 1):
            for frame in range(TAPS - 1 - step):
                rows = shifted_rows(shifted, [frame], pixels, width)
                add_rows(total, dot(rows, taps_of(weights, step, chans), ROWS_ROWS), 0)


def input_grad_body(frames, height, width, beyond, weights, partial, slope, normed, gain, tab, latent,
                    ws, wt, gamma, beta, feats_grad, small, lat_own, lat_far, shifted, total):
    pixels = height * width
    chans = gain.shape[1]
    device = lax.axis_index("ctx")
    put_shifts(shifted, beyond, frames, pixels, width)
    total[...] = partial[...]
    for step in range(TAPS):
        pairs = [(t, t + TAPS - 1 - step - frames) for t in range(frames) if t + TAPS - 1 - step >= frames]
        if pairs:
            rows = shifted_rows(shifted, [frame for _, frame in pairs], pixels, width)
            add_rows(total, dot(rows, taps_of(weights, step, chans), ROWS_ROWS), pairs[0][0] * pixels)

    pooled_shift = jnp.zeros((pixels, chans), f32)
    pooled_norm = jnp.zeros((pixels, chans), f32)
    for frame in range(frames):
        at = pl.ds(frame * pixels, pixels)
        pre = total[at, :] * slope[at, :]
        feats_grad[at, :] = (pre * gain[...]).astype(bf16)
        pooled_shift += pre
        pooled_norm += pre * normed[at, :]
    lat = latent[0, device * frames // CELL]
    depth, length = lat.shape
    cells = cell_matrix(height, width, length)
    shift_pool = exact(cells, pooled_shift, COLS_COLS)
    norm_pool = exact(cells, pooled_norm, COLS_COLS)
    scale_pool = norm_pool * gamma[...] + shift_pool * beta[...]
    parts = [exact(lat, scale_pool, ROWS_COLS), exact(lat, shift_pool, ROWS_COLS)]
    for field in (norm_pool * tab[...], shift_pool * tab[...], scale_pool, shift_pool):
        parts.append(jnp.sum(field, axis=0, keepdims=True))
    lanes = small.shape[1]
    small[small.shape[0] - TILE:] = jnp.zeros((TILE, lanes), f32)
    at = 0
    for k in range(chans // lanes):
        for part in parts:
            small[at:at + part.shape[0]] = part[:, k * lanes:(k + 1) * lanes]
            at += part.shape[0]
    latent_sum = exact(scale_pool, ws[...], ROWS_ROWS) + exact(shift_pool, wt[...], ROWS_ROWS)
    first, second = latent_sum[:length // 2], latent_sum[length // 2:]
    even = device % 2 == 0
    lat_own[...] = jnp.where(even, first, second)
    lat_far[...] = jnp.where(even, second, first)


class FilterParts:
    def __init__(self, frames, height, width, videos, near, piece, packs, blocks, lanes, chans):
        self.frames, self.pixels, self.width, self.videos, self.near = frames, height * width, width, videos, near
        self.piece, self.packs, self.blocks, self.lanes, self.chans = piece, packs, blocks, lanes, chans
        self.cols = lanes // videos
        self.per = min(videos, TAPS)
        self.banks = -(-TAPS // self.per)
        self.slots = [(row, bank) for row in range(TAPS) for bank in range(self.banks)]
        self.rows = TAPS**3 * chans // (blocks.shape[0] * near)

    def pack(self, sources):
        clear_borders(self.packs, self.width)
        lane = lax.broadcasted_iota(jnp.int32, (1, self.lanes), 1)
        turn = lax.rem(self.lanes - lax.axis_index("vid") * self.cols, self.lanes)
        for video, source in enumerate(sources):
            moved = column_shifts(pltpu.roll(source[...].astype(f32), turn, 1), self.width)
            for bank in range(self.banks):
                packed = moved[bank * self.per]
                for k in range(1, min(self.per, TAPS - bank * self.per)):
                    other = pltpu.roll(moved[bank * self.per + k], k * self.cols, 1)
                    packed = jnp.where(lane >= k * self.cols, other, packed)
                packed = packed.astype(bf16)
                for frame in range(self.frames):
                    self.packs[video, bank, frame, self.width:self.width + self.pixels] = (
                        packed[frame * self.pixels:(frame + 1) * self.pixels])

    def product(self, acts, pairs):
        def window(video, frame, row, bank):
            start = (TAPS - 1 - row) * self.width
            return self.packs[video, bank, frame, start:start + self.pixels]

        left = jnp.concatenate(
            [acts[t * self.videos + video][...] for video in range(self.videos) for t, _ in pairs], axis=1)
        right = jnp.concatenate(
            [jnp.concatenate([window(video, frame, row, bank) for row, bank in self.slots], axis=1)
             for video in range(self.videos) for _, frame in pairs], axis=0)
        return dot(left, right, ROWS_COLS)

    def put(self, step, result, add):
        for place, (row, bank) in enumerate(self.slots):
            tile = None if result is None else result[:, place * self.lanes:(place + 1) * self.lanes]
            for k in range(min(self.per, TAPS - bank * self.per)):
                tap = (step * TAPS + row) * TAPS + bank * self.per + k
                done = 0
                while done < self.chans:
                    index = tap * self.chans + done
                    owner, inside = index // self.rows, index % self.rows
                    part, at = inside // self.piece, inside % self.piece
                    length = min(self.chans - done, self.rows - inside, self.piece - at)
                    low, high = part * self.cols, (part + 1) * self.cols
                    dest = self.blocks.at[owner // self.near, owner % self.near, at:at + length, low:high]
                    if tile is None:
                        dest[...] = jnp.zeros((length, self.cols), f32)
                    else:
                        value = tile[done:done + length]
                        turn = (part - k) * self.cols % self.lanes
                        if turn:
                            value = pltpu.roll(value, turn, 1)
                        value = value[:, low:high]
                        dest[...] = dest[...] + value if add else value
                    done += length


def filter_own_body(frames, height, width, videos, near, piece, *refs):
    acts, refs = refs[:frames * videos], refs[frames * videos:]
    grads, (_, blocks, packs) = refs[:videos], refs[videos:]
    parts = FilterParts(frames, height, width, videos, near, piece, packs, blocks, grads[0].shape[1], acts[0].shape[0])
    parts.pack(grads)
    far, lanes = blocks.shape[0], blocks.shape[3]
    first = lax.axis_index("ctx") == 0
    if piece * videos > parts.rows:
        blocks[:, :, piece - TILE:] = jnp.zeros((far, near, TILE, lanes), f32)
    for step in range(TAPS):
        pairs = [(t, t + TAPS - 1 - step) for t in range(frames) if t + TAPS - 1 - step < frames]
        parts.put(step, parts.product(acts, pairs) if pairs else None, False)
        if step < TAPS - 1:
            @pl.when(first)
            def _(step=step):
                extra = [parts.product(acts, [(0, frame)]) for frame in range(TAPS - 1 - step)]
                parts.put(step, functools.reduce(lambda a, b: a + b, extra), True)


def filter_grad_body(frames, height, width, videos, near, piece, *refs):
    acts, refs = refs[:frames * videos], refs[frames * videos:]
    beyond, refs = refs[:videos], refs[videos + 2:]
    blocks, own_far, own_line, line_send, *sends, packs = refs
    parts = FilterParts(frames, height, width, videos, near, piece, packs, blocks, beyond[0].shape[1], acts[0].shape[0])
    parts.pack(beyond)
    far = blocks.shape[0]
    for step in range(TAPS):
        pairs = [(t, t + TAPS - 1 - step - frames) for t in range(frames) if t + TAPS - 1 - step >= frames]
        if pairs:
            parts.put(step, parts.product(acts, pairs), True)
    device = lax.axis_index("ctx")
    line, place = device // near, device % near
    own_line[...] = blocks[line]
    for k in range(near):
        line_send[k * piece:(k + 1) * piece] = blocks[line ^ 1, k].astype(bf16)
    for k in range(far - 2):
        own_far[k] = blocks[line ^ (k + 2), place]
        for turn, send in enumerate(sends, 1):
            send[k * piece:(k + 1) * piece] = blocks[line ^ (k + 2), place ^ turn].astype(bf16)


def first_sum_body(near, far, videos, *refs):
    own_far, own_line, line_got, refs = refs[0], refs[1], refs[2], refs[3:]
    plane_got, refs = refs[:near - 1][::-1], refs[near - 1:]
    smalls, lat_far, refs = refs[:videos], refs[videos], refs[videos + 1:]
    kept, small_out, refs = refs[0], refs[1], refs[2:]
    plane_sends, line_sends, total = refs[:near - 1], refs[near - 1:-1], refs[-1]
    piece = own_line.shape[1]
    count = smalls[0].shape[0]
    place = lax.axis_index("ctx") % near
    for k, send in enumerate(line_sends):
        send[...] = functools.reduce(
            lambda a, b: a + b[k * piece:(k + 1) * piece].astype(f32), plane_got, own_far[k]).astype(bf16)
    for k in range(near):
        total[k] = own_line[k] + line_got[k * piece:(k + 1) * piece].astype(f32)
    kept[...] = total[place]
    summed = functools.reduce(lambda a, b: a + b, [ref[...] for ref in smalls])
    small_out[...] = summed
    top, rest = halves(summed)
    lat_top, lat_rest = halves(lat_far[...])
    cells, depth = lat_top.shape
    at = piece + 2 * count
    for turn, send in enumerate(plane_sends, 1):
        send[0:piece] = total[place ^ turn].astype(bf16)
        send[piece:piece + count] = top
        send[piece + count:at] = rest
        send[at:at + cells, :depth] = lat_top
        send[at + cells:at + 2 * cells, :depth] = lat_rest


def last_sum_body(near, far, *refs):
    kept, small, lat_own, refs = refs[0], refs[1], refs[2], refs[3:]
    line_got, plane_got, refs = refs[:far - 2], refs[far - 2:near + far - 3][::-1], refs[near + far - 3:]
    filter_grad, mod_grads, vector_grads, latent_grad = refs
    piece, lanes = kept.shape
    count = small.shape[0]

    def joined(ref, start, length):
        return ref[start:start + length].astype(f32) + ref[start + length:start + 2 * length].astype(f32)

    total = functools.reduce(lambda a, b: a + b[0:piece].astype(f32), plane_got + line_got, kept[...])
    cols, rows = filter_grad.shape
    turned = total.T
    for part in range(lanes // cols):
        first, last = part * piece, min(rows, (part + 1) * piece)
        if first < last:
            filter_grad[:, first:last] = turned[part * cols:(part + 1) * cols, :last - first]
    summed = functools.reduce(lambda a, b: a + joined(b, piece, count), plane_got, small[...])
    split, length = mod_grads.shape[0], mod_grads.shape[0] + vector_grads.shape[0]
    for k in range(mod_grads.shape[1] // lanes):
        mod_grads[:, k * lanes:(k + 1) * lanes] = summed[k * length:k * length + split]
        vector_grads[:, k * lanes:(k + 1) * lanes] = summed[k * length + split:(k + 1) * length]
    cells, depth = lat_own.shape
    latent_grad[...] = lat_own[...] + joined(plane_got[0], piece + 2 * count, cells)[:, :depth]


def local(features, grad_out, mean, rstd, latent, gamma, beta, ws, bs, wt, bt, kernel):
    _, frames, height, width, chans = features.shape
    outs = grad_out.shape[-1]
    depth, length = latent.shape[2:]
    count, videos = lax.axis_size("ctx"), lax.axis_size("vid")
    near = math.gcd(count, NEAR)
    far = count // near
    pixels = height * width
    size = frames * pixels
    rows, cols = TAPS**3 * chans // count, outs // videos
    piece = -(-rows // (TILE * videos)) * TILE
    gamma, beta, bs, bt = (value.reshape(1, chans) for value in (gamma, beta, bs, bt))
    feats = features.reshape(size, chans)
    grads = grad_out.reshape(size, outs)

    def along_ctx(value, target):
        return lax.ppermute(value, "ctx", [(s, target(s)) for s in range(count)])

    def others(value):
        return [value] + [
            lax.ppermute(value, "vid", [(s, (s + turn) % videos) for s in range(videos)])
            for turn in range(1, videos)]

    def plane_got(values):
        got = {turn: along_ctx(values[turn - 1], lambda s: s ^ turn) for turn in range(near - 1, 0, -1)}
        return [got[turn] for turn in range(1, near)]

    def line_got(values, first):
        turns = range(first, first + len(values))
        got = {turn: along_ctx(values[turn - first], lambda s: s ^ (turn * near)) for turn in reversed(turns)}
        return [got[turn] for turn in turns]

    beyond = lax.ppermute(grads, "ctx", [(s, s - 1) for s in range(1, count)])
    shifts = pltpu.VMEM((TAPS, frames, (height + 2) * width, outs), bf16)
    *acts, slope, normed, gain, tab, partial, latent, gamma, beta, ws, wt, grads_near, kernel = call(
        functools.partial(modulate_body, frames, height, width),
        [shaped((chans, pixels), bf16)] * frames
        + [shaped((size, chans)), shaped((size, chans)), shaped((pixels, chans)),
         shaped((length, chans)), shaped((size, chans))],
        (shifts,),
        name="modulate",
        far_args=tuple(range(12)),
        keep=(3, 4, 5, 6, 8, 10, 11),
    )(feats, mean, rstd, latent, gamma, beta, ws, bs, wt, bt, grads, kernel)
    acts_all = [value for act in acts for value in others(act)]
    grads_all = others(grads_near)
    beyond_all = others(beyond)
    cells = length // 2
    count_small = -(-(2 * depth + 4) * (chans // outs) // TILE) * TILE
    feats_grad, small, lat_own, lat_far = call(
        functools.partial(input_grad_body, frames, height, width),
        (shaped((size, chans), bf16), shaped((count_small, outs)), shaped((cells, depth)), shaped((cells, depth))),
        (shifts, pltpu.VMEM((size, chans), f32)),
        name="input_grad",
        work=2 * size * TAPS**3 * chans * outs,
    )(beyond, kernel, partial, slope, normed, gain, tab, latent, ws, wt, gamma, beta)
    banks = -(-TAPS // min(videos, TAPS))
    packs = pltpu.VMEM((videos, banks, frames, (height + 2) * width, outs), bf16)
    blocks, = call(
        functools.partial(filter_own_body, frames, height, width, videos, near, piece),
        (shaped((far, near, piece, outs)),),
        (packs,),
        name="filter_own",
    )(*acts_all, *grads_all, lat_far)
    got, blocks = lax.optimization_barrier((along_ctx(small, lambda s: s ^ near), blocks))
    small = small + got
    blocks, own_far, own_line, line_send, *plane_sends = call(
        functools.partial(filter_grad_body, frames, height, width, videos, near, piece),
        [shaped(blocks.shape), shaped((far - 2, piece, outs)), shaped((near, piece, outs)),
         shaped((near * piece, outs), bf16)]
        + [shaped(((far - 2) * piece, outs), bf16)] * (near - 1),
        (packs,),
        name="filter_grad",
        aliases={(frames + 1) * videos: 0},
    )(*acts_all, *beyond_all, blocks, small)
    step = 2
    while step < far:
        got = along_ctx(small, lambda s: s ^ (step * near))
        got, line_send, *plane_sends = lax.optimization_barrier((got, line_send, *plane_sends))
        small = small + got
        step *= 2
    extra = 2 * count_small + -(-2 * cells // TILE) * TILE
    line_in = line_got([line_send], 1)
    plane_in = plane_got(plane_sends)
    kept, small, *sends = call(
        functools.partial(first_sum_body, near, far, videos),
        [shaped((piece, outs)), shaped((count_small, outs))]
        + [shaped((piece + extra, outs), bf16)] * (near - 1) + [shaped((piece, outs), bf16)] * (far - 2),
        (pltpu.VMEM((near, piece, outs), f32),),
        name="first_sum",
    )(own_far, own_line, *line_in, *plane_in[::-1], *others(small), lat_far)
    line_in = line_got(sends[near - 1:], 2)
    plane_in = plane_got(sends[:near - 1])
    filter_grad, mod_grads, vector_grads, latent_grad = call(
        functools.partial(last_sum_body, near, far),
        (shaped((cols, rows)), shaped((2 * depth, chans)), shaped((4, chans)), shaped((cells, depth))),
        name="last_sum",
    )(kept, small, lat_own, *line_in[::-1], *plane_in[::-1])
    return (
        feats_grad.reshape(features.shape),
        filter_grad.T,
        mod_grads.reshape(2, depth, chans),
        vector_grads,
        latent_grad.T[None, None],
    )


def solution(mesh):
    split = P("vid", "ctx", None, None, None)
    return jax.shard_map(
        local,
        mesh=mesh,
        in_specs=(split, split, P("vid", None), P("vid", None), P("vid", None, None, None)) + (P(),) * 7,
        out_specs=(split, P("ctx", "vid"), P(), P(), P("vid", "ctx", None, None)),
        check_vma=False,
    )
```

profile of v0, /device:TPU:0, one launch (start us, length us, event | category | flops | bytes accessed | tf_op | source)
XLA Modules:
  0.0 44.2 jit_solution(13024576277110767673)
XLA Ops:
  0.6 1.3 %collective-permute-start = (bf16[512,128]{1,0:T(8,128)(2,1)}, bf16[512,128]{1,0:T(8,128)(2,1)S(1)}, u32[]{:S(2)}, u32[]{:S(2)}) collective-permute-start(bf16[512,128]{1,0:T(8,128)(2,1)} %bitcast.13), channel_id=1, source_target_pairs={{2,0},{4,2},{6,4},{8,6},{10,8},{12,10},{14,12},{16,14},{18,16},{20... | collective-permute-start | bytes 393224 | tf_op jit(solution)/shard_map/ppermute | solution.py:411
  1.9 4.1 %modulate.1 = (bf16[256,256]{1,0:T(8,128)(2,1)S(1)}, bf16[256,256]{1,0:T(8,128)(2,1)S(1)}, f32[512,256]{1,0:T(8,128)S(1)}, f32[512,256]{1,0:T(8,128)S(1)}, f32[2...) custom-call(bf16[512,256]{1,0:T(8,128)(2,1)} %bitcast.12, ...), custom_call_target="tpu_custom_call" | custom-call | flops 1000 | bytes 1000 | tf_op jit(solution)/shard_map/modulate/pallas_call | solution.py:48
  6.1 0.5 %collective-permute-start.1 = (bf16[256,256]{1,0:T(8,128)(2,1)S(1)}, bf16[256,256]{1,0:T(8,128)(2,1)S(1)}, u32[]{:S(2)}, u32[]{:S(2)}) collective-permute-start(bf16[256,256]{1,0:T(8,128)(2,1)S(1)} %get-tuple-element.59.refs_0_), channel_id=1, source_target_pairs={{0,1},{1,0},{2,3},{3,2},{4,5},{5,4},{6,7},{7,6},{8,9},{9,8},{10,11... | collective-permute-start | bytes 393224 | tf_op jit(solution)/shard_map/ppermute | solution.py:399
  6.6 0.1 collective-permute-start.2
  6.7 0.4 collective-permute-start.5
  7.1 2.1 %collective-permute-done.beyond.refs_4_ = bf16[512,128]{1,0:T(8,128)(2,1)S(1)} collective-permute-done((bf16[512,128]{1,0:T(8,128)(2,1)}, bf16[512,128]{1,0:T(8,128)(2,1)S(1)}, u32[]{:S(2)}, u32[]{:S(2)}) %collective-permute-start) | collective-permute-done | bytes 131104 | tf_op jit(solution)/shard_map/ppermute | solution.py:411
  9.2 0.0 collective-permute-start.3
  9.2 2.1 %input_grad.1 = (bf16[512,256]{1,0:T(8,128)(2,1)}, f32[80,128]{1,0:T(8,128)S(1)}, f32[8,16]{1,0:T(8,128)S(1)}, f32[8,16]{1,0:T(8,128)S(1)}) custom-call(bf16[512,128]{1,0:T(8,128)(2,1)S(1)} %collective-permute-done.beyond.refs_4_, bf16[6912,128]{1,0:T(8,128)(2,1)S(1)} %get-tuple-element.47.weights, f32[512,256]{1,0:T(8,128)S(1)} %get-tuple-element.48.partial, ...), custom_call_target="tpu_custom_call" | custom-call | flops 905969664 | bytes 905969664 | tf_op jit(solution)/shard_map/input_grad/pallas_call | solution.py:48
  11.3 3.3 %collective-permute-start.4 = (f32[80,128]{1,0:T(8,128)S(1)}, f32[80,128]{1,0:T(8,128)S(1)}, u32[]{:S(2)}, u32[]{:S(2)}) collective-permute-start(f32[80,128]{1,0:T(8,128)S(1)} %get-tuple-element.61), channel_id=1, source_target_pairs={{0,8},{2,10},{4,12},{6,14},{8,0},{10,2},{12,4},{14,6},{16,24},{18,... | collective-permute-start | bytes 122888 | tf_op jit(solution)/shard_map/ppermute | solution.py:395
  14.6 0.0 collective-permute-done.5.refs_5_
  14.6 2.7 %filter_own.1.refs_6_ = f32[4,4,224,128]{3,2,1,0:T(8,128)S(1)} custom-call(bf16[256,256]{1,0:T(8,128)(2,1)S(1)} %get-tuple-element.59.refs_0_, bf16[256,256]{1,0:T(8,128)(2,1)S(1)} %collective-permute-done.1.refs_1_, bf16[256,256]{1,0:T(8,128)(2,1)S(1)} %get-tuple-element.60.refs_2_, bf16[256,256]{1,0:T(8,128)(2,1)S(1)} %collective-permute-done.2.refs_3_, ...), custom_call_target="tpu_custom_call" | custom-call | flops 1000 | bytes 1000 | tf_op jit(solution)/shard_map/filter_own/pallas_call | solution.py:48
  17.2 0.0 collective-permute-done.4
  17.3 2.3 %collective-permute-start.6 = (f32[80,128]{1,0:T(8,128)S(1)}, f32[80,128]{1,0:T(8,128)S(1)}, u32[]{:S(2)}, u32[]{:S(2)}) collective-permute-start(f32[80,128]{1,0:T(8,128)S(1)} %add.6.refs_7_), channel_id=1, source_target_pairs={{0,16},{2,18},{4,20},{6,22},{8,24},{10,26},{12,28},{14,30},{16,0},... | collective-permute-start | bytes 122888 | tf_op jit(solution)/shard_map/ppermute | solution.py:395
  19.6 0.0 collective-permute-done.3.refs_5_
  19.6 1.4 %filter_grad.1 = (f32[4,4,224,128]{3,2,1,0:T(8,128)S(1)}, f32[2,224,128]{2,1,0:T(8,128)S(1)}, f32[4,224,128]{2,1,0:T(8,128)S(1)}, bf16[896,128]{1,0:T(8,128)(2,1...) custom-call(bf16[256,256]{1,0:T(8,128)(2,1)S(1)} %get-tuple-element., ...), custom_call_target="tpu_custom_call", output_to_operand_aliasing={{0}: (6, {})} | custom-call | flops 1000 | bytes 1000 | tf_op jit(solution)/shard_map/filter_grad/pallas_call | solution.py:48
  21.0 1.3 %collective-permute-done.6 = f32[80,128]{1,0:T(8,128)S(1)} collective-permute-done((f32[80,128]{1,0:T(8,128)S(1)}, f32[80,128]{1,0:T(8,128)S(1)}, u32[]{:S(2)}, u32[]{:S(2)}) %collective-permute-start.6) | collective-permute-done | bytes 40992 | tf_op jit(solution)/shard_map/ppermute | solution.py:395
  22.2 1.2 %collective-permute-start.7 = (bf16[896,128]{1,0:T(8,128)(2,1)S(1)}, bf16[896,128]{1,0:T(8,128)(2,1)S(1)}, u32[]{:S(2)}, u32[]{:S(2)}) collective-permute-start(bf16[896,128]{1,0:T(8,128)(2,1)S(1)} %get-tuple-element.72), channel_id=1, source_target_pairs={{0,8},{2,10},{4,12},{6,14},{8,0},{10,2},{12,4},{14,6},{16,24},{18,... | collective-permute-start | bytes 688136 | tf_op jit(solution)/shard_map/ppermute | solution.py:395
  23.5 1.0 %collective-permute-start.10 = (bf16[448,128]{1,0:T(8,128)(2,1)S(1)}, bf16[448,128]{1,0:T(8,128)(2,1)S(1)}, u32[]{:S(2)}, u32[]{:S(2)}) collective-permute-start(bf16[448,128]{1,0:T(8,128)(2,1)S(1)} %get-tuple-element.75), channel_id=1, source_target_pairs={{0,2},{2,0},{4,6},{6,4},{8,10},{10,8},{12,14},{14,12},{16,18},{18,... | collective-permute-start | bytes 344072 | tf_op jit(solution)/shard_map/ppermute | solution.py:395
  24.4 1.9 %collective-permute-start.8 = (bf16[448,128]{1,0:T(8,128)(2,1)S(1)}, bf16[448,128]{1,0:T(8,128)(2,1)S(1)}, u32[]{:S(2)}, u32[]{:S(2)}) collective-permute-start(bf16[448,128]{1,0:T(8,128)(2,1)S(1)} %get-tuple-element.73), channel_id=1, source_target_pairs={{0,6},{2,4},{4,2},{6,0},{8,14},{10,12},{12,10},{14,8},{16,22},{18,... | collective-permute-start | bytes 344072 | tf_op jit(solution)/shard_map/ppermute | solution.py:395
  26.3 0.7 %collective-permute-start.9 = (bf16[448,128]{1,0:T(8,128)(2,1)S(1)}, bf16[448,128]{1,0:T(8,128)(2,1)S(1)}, u32[]{:S(2)}, u32[]{:S(2)}) collective-permute-start(bf16[448,128]{1,0:T(8,128)(2,1)S(1)} %get-tuple-element.74), channel_id=1, source_target_pairs={{0,4},{2,6},{4,0},{6,2},{8,12},{10,14},{12,8},{14,10},{16,20},{18,... | collective-permute-start | bytes 344072 | tf_op jit(solution)/shard_map/ppermute | solution.py:395
  27.0 1.2 %collective-permute-done.11.refs_7_ = f32[80,128]{1,0:T(8,128)S(1)} collective-permute-done((f32[80,128]{1,0:T(8,128)S(1)}, f32[80,128]{1,0:T(8,128)S(1)}, u32[]{:S(2)}, u32[]{:S(2)}) %collective-permute-start.11) | collective-permute-done | bytes 40992 | tf_op jit(solution)/shard_map/ppermute | solution.py:399
  28.2 0.8 %collective-permute-done.10.refs_5_ = bf16[448,128]{1,0:T(8,128)(2,1)S(1)} collective-permute-done((bf16[448,128]{1,0:T(8,128)(2,1)S(1)}, bf16[448,128]{1,0:T(8,128)(2,1)S(1)}, u32[]{:S(2)}, u32[]{:S(2)}) %collective-permute-start.10) | collective-permute-done | bytes 114720 | tf_op jit(solution)/shard_map/ppermute | solution.py:395
  29.0 1.3 %collective-permute-done.8.refs_3_ = bf16[448,128]{1,0:T(8,128)(2,1)S(1)} collective-permute-done((bf16[448,128]{1,0:T(8,128)(2,1)S(1)}, bf16[448,128]{1,0:T(8,128)(2,1)S(1)}, u32[]{:S(2)}, u32[]{:S(2)}) %collective-permute-start.8) | collective-permute-done | bytes 114720 | tf_op jit(solution)/shard_map/ppermute | solution.py:395
  30.3 1.2 %collective-permute-done.9.refs_4_ = bf16[448,128]{1,0:T(8,128)(2,1)S(1)} collective-permute-done((bf16[448,128]{1,0:T(8,128)(2,1)S(1)}, bf16[448,128]{1,0:T(8,128)(2,1)S(1)}, u32[]{:S(2)}, u32[]{:S(2)}) %collective-permute-start.9) | collective-permute-done | bytes 114720 | tf_op jit(solution)/shard_map/ppermute | solution.py:395
  31.5 0.1 first_sum.1
  31.6 1.8 %collective-permute-start.14 = (bf16[400,128]{1,0:T(8,128)(2,1)S(1)}, bf16[400,128]{1,0:T(8,128)(2,1)S(1)}, u32[]{:S(2)}, u32[]{:S(2)}) collective-permute-start(bf16[400,128]{1,0:T(8,128)(2,1)S(1)} %get-tuple-element.82), channel_id=1, source_target_pairs={{0,6},{2,4},{4,2},{6,0},{8,14},{10,12},{12,10},{14,8},{16,22},{18,... | collective-permute-start | bytes 307208 | tf_op jit(solution)/shard_map/ppermute | solution.py:395
  33.4 1.8 %collective-permute-start.15 = (bf16[400,128]{1,0:T(8,128)(2,1)S(1)}, bf16[400,128]{1,0:T(8,128)(2,1)S(1)}, u32[]{:S(2)}, u32[]{:S(2)}) collective-permute-start(bf16[400,128]{1,0:T(8,128)(2,1)S(1)} %get-tuple-element.83), channel_id=1, source_target_pairs={{0,4},{2,6},{4,0},{6,2},{8,12},{10,14},{12,8},{14,10},{16,20},{18,... | collective-permute-start | bytes 307208 | tf_op jit(solution)/shard_map/ppermute | solution.py:395
  35.2 2.5 %collective-permute-start.12 = (bf16[224,128]{1,0:T(8,128)(2,1)S(1)}, bf16[224,128]{1,0:T(8,128)(2,1)S(1)}, u32[]{:S(2)}, u32[]{:S(2)}) collective-permute-start(bf16[224,128]{1,0:T(8,128)(2,1)S(1)} %get-tuple-element.80), channel_id=1, source_target_pairs={{0,24},{2,26},{4,28},{6,30},{8,16},{10,18},{12,20},{14,22},{16,8},... | collective-permute-start | bytes 172040 | tf_op jit(solution)/shard_map/ppermute | solution.py:395
  37.7 0.3 collective-permute-start.13
  38.0 3.2 %collective-permute-done.12.refs_3_ = bf16[224,128]{1,0:T(8,128)(2,1)S(1)} collective-permute-done((bf16[224,128]{1,0:T(8,128)(2,1)S(1)}, bf16[224,128]{1,0:T(8,128)(2,1)S(1)}, u32[]{:S(2)}, u32[]{:S(2)}) %collective-permute-start.12) | collective-permute-done | bytes 57376 | tf_op jit(solution)/shard_map/ppermute | solution.py:395
  41.2 2.2 %collective-permute-done.13.refs_4_ = bf16[224,128]{1,0:T(8,128)(2,1)S(1)} collective-permute-done((bf16[224,128]{1,0:T(8,128)(2,1)S(1)}, bf16[224,128]{1,0:T(8,128)(2,1)S(1)}, u32[]{:S(2)}, u32[]{:S(2)}) %collective-permute-start.13) | collective-permute-done | bytes 57376 | tf_op jit(solution)/shard_map/ppermute | solution.py:395
  43.4 0.9 %last_sum.1 = (f32[64,432]{1,0:T(8,128)}, f32[32,256]{1,0:T(8,128)}, f32[4,256]{1,0:T(4,128)}, f32[8,16]{1,0:T(8,128)}) custom-call(f32[224,128]{1,0:T(8,128)S(1)} %get-tuple-element.77.refs_0_, f32[80,128]{1,0:T(8,128)S(1)} %get-tuple-element.78.refs_1_, f32[8,16]{1,0:T(8,128)S(1)} %get-tuple-element.79.refs_2_, ...), custom_call_target="tpu_custom_call" | custom-call | flops 1000 | bytes 1000 | tf_op jit(solution)/shard_map/last_sum/pallas_call | solution.py:48
  (10 shorter events, 0.0 us)
Async XLA Ops:
  0.6 8.5 %collective-permute-start = (bf16[512,128]{1,0:T(8,128)(2,1)}, bf16[512,128]{1,0:T(8,128)(2,1)S(1)}, u32[]{:S(2)}, u32[]{:S(2)}) collective-permute-start(bf16[512,128]{1,0:T(8,128)(2,1)} %bitcast.13), channel_id=1, source_target_pairs={{2,0},{4,2},{6,4},{8,6},{10,8},{12,10},{14,12},{16,14},{18,16},{20... | collective-permute-start | bytes 393224 | tf_op jit(solution)/shard_map/ppermute | solution.py:411
  6.1 8.5 %collective-permute-start.1 = (bf16[256,256]{1,0:T(8,128)(2,1)S(1)}, bf16[256,256]{1,0:T(8,128)(2,1)S(1)}, u32[]{:S(2)}, u32[]{:S(2)}) collective-permute-start(bf16[256,256]{1,0:T(8,128)(2,1)S(1)} %get-tuple-element.59.refs_0_), channel_id=1, source_target_pairs={{0,1},{1,0},{2,3},{3,2},{4,5},{5,4},{6,7},{7,6},{8,9},{9,8},{10,11... | collective-permute-start | bytes 393224 | tf_op jit(solution)/shard_map/ppermute | solution.py:399
  6.6 8.0 %collective-permute-start.2 = (bf16[256,256]{1,0:T(8,128)(2,1)S(1)}, bf16[256,256]{1,0:T(8,128)(2,1)S(1)}, u32[]{:S(2)}, u32[]{:S(2)}) collective-permute-start(bf16[256,256]{1,0:T(8,128)(2,1)S(1)} %get-tuple-element.60.refs_2_), channel_id=1, source_target_pairs={{0,1},{1,0},{2,3},{3,2},{4,5},{5,4},{6,7},{7,6},{8,9},{9,8},{10,11... | collective-permute-start | bytes 393224 | tf_op jit(solution)/shard_map/ppermute | solution.py:399
  6.7 7.9 %collective-permute-start.5 = (bf16[512,128]{1,0:T(8,128)(2,1)S(1)}, bf16[512,128]{1,0:T(8,128)(2,1)S(1)}, u32[]{:S(2)}, u32[]{:S(2)}) collective-permute-start(bf16[512,128]{1,0:T(8,128)(2,1)S(1)} %get-tuple-element.62.refs_4_), channel_id=1, source_target_pairs={{0,1},{1,0},{2,3},{3,2},{4,5},{5,4},{6,7},{7,6},{8,9},{9,8},{10,11... | collective-permute-start | bytes 393224 | tf_op jit(solution)/shard_map/ppermute | solution.py:399
  9.2 10.4 %collective-permute-start.3 = (bf16[512,128]{1,0:T(8,128)(2,1)S(1)}, bf16[512,128]{1,0:T(8,128)(2,1)S(1)}, u32[]{:S(2)}, u32[]{:S(2)}) collective-permute-start(bf16[512,128]{1,0:T(8,128)(2,1)S(1)} %collective-permute-done.beyond.refs_4_), channel_id=1, source_target_pairs={{0,1},{1,0},{2,3},{3,2},{4,5},{5,4},{6,7},{7,6},{8,9},{9,8},{10,11... | collective-permute-start | bytes 393224 | tf_op jit(solution)/shard_map/ppermute | solution.py:399
  11.3 5.9 %collective-permute-start.4 = (f32[80,128]{1,0:T(8,128)S(1)}, f32[80,128]{1,0:T(8,128)S(1)}, u32[]{:S(2)}, u32[]{:S(2)}) collective-permute-start(f32[80,128]{1,0:T(8,128)S(1)} %get-tuple-element.61), channel_id=1, source_target_pairs={{0,8},{2,10},{4,12},{6,14},{8,0},{10,2},{12,4},{14,6},{16,24},{18,... | collective-permute-start | bytes 122888 | tf_op jit(solution)/shard_map/ppermute | solution.py:395
  17.3 5.0 %collective-permute-start.6 = (f32[80,128]{1,0:T(8,128)S(1)}, f32[80,128]{1,0:T(8,128)S(1)}, u32[]{:S(2)}, u32[]{:S(2)}) collective-permute-start(f32[80,128]{1,0:T(8,128)S(1)} %add.6.refs_7_), channel_id=1, source_target_pairs={{0,16},{2,18},{4,20},{6,22},{8,24},{10,26},{12,28},{14,30},{16,0},... | collective-permute-start | bytes 122888 | tf_op jit(solution)/shard_map/ppermute | solution.py:395
  22.2 9.3 %collective-permute-start.7 = (bf16[896,128]{1,0:T(8,128)(2,1)S(1)}, bf16[896,128]{1,0:T(8,128)(2,1)S(1)}, u32[]{:S(2)}, u32[]{:S(2)}) collective-permute-start(bf16[896,128]{1,0:T(8,128)(2,1)S(1)} %get-tuple-element.72), channel_id=1, source_target_pairs={{0,8},{2,10},{4,12},{6,14},{8,0},{10,2},{12,4},{14,6},{16,24},{18,... | collective-permute-start | bytes 688136 | tf_op jit(solution)/shard_map/ppermute | solution.py:395
  23.5 5.5 %collective-permute-start.10 = (bf16[448,128]{1,0:T(8,128)(2,1)S(1)}, bf16[448,128]{1,0:T(8,128)(2,1)S(1)}, u32[]{:S(2)}, u32[]{:S(2)}) collective-permute-start(bf16[448,128]{1,0:T(8,128)(2,1)S(1)} %get-tuple-element.75), channel_id=1, source_target_pairs={{0,2},{2,0},{4,6},{6,4},{8,10},{10,8},{12,14},{14,12},{16,18},{18,... | collective-permute-start | bytes 344072 | tf_op jit(solution)/shard_map/ppermute | solution.py:395
  24.4 5.9 %collective-permute-start.8 = (bf16[448,128]{1,0:T(8,128)(2,1)S(1)}, bf16[448,128]{1,0:T(8,128)(2,1)S(1)}, u32[]{:S(2)}, u32[]{:S(2)}) collective-permute-start(bf16[448,128]{1,0:T(8,128)(2,1)S(1)} %get-tuple-element.73), channel_id=1, source_target_pairs={{0,6},{2,4},{4,2},{6,0},{8,14},{10,12},{12,10},{14,8},{16,22},{18,... | collective-permute-start | bytes 344072 | tf_op jit(solution)/shard_map/ppermute | solution.py:395
  26.3 5.2 %collective-permute-start.9 = (bf16[448,128]{1,0:T(8,128)(2,1)S(1)}, bf16[448,128]{1,0:T(8,128)(2,1)S(1)}, u32[]{:S(2)}, u32[]{:S(2)}) collective-permute-start(bf16[448,128]{1,0:T(8,128)(2,1)S(1)} %get-tuple-element.74), channel_id=1, source_target_pairs={{0,4},{2,6},{4,0},{6,2},{8,12},{10,14},{12,8},{14,10},{16,20},{18,... | collective-permute-start | bytes 344072 | tf_op jit(solution)/shard_map/ppermute | solution.py:395
  27.0 1.2 %collective-permute-start.11 = (f32[80,128]{1,0:T(8,128)S(1)}, f32[80,128]{1,0:T(8,128)S(1)}, u32[]{:S(2)}, u32[]{:S(2)}) collective-permute-start(f32[80,128]{1,0:T(8,128)S(1)} %add.7.refs_6_), channel_id=1, source_target_pairs={{0,1},{1,0},{2,3},{3,2},{4,5},{5,4},{6,7},{7,6},{8,9},{9,8},{10,11... | collective-permute-start | bytes 122888 | tf_op jit(solution)/shard_map/ppermute | solution.py:399
  31.6 11.7 %collective-permute-start.14 = (bf16[400,128]{1,0:T(8,128)(2,1)S(1)}, bf16[400,128]{1,0:T(8,128)(2,1)S(1)}, u32[]{:S(2)}, u32[]{:S(2)}) collective-permute-start(bf16[400,128]{1,0:T(8,128)(2,1)S(1)} %get-tuple-element.82), channel_id=1, source_target_pairs={{0,6},{2,4},{4,2},{6,0},{8,14},{10,12},{12,10},{14,8},{16,22},{18,... | collective-permute-start | bytes 307208 | tf_op jit(solution)/shard_map/ppermute | solution.py:395
  33.4 10.0 %collective-permute-start.15 = (bf16[400,128]{1,0:T(8,128)(2,1)S(1)}, bf16[400,128]{1,0:T(8,128)(2,1)S(1)}, u32[]{:S(2)}, u32[]{:S(2)}) collective-permute-start(bf16[400,128]{1,0:T(8,128)(2,1)S(1)} %get-tuple-element.83), channel_id=1, source_target_pairs={{0,4},{2,6},{4,0},{6,2},{8,12},{10,14},{12,8},{14,10},{16,20},{18,... | collective-permute-start | bytes 307208 | tf_op jit(solution)/shard_map/ppermute | solution.py:395
  35.2 8.2 %collective-permute-start.16 = (bf16[400,128]{1,0:T(8,128)(2,1)S(1)}, bf16[400,128]{1,0:T(8,128)(2,1)S(1)}, u32[]{:S(2)}, u32[]{:S(2)}) collective-permute-start(bf16[400,128]{1,0:T(8,128)(2,1)S(1)} %get-tuple-element.84), channel_id=1, source_target_pairs={{0,2},{2,0},{4,6},{6,4},{8,10},{10,8},{12,14},{14,12},{16,18},{18,... | collective-permute-start | bytes 307208 | tf_op jit(solution)/shard_map/ppermute | solution.py:395
  35.2 6.0 %collective-permute-start.12 = (bf16[224,128]{1,0:T(8,128)(2,1)S(1)}, bf16[224,128]{1,0:T(8,128)(2,1)S(1)}, u32[]{:S(2)}, u32[]{:S(2)}) collective-permute-start(bf16[224,128]{1,0:T(8,128)(2,1)S(1)} %get-tuple-element.80), channel_id=1, source_target_pairs={{0,24},{2,26},{4,28},{6,30},{8,16},{10,18},{12,20},{14,22},{16,8},... | collective-permute-start | bytes 172040 | tf_op jit(solution)/shard_map/ppermute | solution.py:395
  37.7 5.7 %collective-permute-start.13 = (bf16[224,128]{1,0:T(8,128)(2,1)S(1)}, bf16[224,128]{1,0:T(8,128)(2,1)S(1)}, u32[]{:S(2)}, u32[]{:S(2)}) collective-permute-start(bf16[224,128]{1,0:T(8,128)(2,1)S(1)} %get-tuple-element.81), channel_id=1, source_target_pairs={{0,16},{2,18},{4,20},{6,22},{8,24},{10,26},{12,28},{14,30},{16,0},... | collective-permute-start | bytes 172040 | tf_op jit(solution)/shard_map/ppermute | solution.py:395
where the time goes:
time: 44.4 us; the launch traced here: 44.2 us
  starting transfers between devices  18.9 us (43%)
  waiting for transfers between devices  13.3 us (30%)
  Pallas kernels  11.3 us (25%)
  between operations  0.72 us (2%)
    ppermute x11, starting transfers between devices, along_ctx(): return lax.ppermute(value, 'ctx', [(s, target(s)) for s in range(count)])  16.6 us
    pallas_call x6, Pallas kernels, run(): pl.pallas_call(full if far_args else body, out_shape=outs + [shaped(args[...  11.3 us
    ppermute x11, waiting for transfers between devices, along_ctx(): return lax.ppermute(value, 'ctx', [(s, target(s)) for s in range(count)])  10 us
    ppermute x1, waiting for transfers between devices, local(): beyond = lax.ppermute(grads, 'ctx', [(s, s - 1) for s in range(1, count)])  2.08 us
    ppermute x1, starting transfers between devices, local(): beyond = lax.ppermute(grads, 'ctx', [(s, s - 1) for s in range(1, count)])  1.29 us
    ppermute x5, waiting for transfers between devices, others(): lax.ppermute(value, 'vid', [(s, (s + turn) % videos) for s in range(video...  1.22 us
    ppermute x5, starting transfers between devices, others(): lax.ppermute(value, 'vid', [(s, (s + turn) % videos) for s in range(video...  1.03 us
  transfers between devices with their start and end apart: 17, of which 8 were waited for; matrix products, arithmetic and copies ran while one was open for 0% of the time, Pallas kernels for 23%

commit v1 on v0

v1 whole, which is shorter than its diff:
```python
import functools
import math

import jax
import jax.numpy as jnp
from jax import lax
from jax.experimental import pallas as pl
from jax.experimental.pallas import tpu as pltpu
from jax.sharding import PartitionSpec as P

NEAR = 4
CELL = 4
TAPS = 3
TILE = 16

f32 = jnp.float32
bf16 = jnp.bfloat16
dot = functools.partial(lax.dot_general, preferred_element_type=f32)
exact = functools.partial(dot, precision=lax.Precision.HIGHEST)
ROWS_COLS = (((1,), (0,)), ((), ()))
ROWS_ROWS = (((1,), (1,)), ((), ()))
COLS_COLS = (((0,), (0,)), ((), ()))


def call(body, outs, scratch=(), name=None, far_args=(), keep=(), work=1000):
    outs = list(outs)
    lost = [k for k in far_args if k not in keep]

    def run(*args):
        args = [pltpu.with_memory_space_constraint(arg, pltpu.HBM) if k in far_args else arg
                for k, arg in enumerate(args)]

        def full(*refs):
            refs = list(refs)
            sems = refs.pop()
            buffers = {k: refs.pop() for k in lost[::-1]}
            first = len(args) + len(outs)
            buffers.update({k: refs.pop(first) for k in keep})
            moves = [pltpu.make_async_copy(refs[k], buffers[k], sems.at[at]) for at, k in enumerate(far_args)]
            for move in moves:
                move.start()
            for k in far_args:
                refs[k] = buffers[k]
            for move in moves:
                move.wait()
            body(*refs)

        return pl.pallas_call(
            full if far_args else body,
            out_shape=outs + [shaped(args[k].shape, args[k].dtype) for k in keep],
            in_specs=[pl.BlockSpec(memory_space=pltpu.HBM if k in far_args else pltpu.VMEM) for k in range(len(args))],
            scratch_shapes=list(scratch) + [pltpu.VMEM(args[k].shape, args[k].dtype) for k in lost]
            + ([pltpu.SemaphoreType.DMA((len(far_args),))] if far_args else []),
            name=name,
            cost_estimate=pl.CostEstimate(flops=work, bytes_accessed=work, transcendentals=0),
            compiler_params=pltpu.CompilerParams(vmem_limit_bytes=28 * 2**20),
        )(*args)

    return run


def halves(value):
    top = value.astype(bf16)
    return top, (value - top.astype(f32)).astype(bf16)


def shaped(shape, kind=f32):
    return jax.ShapeDtypeStruct(shape, kind)


def cell_matrix(height, width, cells):
    pixel = lax.broadcasted_iota(jnp.int32, (height * width, cells), 0)
    cell = lax.broadcasted_iota(jnp.int32, (height * width, cells), 1)
    place = (pixel // width) // CELL * (width // CELL) + pixel % width // CELL
    return jnp.where(place == cell, 1.0, 0.0).astype(f32)


def modulate_body(frames, height, width, feats, mean, rstd, latent, gamma, beta, ws, bs, wt, bt, grads, weights, *refs):
    acts, (slope, normed_out, gain_out, tab_out, partial, shifted) = refs[:frames], refs[frames:]
    chans = feats.shape[1]
    groups = mean.shape[1]
    pixels = height * width
    lat = latent[0, lax.axis_index("ctx") * frames // CELL]
    group = lax.broadcasted_iota(jnp.int32, (groups, chans), 0)
    chan = lax.broadcasted_iota(jnp.int32, (groups, chans), 1)
    member = jnp.where(chan // (chans // groups) == group, 1.0, 0.0).astype(f32)
    mean_chan = exact(mean[...], member, ROWS_COLS)
    rstd_chan = exact(rstd[...], member, ROWS_COLS)
    scale_tab = exact(lat, ws[...], COLS_COLS) + bs[...]
    shift_tab = exact(lat, wt[...], COLS_COLS) + bt[...]
    tab_out[...] = scale_tab
    cells = cell_matrix(height, width, lat.shape[1])
    scale_map = exact(cells, scale_tab, ROWS_COLS)
    shift_map = exact(cells, shift_tab, ROWS_COLS)
    gain_out[...] = scale_map * (gamma[...] * rstd_chan)
    for frame in range(frames):
        at = pl.ds(frame * pixels, pixels)
        normed = (feats[at, :].astype(f32) - mean_chan) * rstd_chan
        modulated = (normed * gamma[...] + beta[...]) * scale_map + shift_map
        squashed = jax.nn.sigmoid(modulated)
        normed_out[at, :] = normed
        slope[at, :] = squashed * (1.0 + modulated * (1.0 - squashed))
        acts[frame][...] = (modulated * squashed).T.astype(bf16)
    conv_own_body(frames, height, width, grads, weights, partial, shifted)


def column_shifts(value, width):
    column = lax.broadcasted_iota(jnp.int32, value.shape, 0) % width
    rows = value.shape[0]
    return (
        jnp.where(column == width - 1, 0.0, pltpu.roll(value, rows - 1, 0)),
        value,
        jnp.where(column == 0, 0.0, pltpu.roll(value, 1, 0)),
    )


def clear_borders(padded, width):
    lead = padded.shape[:-2]
    length, lanes = padded.shape[-2:]
    edge = jnp.zeros(lead + (width, lanes), padded.dtype)
    every = (slice(None),) * len(lead)
    padded[every + (slice(0, width),)] = edge
    padded[every + (slice(length - width, length),)] = edge


def put_shifts(shifted, source, frames, pixels, width):
    clear_borders(shifted, width)
    for col, value in enumerate(column_shifts(source[...].astype(f32), width)):
        for frame in range(frames):
            shifted[col, frame, width:width + pixels] = value[frame * pixels:(frame + 1) * pixels].astype(bf16)


def taps_of(weights, step, chans):
    return jnp.concatenate(
        [weights[(step * TAPS * TAPS + k) * chans:(step * TAPS * TAPS + k + 1) * chans, :]
         for k in range(TAPS * TAPS)], axis=1)


def shifted_rows(shifted, frame_list, pixels, width):
    def window(frame, row, col):
        start = (TAPS - 1 - row) * width
        return shifted[col, frame, start:start + pixels]

    return jnp.concatenate(
        [jnp.concatenate([window(frame, k // TAPS, k % TAPS) for k in range(TAPS * TAPS)], axis=1)
         for frame in frame_list], axis=0)


def add_rows(total, term, first):
    if first == 0 and term.shape[0] == total.shape[0]:
        total[...] += term
    else:
        total[first:first + term.shape[0]] += term


def conv_own_body(frames, height, width, grads, weights, total, shifted):
    pixels = height * width
    chans = total.shape[1]
    put_shifts(shifted, grads, frames, pixels, width)
    total[...] = jnp.zeros_like(total)
    for step in range(TAPS):
        pairs = [(t, t + TAPS - 1 - step) for t in range(frames) if t + TAPS - 1 - step < frames]
        if pairs:
            rows = shifted_rows(shifted, [frame for _, frame in pairs], pixels, width)
            add_rows(total, dot(rows, taps_of(weights, step, chans), ROWS_ROWS), pairs[0][0] * pixels)

    @pl.when(lax.axis_index("ctx") == 0)
    def _():
        for step in range(TAPS - 1):
            for frame in range(TAPS - 1 - step):
                rows = shifted_rows(shifted, [frame], pixels, width)
                add_rows(total, dot(rows, taps_of(weights, step, chans), ROWS_ROWS), 0)


def input_grad_body(frames, height, width, beyond, weights, partial, slope, normed, gain, tab, latent,
                    ws, wt, gamma, beta, feats_grad, small, lat_own, shifted, total):
    pixels = height * width
    chans = gain.shape[1]
    device = lax.axis_index("ctx")
    put_shifts(shifted, beyond, frames, pixels, width)
    total[...] = partial[...]
    for step in range(TAPS):
        pairs = [(t, t + TAPS - 1 - step - frames) for t in range(frames) if t + TAPS - 1 - step >= frames]
        if pairs:
            rows = shifted_rows(shifted, [frame for _, frame in pairs], pixels, width)
            add_rows(total, dot(rows, taps_of(weights, step, chans), ROWS_ROWS), pairs[0][0] * pixels)

    pooled_shift = jnp.zeros((pixels, chans), f32)
    pooled_norm = jnp.zeros((pixels, chans), f32)
    for frame in range(frames):
        at = pl.ds(frame * pixels, pixels)
        pre = total[at, :] * slope[at, :]
        feats_grad[at, :] = (pre * gain[...]).astype(bf16)
        pooled_shift += pre
        pooled_norm += pre * normed[at, :]
    lat = latent[0, device * frames // CELL]
    depth, length = lat.shape
    cells = cell_matrix(height, width, length)
    shift_pool = exact(cells, pooled_shift, COLS_COLS)
    norm_pool = exact(cells, pooled_norm, COLS_COLS)
    scale_pool = norm_pool * gamma[...] + shift_pool * beta[...]
    parts = [exact(lat, scale_pool, ROWS_COLS), exact(lat, shift_pool, ROWS_COLS)]
    for field in (norm_pool * tab[...], shift_pool * tab[...], scale_pool, shift_pool):
        parts.append(jnp.sum(field, axis=0, keepdims=True))
    lanes = small.shape[1]
    small[small.shape[0] - TILE:] = jnp.zeros((TILE, lanes), f32)
    at = 0
    for k in range(chans // lanes):
        for part in parts:
            small[at:at + part.shape[0]] = part[:, k * lanes:(k + 1) * lanes]
            at += part.shape[0]
    latent_sum = exact(scale_pool, ws[...], ROWS_ROWS) + exact(shift_pool, wt[...], ROWS_ROWS)
    first, second = latent_sum[:length // 2], latent_sum[length // 2:]
    even = device % 2 == 0
    lat_own[...] = jnp.where(even, first, second)
    lat_far = jnp.where(even, second, first)
    here = lax.axis_index("vid")
    for video in range(lanes // depth):
        @pl.when(here == video)
        def _(video=video):
            small[at:at + length // 2, video * depth:(video + 1) * depth] = lat_far


class FilterParts:
    def __init__(self, frames, height, width, videos, near, shifted, blocks, chans):
        self.frames, self.pixels, self.width, self.videos, self.near = frames, height * width, width, videos, near
        self.shifted, self.blocks, self.lanes, self.chans = shifted, blocks, blocks.shape[3], chans
        owners = blocks.shape[0] * near
        self.rows = TAPS**3 * chans // owners
        pair = lax.axis_index("ctx") // near // 2
        self.start, self.stop = pair * 2 * near * self.rows, (pair + 1) * 2 * near * self.rows
        self.even = lax.axis_index("vid") % 2 == 0

    def needed(self, step, row):
        low = (step * TAPS + row) * TAPS * self.chans
        high = low + TAPS * self.chans
        inside = (low < self.stop) & (high > self.start)
        outside = (low < self.start) | (high > self.stop)
        return jnp.where(self.even, inside.astype(jnp.int32), outside.astype(jnp.int32)) == 1

    def shift(self, sources):
        for video, source in enumerate(sources):
            put_shifts(self.shifted.at[video], source, self.frames, self.pixels, self.width)

    def product(self, acts, row, pairs):
        start = (TAPS - 1 - row) * self.width
        left = jnp.concatenate(
            [acts[t * self.videos + video][...] for video in range(self.videos) for t, _ in pairs], axis=1)
        right = jnp.concatenate(
            [jnp.concatenate([self.shifted[video, col, frame, start:start + self.pixels] for col in range(TAPS)], axis=1)
             for video in range(self.videos) for _, frame in pairs], axis=0)
        return dot(left, right, ROWS_COLS)

    def put(self, step, row, result, base=None):
        for col in range(TAPS):
            tap = (step * TAPS + row) * TAPS + col
            done = 0
            while done < self.chans:
                index = tap * self.chans + done
                owner, at = index // self.rows, index % self.rows
                length = min(self.chans - done, self.rows - at)
                part = (owner // self.near, owner % self.near, slice(at, at + length))
                terms = [] if base is None else [base[part]]
                if result is not None:
                    terms.append(result[done:done + length, col * self.lanes:(col + 1) * self.lanes])
                self.blocks[part] = sum(terms[1:], terms[0]) if terms else jnp.zeros((length, self.lanes), f32)
                done += length


def filter_own_body(frames, height, width, videos, near, *refs):
    acts, refs = refs[:frames * videos], refs[frames * videos:]
    grads, (_, blocks, shifted) = refs[:videos], refs[videos:]
    parts = FilterParts(frames, height, width, videos, near, shifted, blocks, acts[0].shape[0])
    parts.shift(grads)
    first = lax.axis_index("ctx") == 0
    for step in range(TAPS):
        pairs = [(t, t + TAPS - 1 - step) for t in range(frames) if t + TAPS - 1 - step < frames]
        for row in range(TAPS):
            @pl.when(parts.needed(step, row))
            def _(step=step, row=row, pairs=pairs):
                parts.put(step, row, parts.product(acts, row, pairs) if pairs else None)
                if step < TAPS - 1:
                    @pl.when(first)
                    def _():
                        extra = [parts.product(acts, row, [(0, frame)]) for frame in range(TAPS - 1 - step)]
                        parts.put(step, row, functools.reduce(lambda a, b: a + b, extra), blocks)


def put_pair(ref, at, value):
    top, rest = halves(value)
    ref[at:at + value.shape[0]] = top
    ref[at + value.shape[0]:at + 2 * value.shape[0]] = rest


def take_pair(ref, at, length):
    return ref[at:at + length].astype(f32) + ref[at + length:at + 2 * length].astype(f32)


def filter_grad_body(frames, height, width, videos, near, *refs):
    acts, refs = refs[:frames * videos], refs[frames * videos:]
    beyond, refs = refs[:videos], refs[videos:]
    smalls, base, refs = refs[:videos], refs[videos], refs[videos + 1:]
    own_far, own_line, small_out, line_send, *sends, shifted, blocks = refs
    parts = FilterParts(frames, height, width, videos, near, shifted, blocks, acts[0].shape[0])
    parts.shift(beyond)
    far, _, piece, _ = blocks.shape
    for step in range(TAPS):
        pairs = [(t, t + TAPS - 1 - step - frames) for t in range(frames) if t + TAPS - 1 - step >= frames]
        for row in range(TAPS):
            @pl.when(parts.needed(step, row))
            def _(step=step, row=row, pairs=pairs):
                parts.put(step, row, parts.product(acts, row, pairs) if pairs else None, base)
    device = lax.axis_index("ctx")
    line, place = device // near, device % near
    small = functools.reduce(lambda a, b: a + b, [ref[...] for ref in smalls])
    small_out[...] = small

    @pl.when(parts.even)
    def _():
        own_line[...] = blocks[line]
        for k in range(near):
            line_send[k * piece:(k + 1) * piece] = blocks[line ^ 1, k].astype(bf16)

    @pl.when(jnp.logical_not(parts.even))
    def _():
        for k in range(far - 2):
            own_far[k] = blocks[line ^ (k + 2), place]
        for turn, send in enumerate(sends, 1):
            for k in range(far - 2):
                send[k * piece:(k + 1) * piece] = blocks[line ^ (k + 2), place ^ turn].astype(bf16)
            put_pair(send, (far - 2) * piece, small)


def first_sum_body(near, far, entries, *refs):
    own_far, own_line, small, line_got, refs = *refs[:4], refs[4:]
    plane_got, refs = refs[:near - 1][::-1], refs[near - 1:]
    kept, small_out, small_send, refs = *refs[:3], refs[3:]
    plane_sends, line_sends, total = refs[:near - 1], refs[near - 1:-1], refs[-1]
    piece = own_line.shape[1]
    count = small.shape[0]
    place = lax.axis_index("ctx") % near
    even = lax.axis_index("vid") % 2 == 0

    @pl.when(even)
    def _():
        for k in range(near):
            total[k] = own_line[k] + line_got[k * piece:(k + 1) * piece].astype(f32)
        kept[...] = total[place]
        for turn, send in enumerate(plane_sends, 1):
            send[...] = total[place ^ turn].astype(bf16)

    @pl.when(jnp.logical_not(even))
    def _():
        got = [take_pair(ref, (far - 2) * piece, count) for ref in plane_got]
        row = lax.broadcasted_iota(jnp.int32, small.shape, 0)
        summed = jnp.where(row < entries, functools.reduce(lambda a, b: a + b, got, small[...]), got[0])
        small_out[...] = summed
        put_pair(small_send, 0, summed)
        for k, send in enumerate(line_sends):
            send[0:piece] = functools.reduce(
                lambda a, b: a + b[k * piece:(k + 1) * piece].astype(f32), plane_got, own_far[k]).astype(bf16)
            put_pair(send, piece, summed)


def last_sum_body(near, far, entries, *refs):
    kept, small, small_got, refs = *refs[:3], refs[3:]
    line_got, plane_got, refs = refs[:far - 2], refs[far - 2:near + far - 3], refs[near + far - 3:]
    mine, theirs, small_out, turned = refs
    piece = kept.shape[0]
    count = small.shape[0]
    cols, rows = mine.shape
    here = lax.axis_index("vid")
    even = here % 2 == 0

    @pl.when(even)
    def _():
        turned[...] = functools.reduce(lambda a, b: a + b[...].astype(f32), plane_got, kept[...]).T

    @pl.when(jnp.logical_not(even))
    def _():
        total = functools.reduce(lambda a, b: a + b, [ref[0:piece].astype(f32) for ref in line_got])
        turned[...] = total.T
        got = [take_pair(ref, piece, count) for ref in line_got] + [take_pair(small_got, 0, count)]
        row = lax.broadcasted_iota(jnp.int32, small.shape, 0)
        small_out[...] = jnp.where(row < entries, functools.reduce(lambda a, b: a + b, got, small[...]), small[...])

    mine[...] = turned[pl.ds(pl.multiple_of(here * cols, cols), cols)][:, :rows]
    theirs[...] = turned[pl.ds(pl.multiple_of((here ^ 1) * cols, cols), cols)][:, :rows]


def finish_body(entries, mine, theirs, small, small_got, lat_own, filter_grad, mod_grads, vector_grads, latent_grad):
    filter_grad[...] = mine[...] + theirs[...]
    here = lax.axis_index("vid")
    summed = jnp.where(here % 2 == 0, small_got[...], small[...])
    lanes = small.shape[1]
    split, length = mod_grads.shape[0], mod_grads.shape[0] + vector_grads.shape[0]
    for k in range(mod_grads.shape[1] // lanes):
        mod_grads[:, k * lanes:(k + 1) * lanes] = summed[k * length:k * length + split]
        vector_grads[:, k * lanes:(k + 1) * lanes] = summed[k * length + split:(k + 1) * length]
    cells, depth = lat_own.shape
    for video in range(lanes // depth):
        @pl.when(here == video)
        def _(video=video):
            latent_grad[...] = lat_own[...] + summed[entries:entries + cells, video * depth:(video + 1) * depth]


def local(features, grad_out, mean, rstd, latent, gamma, beta, ws, bs, wt, bt, kernel):
    _, frames, height, width, chans = features.shape
    outs = grad_out.shape[-1]
    depth, length = latent.shape[2:]
    count, videos = lax.axis_size("ctx"), lax.axis_size("vid")
    near = math.gcd(count, NEAR)
    far = count // near
    pixels = height * width
    size = frames * pixels
    rows, cols = TAPS**3 * chans // count, outs // videos
    piece = -(-rows // TILE) * TILE
    gamma, beta, bs, bt = (value.reshape(1, chans) for value in (gamma, beta, bs, bt))
    feats = features.reshape(size, chans)
    grads = grad_out.reshape(size, outs)

    def along_ctx(value, target, odd):
        pairs = [(s * videos + v, target(s) * videos + v) for s in range(count) for v in range(odd, videos, 2)]
        return lax.ppermute(value, ("ctx", "vid"), pairs)

    def other_core(value):
        return lax.ppermute(value, "vid", [(v, v ^ 1) for v in range(videos)])

    def others(value):
        return [value] + [
            lax.ppermute(value, "vid", [(s, (s + turn) % videos) for s in range(videos)])
            for turn in range(1, videos)]

    def plane_got(values, odd):
        return [along_ctx(value, lambda s: s ^ turn, odd) for turn, value in enumerate(values, 1)]

    def line_got(values, first, odd):
        return [along_ctx(value, lambda s: s ^ (turn * near), odd) for turn, value in enumerate(values, first)]

    beyond = lax.ppermute(grads, "ctx", [(s, s - 1) for s in range(1, count)])
    shifts = pltpu.VMEM((TAPS, frames, (height + 2) * width, outs), bf16)
    *acts, slope, normed, gain, tab, partial, latent, gamma, beta, ws, wt, grads_near, kernel = call(
        functools.partial(modulate_body, frames, height, width),
        [shaped((chans, pixels), bf16)] * frames
        + [shaped((size, chans)), shaped((size, chans)), shaped((pixels, chans)),
         shaped((length, chans)), shaped((size, chans))],
        (shifts,),
        name="modulate",
        far_args=tuple(range(12)),
        keep=(3, 4, 5, 6, 8, 10, 11),
    )(feats, mean, rstd, latent, gamma, beta, ws, bs, wt, bt, grads, kernel)
    acts_all = [value for act in acts for value in others(act)]
    grads_all = others(grads_near)
    beyond_all = others(beyond)
    cells = length // 2
    entries = (2 * depth + 4) * (chans // outs)
    count_small = -(-(entries + cells) // TILE) * TILE
    feats_grad, small, lat_own = call(
        functools.partial(input_grad_body, frames, height, width),
        (shaped((size, chans), bf16), shaped((count_small, outs)), shaped((cells, depth))),
        (shifts, pltpu.VMEM((size, chans), f32)),
        name="input_grad",
    )(beyond, kernel, partial, slope, normed, gain, tab, latent, ws, wt, gamma, beta)
    smalls = others(small)
    shifts = pltpu.VMEM((videos, TAPS, frames, (height + 2) * width, outs), bf16)
    blocks, = call(
        functools.partial(filter_own_body, frames, height, width, videos, near),
        (shaped((far, near, piece, outs)),),
        (shifts,),
        name="filter_own",
    )(*acts_all, *grads_all, lat_own)
    own_far, own_line, small, line_send, *plane_sends = call(
        functools.partial(filter_grad_body, frames, height, width, videos, near),
        [shaped((far - 2, piece, outs)), shaped((near, piece, outs)),
         shaped((count_small, outs)), shaped((near * piece, outs), bf16)]
        + [shaped(((far - 2) * piece + 2 * count_small, outs), bf16)] * (near - 1),
        (shifts, pltpu.VMEM(blocks.shape, f32)),
        name="filter_grad",
    )(*acts_all, *beyond_all, *smalls, blocks)
    line_in = line_got([line_send], 1, 0)
    plane_in = plane_got(plane_sends, 1)
    kept, small, small_send, *sends = call(
        functools.partial(first_sum_body, near, far, entries),
        [shaped((piece, outs)), shaped((count_small, outs)), shaped((2 * count_small, outs), bf16)]
        + [shaped((piece, outs), bf16)] * (near - 1) + [shaped((piece + 2 * count_small, outs), bf16)] * (far - 2),
        (pltpu.VMEM((near, piece, outs), f32),),
        name="first_sum",
    )(own_far, own_line, small, *line_in, *plane_in[::-1])
    line_in = line_got(sends[near - 1:], 2, 1)
    plane_in = plane_got(sends[:near - 1], 0)
    mine, theirs, small = call(
        functools.partial(last_sum_body, near, far, entries),
        (shaped((cols, rows)), shaped((cols, rows)), shaped((count_small, outs))),
        (pltpu.VMEM((outs, piece), f32),),
        name="last_sum",
    )(kept, small, *line_got([small_send], 1, 1), *line_in[::-1], *plane_in[::-1])
    filter_grad, mod_grads, vector_grads, latent_grad = call(
        functools.partial(finish_body, entries),
        (shaped((cols, rows)), shaped((2 * depth, chans)), shaped((4, chans)), shaped((cells, depth))),
        name="finish",
    )(mine, other_core(theirs), small, other_core(small), lat_own)
    return (
        feats_grad.reshape(features.shape),
        filter_grad.T,
        mod_grads.reshape(2, depth, chans),
        vector_grads,
        latent_grad.T[None, None],
    )


def solution(mesh):
    split = P("vid", "ctx", None, None, None)
    return jax.shard_map(
        local,
        mesh=mesh,
        in_specs=(split, split, P("vid", None), P("vid", None), P("vid", None, None, None)) + (P(),) * 7,
        out_specs=(split, P("ctx", "vid"), P(), P(), P("vid", "ctx", None, None)),
        check_vma=False,
    )
```

time: 44.4 us -> 49.5 us (1.11)
  starting transfers between devices: 18.9 us -> 23.4 us
  Pallas kernels: 11.3 us -> 12.7 us
  waiting for transfers between devices: 13.3 us -> 12.2 us
    ppermute x11 -> x12, starting transfers between devices: 16.6 us -> 20.5 us  [the longest x10 16.3 us: along_ctx(): return lax.ppermute(value, ('ctx', 'vid'), pairs)]
    pallas_call x6 -> x7, Pallas kernels: 11.3 us -> 12.7 us  [run(): pl.pallas_call(full if far_args else body, out_shape=outs + [shaped(args[...]
    ppermute x5, waiting for transfers between devices: 1.22 us -> 0.01 us  [others(): lax.ppermute(value, 'vid', [(s, (s + turn) % videos) for s in range(video...]
    ppermute x5, starting transfers between devices: 1.03 us -> 1.6 us  [others(): lax.ppermute(value, 'vid', [(s, (s + turn) % videos) for s in range(video...]
    ppermute x11 -> x12, waiting for transfers between devices: 10 us -> 10.1 us  [the longest x10 9.01 us: along_ctx(): return lax.ppermute(value, ('ctx', 'vid'), pairs)]
  transfers between devices with their start and end apart: 17 -> 18, of which waited for: 8 -> 5; matrix products, arithmetic and copies ran while one was open for 0% -> 0% of each run, Pallas kernels for 23% -> 19%
where the time goes in v1:
time: 49.5 us; the launch traced here: 49.2 us
  starting transfers between devices  23.4 us (47%)
  Pallas kernels  12.7 us (26%)
  waiting for transfers between devices  12.2 us (25%)
  between operations  0.83 us (2%)
    ppermute x10, starting transfers between devices, along_ctx(): return lax.ppermute(value, ('ctx', 'vid'), pairs)  16.3 us
    pallas_call x7, Pallas kernels, run(): pl.pallas_call(full if far_args else body, out_shape=outs + [shaped(args[...  12.7 us
    ppermute x10, waiting for transfers between devices, along_ctx(): return lax.ppermute(value, ('ctx', 'vid'), pairs)  9.01 us
    ppermute x2, starting transfers between devices, other_core(): return lax.ppermute(value, 'vid', [(v, v ^ 1) for v in range(videos)])  4.25 us
    ppermute x1, waiting for transfers between devices, local(): beyond = lax.ppermute(grads, 'ctx', [(s, s - 1) for s in range(1, count)])  2.08 us
    ppermute x5, starting transfers between devices, others(): lax.ppermute(value, 'vid', [(s, (s + turn) % videos) for s in range(video...  1.6 us
    ppermute x1, starting transfers between devices, local(): beyond = lax.ppermute(grads, 'ctx', [(s, s - 1) for s in range(1, count)])  1.29 us
    ppermute x2, waiting for transfers between devices, other_core(): return lax.ppermute(value, 'vid', [(v, v ^ 1) for v in range(videos)])  1.14 us
  transfers between devices with their start and end apart: 18, of which 5 were waited for; matrix products, arithmetic and copies ran while one was open for 0% of the time, Pallas kernels for 19%

profile of v1, /device:TPU:0, one launch (start us, length us, event | category | flops | bytes accessed | tf_op | source)
XLA Modules:
  0.0 49.2 jit_solution(8702361311231836890)
XLA Ops:
  0.6 1.3 %collective-permute-start = (bf16[512,128]{1,0:T(8,128)(2,1)}, bf16[512,128]{1,0:T(8,128)(2,1)S(1)}, u32[]{:S(2)}, u32[]{:S(2)}) collective-permute-start(bf16[512,128]{1,0:T(8,128)(2,1)} %bitcast.13), channel_id=1, source_target_pairs={{2,0},{4,2},{6,4},{8,6},{10,8},{12,10},{14,12},{16,14},{18,16},{20... | collective-permute-start | bytes 393224 | tf_op jit(solution)/shard_map/ppermute | solution.py:440
  1.9 4.1 %modulate.1 = (bf16[256,256]{1,0:T(8,128)(2,1)S(1)}, bf16[256,256]{1,0:T(8,128)(2,1)S(1)}, f32[512,256]{1,0:T(8,128)S(1)}, f32[512,256]{1,0:T(8,128)S(1)}, f32[2...) custom-call(bf16[512,256]{1,0:T(8,128)(2,1)} %bitcast.12, ...), custom_call_target="tpu_custom_call" | custom-call | flops 1000 | bytes 1000 | tf_op jit(solution)/shard_map/modulate/pallas_call | solution.py:48
  6.1 0.5 %collective-permute-start.5 = (bf16[512,128]{1,0:T(8,128)(2,1)S(1)}, bf16[512,128]{1,0:T(8,128)(2,1)S(1)}, u32[]{:S(2)}, u32[]{:S(2)}) collective-permute-start(bf16[512,128]{1,0:T(8,128)(2,1)S(1)} %get-tuple-element.59.refs_4_), channel_id=1, source_target_pairs={{0,1},{1,0},{2,3},{3,2},{4,5},{5,4},{6,7},{7,6},{8,9},{9,8},{10,11... | collective-permute-start | bytes 393224 | tf_op jit(solution)/shard_map/ppermute | solution.py:431
  6.6 0.1 collective-permute-start.1
  6.7 0.4 collective-permute-start.2
  7.1 2.1 %collective-permute-done.beyond.refs_4_ = bf16[512,128]{1,0:T(8,128)(2,1)S(1)} collective-permute-done((bf16[512,128]{1,0:T(8,128)(2,1)}, bf16[512,128]{1,0:T(8,128)(2,1)S(1)}, u32[]{:S(2)}, u32[]{:S(2)}) %collective-permute-start) | collective-permute-done | bytes 131104 | tf_op jit(solution)/shard_map/ppermute | solution.py:440
  9.2 0.0 collective-permute-start.3
  9.2 2.6 %input_grad.1 = (bf16[512,256]{1,0:T(8,128)(2,1)}, f32[80,128]{1,0:T(8,128)S(1)}, f32[8,16]{1,0:T(8,128)S(1)}) custom-call(bf16[512,128]{1,0:T(8,128)(2,1)S(1)} %collective-permute-done.beyond.refs_4_, bf16[6912,128]{1,0:T(8,128)(2,1)S(1)} %get-tuple-element.44.weights, f32[512,256]{1,0:T(8,128)S(1)} %get-tuple-element.45.partial, ...), custom_call_target="tpu_custom_call" | custom-call | flops 1000 | bytes 1000 | tf_op jit(solution)/shard_map/input_grad/pallas_call | solution.py:48
  11.7 0.6 %collective-permute-start.4 = (f32[80,128]{1,0:T(8,128)S(1)}, f32[80,128]{1,0:T(8,128)S(1)}, u32[]{:S(2)}, u32[]{:S(2)}) collective-permute-start(f32[80,128]{1,0:T(8,128)S(1)} %get-tuple-element.58.refs_6_), channel_id=1, source_target_pairs={{0,1},{1,0},{2,3},{3,2},{4,5},{5,4},{6,7},{7,6},{8,9},{9,8},{10,11... | collective-permute-start | bytes 122888 | tf_op jit(solution)/shard_map/ppermute | solution.py:431
  12.3 0.0 collective-permute-done.2.refs_3_
  12.3 2.8 %filter_own.1.refs_8_ = f32[4,4,432,128]{3,2,1,0:T(8,128)S(1)} custom-call(bf16[256,256]{1,0:T(8,128)(2,1)S(1)} %get-tuple-element.56.refs_0_, bf16[256,256]{1,0:T(8,128)(2,1)S(1)} %collective-permute-done.1.refs_1_, bf16[256,256]{1,0:T(8,128)(2,1)S(1)} %get-tuple-element.57.refs_2_, bf16[256,256]{1,0:T(8,128)(2,1)S(1)} %collective-permute-done.2.refs_3_, ...), custom_call_target="tpu_custom_call" | custom-call | flops 1000 | bytes 1000 | tf_op jit(solution)/shard_map/filter_own/pallas_call | solution.py:48
  15.1 0.0 collective-permute-done.3.refs_5_
  15.1 2.2 %filter_grad.1 = (f32[2,432,128]{2,1,0:T(8,128)S(1)}, f32[4,432,128]{2,1,0:T(8,128)S(1)}, f32[80,128]{1,0:T(8,128)S(1)}, bf16[1728,128]{1,0:T(8,128)(2,1)S(1)}, ...) custom-call(bf16[256,256]{1,0:T(8,128)(2,1)S(1)} %get-tuple-element.56.refs_0_, ...), custom_call_target="tpu_custom_call" | custom-call | flops 1000 | bytes 1000 | tf_op jit(solution)/shard_map/filter_grad/pallas_call | solution.py:48
  17.4 3.0 %collective-permute-start.6 = (bf16[1728,128]{1,0:T(8,128)(2,1)S(1)}, bf16[1728,128]{1,0:T(8,128)(2,1)S(1)}, u32[]{:S(2)}, u32[]{:S(2)}) collective-permute-start(bf16[1728,128]{1,0:T(8,128)(2,1)S(1)} %get-tuple-element.64), channel_id=1, source_target_pairs={{0,8},{2,10},{4,12},{6,14},{8,0},{10,2},{12,4},{14,6},{16,24},{18,... | collective-permute-start | bytes 1327112 | tf_op jit(solution)/shard_map/ppermute | solution.py:424
  20.4 0.7 %collective-permute-start.7 = (bf16[1024,128]{1,0:T(8,128)(2,1)S(1)}, bf16[1024,128]{1,0:T(8,128)(2,1)S(1)}, u32[]{:S(2)}, u32[]{:S(2)}) collective-permute-start(bf16[1024,128]{1,0:T(8,128)(2,1)S(1)} %get-tuple-element.65), channel_id=1, source_target_pairs={{1,7},{3,5},{5,3},{7,1},{9,15},{11,13},{13,11},{15,9},{17,23},{19,... | collective-permute-start | bytes 786440 | tf_op jit(solution)/shard_map/ppermute | solution.py:424
  21.1 0.7 %collective-permute-start.8 = (bf16[1024,128]{1,0:T(8,128)(2,1)S(1)}, bf16[1024,128]{1,0:T(8,128)(2,1)S(1)}, u32[]{:S(2)}, u32[]{:S(2)}) collective-permute-start(bf16[1024,128]{1,0:T(8,128)(2,1)S(1)} %get-tuple-element.66), channel_id=1, source_target_pairs={{1,5},{3,7},{5,1},{7,3},{9,13},{11,15},{13,9},{15,11},{17,21},{19,... | collective-permute-start | bytes 786440 | tf_op jit(solution)/shard_map/ppermute | solution.py:424
  21.8 0.7 %collective-permute-start.9 = (bf16[1024,128]{1,0:T(8,128)(2,1)S(1)}, bf16[1024,128]{1,0:T(8,128)(2,1)S(1)}, u32[]{:S(2)}, u32[]{:S(2)}) collective-permute-start(bf16[1024,128]{1,0:T(8,128)(2,1)S(1)} %get-tuple-element.67), channel_id=1, source_target_pairs={{1,3},{3,1},{5,7},{7,5},{9,11},{11,9},{13,15},{15,13},{17,19},{19,... | collective-permute-start | bytes 786440 | tf_op jit(solution)/shard_map/ppermute | solution.py:424
  22.5 5.1 %collective-permute-done.6.refs_3_ = bf16[1728,128]{1,0:T(8,128)(2,1)S(1)} collective-permute-done((bf16[1728,128]{1,0:T(8,128)(2,1)S(1)}, bf16[1728,128]{1,0:T(8,128)(2,1)S(1)}, u32[]{:S(2)}, u32[]{:S(2)}) %collective-permute-start.6) | collective-permute-done | bytes 442400 | tf_op jit(solution)/shard_map/ppermute | solution.py:424
  27.6 0.1 first_sum.1
  27.7 0.7 %collective-permute-start.10 = (bf16[160,128]{1,0:T(8,128)(2,1)S(1)}, bf16[160,128]{1,0:T(8,128)(2,1)S(1)}, u32[]{:S(2)}, u32[]{:S(2)}) collective-permute-start(bf16[160,128]{1,0:T(8,128)(2,1)S(1)} %get-tuple-element.70), channel_id=1, source_target_pairs={{1,9},{3,11},{5,13},{7,15},{9,1},{11,3},{13,5},{15,7},{17,25},{19,... | collective-permute-start | bytes 122888 | tf_op jit(solution)/shard_map/ppermute | solution.py:424
  28.4 0.7 %collective-permute-start.11 = (bf16[592,128]{1,0:T(8,128)(2,1)S(1)}, bf16[592,128]{1,0:T(8,128)(2,1)S(1)}, u32[]{:S(2)}, u32[]{:S(2)}) collective-permute-start(bf16[592,128]{1,0:T(8,128)(2,1)S(1)} %get-tuple-element.71), channel_id=1, source_target_pairs={{1,25},{3,27},{5,29},{7,31},{9,17},{11,19},{13,21},{15,23},{17,9},... | collective-permute-start | bytes 454664 | tf_op jit(solution)/shard_map/ppermute | solution.py:424
  29.1 0.7 %collective-permute-start.12 = (bf16[592,128]{1,0:T(8,128)(2,1)S(1)}, bf16[592,128]{1,0:T(8,128)(2,1)S(1)}, u32[]{:S(2)}, u32[]{:S(2)}) collective-permute-start(bf16[592,128]{1,0:T(8,128)(2,1)S(1)} %get-tuple-element.72), channel_id=1, source_target_pairs={{1,17},{3,19},{5,21},{7,23},{9,25},{11,27},{13,29},{15,31},{17,1},... | collective-permute-start | bytes 454664 | tf_op jit(solution)/shard_map/ppermute | solution.py:424
  29.7 4.6 %collective-permute-start.13 = (bf16[432,128]{1,0:T(8,128)(2,1)S(1)}, bf16[432,128]{1,0:T(8,128)(2,1)S(1)}, u32[]{:S(2)}, u32[]{:S(2)}) collective-permute-start(bf16[432,128]{1,0:T(8,128)(2,1)S(1)} %get-tuple-element.73), channel_id=1, source_target_pairs={{0,6},{2,4},{4,2},{6,0},{8,14},{10,12},{12,10},{14,8},{16,22},{18,... | collective-permute-start | bytes 331784 | tf_op jit(solution)/shard_map/ppermute | solution.py:424
  34.3 1.9 %collective-permute-start.14 = (bf16[432,128]{1,0:T(8,128)(2,1)S(1)}, bf16[432,128]{1,0:T(8,128)(2,1)S(1)}, u32[]{:S(2)}, u32[]{:S(2)}) collective-permute-start(bf16[432,128]{1,0:T(8,128)(2,1)S(1)} %get-tuple-element.74), channel_id=1, source_target_pairs={{0,4},{2,6},{4,0},{6,2},{8,12},{10,14},{12,8},{14,10},{16,20},{18,... | collective-permute-start | bytes 331784 | tf_op jit(solution)/shard_map/ppermute | solution.py:424
  36.2 2.7 %collective-permute-start.15 = (bf16[432,128]{1,0:T(8,128)(2,1)S(1)}, bf16[432,128]{1,0:T(8,128)(2,1)S(1)}, u32[]{:S(2)}, u32[]{:S(2)}) collective-permute-start(bf16[432,128]{1,0:T(8,128)(2,1)S(1)} %get-tuple-element.75), channel_id=1, source_target_pairs={{0,2},{2,0},{4,6},{6,4},{8,10},{10,8},{12,14},{14,12},{16,18},{18,... | collective-permute-start | bytes 331784 | tf_op jit(solution)/shard_map/ppermute | solution.py:424
  39.0 1.9 %collective-permute-done.14.refs_6_ = bf16[432,128]{1,0:T(8,128)(2,1)S(1)} collective-permute-done((bf16[432,128]{1,0:T(8,128)(2,1)S(1)}, bf16[432,128]{1,0:T(8,128)(2,1)S(1)}, u32[]{:S(2)}, u32[]{:S(2)}) %collective-permute-start.14) | collective-permute-done | bytes 110624 | tf_op jit(solution)/shard_map/ppermute | solution.py:424
  40.9 1.9 %collective-permute-done.15.refs_7_ = bf16[432,128]{1,0:T(8,128)(2,1)S(1)} collective-permute-done((bf16[432,128]{1,0:T(8,128)(2,1)S(1)}, bf16[432,128]{1,0:T(8,128)(2,1)S(1)}, u32[]{:S(2)}, u32[]{:S(2)}) %collective-permute-start.15) | collective-permute-done | bytes 110624 | tf_op jit(solution)/shard_map/ppermute | solution.py:424
  42.9 0.2 last_sum.1
  43.1 4.2 %collective-permute-start.16 = (f32[64,432]{1,0:T(8,128)S(1)}, f32[64,432]{1,0:T(8,128)S(1)}, u32[]{:S(2)}, u32[]{:S(2)}) collective-permute-start(f32[64,432]{1,0:T(8,128)S(1)} %get-tuple-element.77), channel_id=1, source_target_pairs={{0,1},{1,0},{2,3},{3,2},{4,5},{5,4},{6,7},{7,6},{8,9},{9,8},{10,11... | collective-permute-start | bytes 331784 | tf_op jit(solution)/shard_map/ppermute | solution.py:427
  47.2 0.1 collective-permute-start.17
  47.3 1.1 %collective-permute-done.17.small_got = f32[80,128]{1,0:T(8,128)S(1)} collective-permute-done((f32[80,128]{1,0:T(8,128)S(1)}, f32[80,128]{1,0:T(8,128)S(1)}, u32[]{:S(2)}, u32[]{:S(2)}) %collective-permute-start.17) | collective-permute-done | bytes 40992 | tf_op jit(solution)/shard_map/ppermute | solution.py:427
  48.5 0.7 %finish.1 = (f32[64,432]{1,0:T(8,128)}, f32[32,256]{1,0:T(8,128)}, f32[4,256]{1,0:T(4,128)}, f32[8,16]{1,0:T(8,128)}) custom-call(f32[64,432]{1,0:T(8,128)S(1)} %get-tuple-element.76.mine, f32[64,432]{1,0:T(8,128)S(1)} %collective-permute-done.16.theirs, f32[80,128]{1,0:T(8,128)S(1)} %get-tuple-element.78.small, ...), custom_call_target="tpu_custom_call" | custom-call | flops 1000 | bytes 1000 | tf_op jit(solution)/shard_map/finish/pallas_call | solution.py:48
  (11 shorter events, 0.0 us)
Async XLA Ops:
  0.6 8.5 %collective-permute-start = (bf16[512,128]{1,0:T(8,128)(2,1)}, bf16[512,128]{1,0:T(8,128)(2,1)S(1)}, u32[]{:S(2)}, u32[]{:S(2)}) collective-permute-start(bf16[512,128]{1,0:T(8,128)(2,1)} %bitcast.13), channel_id=1, source_target_pairs={{2,0},{4,2},{6,4},{8,6},{10,8},{12,10},{14,12},{16,14},{18,16},{20... | collective-permute-start | bytes 393224 | tf_op jit(solution)/shard_map/ppermute | solution.py:440
  6.1 6.3 %collective-permute-start.5 = (bf16[512,128]{1,0:T(8,128)(2,1)S(1)}, bf16[512,128]{1,0:T(8,128)(2,1)S(1)}, u32[]{:S(2)}, u32[]{:S(2)}) collective-permute-start(bf16[512,128]{1,0:T(8,128)(2,1)S(1)} %get-tuple-element.59.refs_4_), channel_id=1, source_target_pairs={{0,1},{1,0},{2,3},{3,2},{4,5},{5,4},{6,7},{7,6},{8,9},{9,8},{10,11... | collective-permute-start | bytes 393224 | tf_op jit(solution)/shard_map/ppermute | solution.py:431
  6.6 5.7 %collective-permute-start.1 = (bf16[256,256]{1,0:T(8,128)(2,1)S(1)}, bf16[256,256]{1,0:T(8,128)(2,1)S(1)}, u32[]{:S(2)}, u32[]{:S(2)}) collective-permute-start(bf16[256,256]{1,0:T(8,128)(2,1)S(1)} %get-tuple-element.56.refs_0_), channel_id=1, source_target_pairs={{0,1},{1,0},{2,3},{3,2},{4,5},{5,4},{6,7},{7,6},{8,9},{9,8},{10,11... | collective-permute-start | bytes 393224 | tf_op jit(solution)/shard_map/ppermute | solution.py:431
  6.7 5.7 %collective-permute-start.2 = (bf16[256,256]{1,0:T(8,128)(2,1)S(1)}, bf16[256,256]{1,0:T(8,128)(2,1)S(1)}, u32[]{:S(2)}, u32[]{:S(2)}) collective-permute-start(bf16[256,256]{1,0:T(8,128)(2,1)S(1)} %get-tuple-element.57.refs_2_), channel_id=1, source_target_pairs={{0,1},{1,0},{2,3},{3,2},{4,5},{5,4},{6,7},{7,6},{8,9},{9,8},{10,11... | collective-permute-start | bytes 393224 | tf_op jit(solution)/shard_map/ppermute | solution.py:431
  9.2 5.9 %collective-permute-start.3 = (bf16[512,128]{1,0:T(8,128)(2,1)S(1)}, bf16[512,128]{1,0:T(8,128)(2,1)S(1)}, u32[]{:S(2)}, u32[]{:S(2)}) collective-permute-start(bf16[512,128]{1,0:T(8,128)(2,1)S(1)} %collective-permute-done.beyond.refs_4_), channel_id=1, source_target_pairs={{0,1},{1,0},{2,3},{3,2},{4,5},{5,4},{6,7},{7,6},{8,9},{9,8},{10,11... | collective-permute-start | bytes 393224 | tf_op jit(solution)/shard_map/ppermute | solution.py:431
  11.7 3.4 %collective-permute-start.4 = (f32[80,128]{1,0:T(8,128)S(1)}, f32[80,128]{1,0:T(8,128)S(1)}, u32[]{:S(2)}, u32[]{:S(2)}) collective-permute-start(f32[80,128]{1,0:T(8,128)S(1)} %get-tuple-element.58.refs_6_), channel_id=1, source_target_pairs={{0,1},{1,0},{2,3},{3,2},{4,5},{5,4},{6,7},{7,6},{8,9},{9,8},{10,11... | collective-permute-start | bytes 122888 | tf_op jit(solution)/shard_map/ppermute | solution.py:431
  17.4 10.2 %collective-permute-start.6 = (bf16[1728,128]{1,0:T(8,128)(2,1)S(1)}, bf16[1728,128]{1,0:T(8,128)(2,1)S(1)}, u32[]{:S(2)}, u32[]{:S(2)}) collective-permute-start(bf16[1728,128]{1,0:T(8,128)(2,1)S(1)} %get-tuple-element.64), channel_id=1, source_target_pairs={{0,8},{2,10},{4,12},{6,14},{8,0},{10,2},{12,4},{14,6},{16,24},{18,... | collective-permute-start | bytes 1327112 | tf_op jit(solution)/shard_map/ppermute | solution.py:424
  20.4 2.1 %collective-permute-start.7 = (bf16[1024,128]{1,0:T(8,128)(2,1)S(1)}, bf16[1024,128]{1,0:T(8,128)(2,1)S(1)}, u32[]{:S(2)}, u32[]{:S(2)}) collective-permute-start(bf16[1024,128]{1,0:T(8,128)(2,1)S(1)} %get-tuple-element.65), channel_id=1, source_target_pairs={{1,7},{3,5},{5,3},{7,1},{9,15},{11,13},{13,11},{15,9},{17,23},{19,... | collective-permute-start | bytes 786440 | tf_op jit(solution)/shard_map/ppermute | solution.py:424
  21.1 1.4 %collective-permute-start.8 = (bf16[1024,128]{1,0:T(8,128)(2,1)S(1)}, bf16[1024,128]{1,0:T(8,128)(2,1)S(1)}, u32[]{:S(2)}, u32[]{:S(2)}) collective-permute-start(bf16[1024,128]{1,0:T(8,128)(2,1)S(1)} %get-tuple-element.66), channel_id=1, source_target_pairs={{1,5},{3,7},{5,1},{7,3},{9,13},{11,15},{13,9},{15,11},{17,21},{19,... | collective-permute-start | bytes 786440 | tf_op jit(solution)/shard_map/ppermute | solution.py:424
  21.8 0.7 %collective-permute-start.9 = (bf16[1024,128]{1,0:T(8,128)(2,1)S(1)}, bf16[1024,128]{1,0:T(8,128)(2,1)S(1)}, u32[]{:S(2)}, u32[]{:S(2)}) collective-permute-start(bf16[1024,128]{1,0:T(8,128)(2,1)S(1)} %get-tuple-element.67), channel_id=1, source_target_pairs={{1,3},{3,1},{5,7},{7,5},{9,11},{11,9},{13,15},{15,13},{17,19},{19,... | collective-permute-start | bytes 786440 | tf_op jit(solution)/shard_map/ppermute | solution.py:424
  27.7 8.5 %collective-permute-start.10 = (bf16[160,128]{1,0:T(8,128)(2,1)S(1)}, bf16[160,128]{1,0:T(8,128)(2,1)S(1)}, u32[]{:S(2)}, u32[]{:S(2)}) collective-permute-start(bf16[160,128]{1,0:T(8,128)(2,1)S(1)} %get-tuple-element.70), channel_id=1, source_target_pairs={{1,9},{3,11},{5,13},{7,15},{9,1},{11,3},{13,5},{15,7},{17,25},{19,... | collective-permute-start | bytes 122888 | tf_op jit(solution)/shard_map/ppermute | solution.py:424
  28.4 14.5 %collective-permute-start.11 = (bf16[592,128]{1,0:T(8,128)(2,1)S(1)}, bf16[592,128]{1,0:T(8,128)(2,1)S(1)}, u32[]{:S(2)}, u32[]{:S(2)}) collective-permute-start(bf16[592,128]{1,0:T(8,128)(2,1)S(1)} %get-tuple-element.71), channel_id=1, source_target_pairs={{1,25},{3,27},{5,29},{7,31},{9,17},{11,19},{13,21},{15,23},{17,9},... | collective-permute-start | bytes 454664 | tf_op jit(solution)/shard_map/ppermute | solution.py:424
  29.1 13.8 %collective-permute-start.12 = (bf16[592,128]{1,0:T(8,128)(2,1)S(1)}, bf16[592,128]{1,0:T(8,128)(2,1)S(1)}, u32[]{:S(2)}, u32[]{:S(2)}) collective-permute-start(bf16[592,128]{1,0:T(8,128)(2,1)S(1)} %get-tuple-element.72), channel_id=1, source_target_pairs={{1,17},{3,19},{5,21},{7,23},{9,25},{11,27},{13,29},{15,31},{17,1},... | collective-permute-start | bytes 454664 | tf_op jit(solution)/shard_map/ppermute | solution.py:424
  29.7 9.3 %collective-permute-start.13 = (bf16[432,128]{1,0:T(8,128)(2,1)S(1)}, bf16[432,128]{1,0:T(8,128)(2,1)S(1)}, u32[]{:S(2)}, u32[]{:S(2)}) collective-permute-start(bf16[432,128]{1,0:T(8,128)(2,1)S(1)} %get-tuple-element.73), channel_id=1, source_target_pairs={{0,6},{2,4},{4,2},{6,0},{8,14},{10,12},{12,10},{14,8},{16,22},{18,... | collective-permute-start | bytes 331784 | tf_op jit(solution)/shard_map/ppermute | solution.py:424
  34.3 6.6 %collective-permute-start.14 = (bf16[432,128]{1,0:T(8,128)(2,1)S(1)}, bf16[432,128]{1,0:T(8,128)(2,1)S(1)}, u32[]{:S(2)}, u32[]{:S(2)}) collective-permute-start(bf16[432,128]{1,0:T(8,128)(2,1)S(1)} %get-tuple-element.74), channel_id=1, source_target_pairs={{0,4},{2,6},{4,0},{6,2},{8,12},{10,14},{12,8},{14,10},{16,20},{18,... | collective-permute-start | bytes 331784 | tf_op jit(solution)/shard_map/ppermute | solution.py:424
  36.2 6.6 %collective-permute-start.15 = (bf16[432,128]{1,0:T(8,128)(2,1)S(1)}, bf16[432,128]{1,0:T(8,128)(2,1)S(1)}, u32[]{:S(2)}, u32[]{:S(2)}) collective-permute-start(bf16[432,128]{1,0:T(8,128)(2,1)S(1)} %get-tuple-element.75), channel_id=1, source_target_pairs={{0,2},{2,0},{4,6},{6,4},{8,10},{10,8},{12,14},{14,12},{16,18},{18,... | collective-permute-start | bytes 331784 | tf_op jit(solution)/shard_map/ppermute | solution.py:424
  43.1 5.4 %collective-permute-start.16 = (f32[64,432]{1,0:T(8,128)S(1)}, f32[64,432]{1,0:T(8,128)S(1)}, u32[]{:S(2)}, u32[]{:S(2)}) collective-permute-start(f32[64,432]{1,0:T(8,128)S(1)} %get-tuple-element.77), channel_id=1, source_target_pairs={{0,1},{1,0},{2,3},{3,2},{4,5},{5,4},{6,7},{7,6},{8,9},{9,8},{10,11... | collective-permute-start | bytes 331784 | tf_op jit(solution)/shard_map/ppermute | solution.py:427
  47.2 1.2 %collective-permute-start.17 = (f32[80,128]{1,0:T(8,128)S(1)}, f32[80,128]{1,0:T(8,128)S(1)}, u32[]{:S(2)}, u32[]{:S(2)}) collective-permute-start(f32[80,128]{1,0:T(8,128)S(1)} %get-tuple-element.78.small), channel_id=1, source_target_pairs={{0,1},{1,0},{2,3},{3,2},{4,5},{5,4},{6,7},{7,6},{8,9},{9,8},{10,11... | collective-permute-start | bytes 122888 | tf_op jit(solution)/shard_map/ppermute | solution.py:427

commit v2 on v0

--- a/solution.py
+++ b/solution.py
@@ -22,7 +22,7 @@
 COLS_COLS = (((0,), (0,)), ((), ()))
 
 
-def call(body, outs, scratch=(), name=None, far_args=(), keep=(), aliases=None, work=1000):
+def call(body, outs, scratch=(), name=None, far_args=(), keep=(), work=1000):
     outs = list(outs)
     lost = [k for k in far_args if k not in keep]
 
@@ -51,10 +51,9 @@
             in_specs=[pl.BlockSpec(memory_space=pltpu.HBM if k in far_args else pltpu.VMEM) for k in range(len(args))],
             scratch_shapes=list(scratch) + [pltpu.VMEM(args[k].shape, args[k].dtype) for k in lost]
             + ([pltpu.SemaphoreType.DMA((len(far_args),))] if far_args else []),
-            input_output_aliases=aliases or {},
             name=name,
             cost_estimate=pl.CostEstimate(flops=work, bytes_accessed=work, transcendentals=0),
-            compiler_params=pltpu.CompilerParams(vmem_limit_bytes=50 * 2**20),
+            compiler_params=pltpu.CompilerParams(vmem_limit_bytes=28 * 2**20),
         )(*args)
 
     return run
@@ -174,7 +173,7 @@
 
 
 def input_grad_body(frames, height, width, beyond, weights, partial, slope, normed, gain, tab, latent,
-                    ws, wt, gamma, beta, feats_grad, small, lat_own, lat_far, shifted, total):
+                    ws, wt, gamma, beta, feats_grad, small, lat_own, shifted, total):
     pixels = height * width
     chans = gain.shape[1]
     device = lax.axis_index("ctx")
@@ -214,7 +213,12 @@
     first, second = latent_sum[:length // 2], latent_sum[length // 2:]
     even = device % 2 == 0
     lat_own[...] = jnp.where(even, first, second)
-    lat_far[...] = jnp.where(even, second, first)
+    lat_far = jnp.where(even, second, first)
+    here = lax.axis_index("vid")
+    for video in range(lanes // depth):
+        @pl.when(here == video)
+        def _(video=video):
+            small[at:at + length // 2, video * depth:(video + 1) * depth] = lat_far
 
 
 class FilterParts:
@@ -255,7 +259,7 @@
              for video in range(self.videos) for _, frame in pairs], axis=0)
         return dot(left, right, ROWS_COLS)
 
-    def put(self, step, result, add):
+    def put(self, step, result, base=None):
         for place, (row, bank) in enumerate(self.slots):
             tile = None if result is None else result[:, place * self.lanes:(place + 1) * self.lanes]
             for k in range(min(self.per, TAPS - bank * self.per)):
@@ -267,16 +271,15 @@
                     part, at = inside // self.piece, inside % self.piece
                     length = min(self.chans - done, self.rows - inside, self.piece - at)
                     low, high = part * self.cols, (part + 1) * self.cols
-                    dest = self.blocks.at[owner // self.near, owner % self.near, at:at + length, low:high]
-                    if tile is None:
-                        dest[...] = jnp.zeros((length, self.cols), f32)
-                    else:
+                    dest = (owner // self.near, owner % self.near, slice(at, at + length), slice(low, high))
+                    terms = [] if base is None else [base[dest]]
+                    if tile is not None:
                         value = tile[done:done + length]
                         turn = (part - k) * self.cols % self.lanes
                         if turn:
                             value = pltpu.roll(value, turn, 1)
-                        value = value[:, low:high]
-                        dest[...] = dest[...] + value if add else value
+                        terms.append(value[:, low:high])
+                    self.blocks[dest] = sum(terms[1:], terms[0]) if terms else jnp.zeros((length, self.cols), f32)
                     done += length
 
 
@@ -291,89 +294,101 @@
         blocks[:, :, piece - TILE:] = jnp.zeros((far, near, TILE, lanes), f32)
     for step in range(TAPS):
         pairs = [(t, t + TAPS - 1 - step) for t in range(frames) if t + TAPS - 1 - step < frames]
-        parts.put(step, parts.product(acts, pairs) if pairs else None, False)
+        parts.put(step, parts.product(acts, pairs) if pairs else None)
         if step < TAPS - 1:
             @pl.when(first)
             def _(step=step):
                 extra = [parts.product(acts, [(0, frame)]) for frame in range(TAPS - 1 - step)]
-                parts.put(step, functools.reduce(lambda a, b: a + b, extra), True)
+                parts.put(step, functools.reduce(lambda a, b: a + b, extra), blocks)
+
+
+def put_pair(ref, at, value):
+    top, rest = halves(value)
+    ref[at:at + value.shape[0]] = top
+    ref[at + value.shape[0]:at + 2 * value.shape[0]] = rest
+
+
+def take_pair(ref, at, length):
+    return ref[at:at + length].astype(f32) + ref[at + length:at + 2 * length].astype(f32)
 
 
 def filter_grad_body(frames, height, width, videos, near, piece, *refs):
     acts, refs = refs[:frames * videos], refs[frames * videos:]
-    beyond, refs = refs[:videos], refs[videos + 2:]
-    blocks, own_far, own_line, line_send, *sends, packs = refs
+    beyond, refs = refs[:videos], refs[videos:]
+    smalls, base, refs = refs[:videos], refs[videos], refs[videos + 1:]
+    own_far, own_line, small_out, line_send, *sends, packs, blocks = refs
     parts = FilterParts(frames, height, width, videos, near, piece, packs, blocks, beyond[0].shape[1], acts[0].shape[0])
     parts.pack(beyond)
-    far = blocks.shape[0]
+    far, lanes = blocks.shape[0], blocks.shape[3]
+    if piece * videos > parts.rows:
+        blocks[:, :, piece - TILE:] = jnp.zeros((far, near, TILE, lanes), f32)
     for step in range(TAPS):
         pairs = [(t, t + TAPS - 1 - step - frames) for t in range(frames) if t + TAPS - 1 - step >= frames]
-        if pairs:
-            parts.put(step, parts.product(acts, pairs), True)
+        parts.put(step, parts.product(acts, pairs) if pairs else None, base)
     device = lax.axis_index("ctx")
     line, place = device // near, device % near
+    small = functools.reduce(lambda a, b: a + b, [ref[...] for ref in smalls])
+    small_out[...] = small
     own_line[...] = blocks[line]
     for k in range(near):
         line_send[k * piece:(k + 1) * piece] = blocks[line ^ 1, k].astype(bf16)
     for k in range(far - 2):
         own_far[k] = blocks[line ^ (k + 2), place]
-        for turn, send in enumerate(sends, 1):
+    for turn, send in enumerate(sends, 1):
+        for k in range(far - 2):
             send[k * piece:(k + 1) * piece] = blocks[line ^ (k + 2), place ^ turn].astype(bf16)
-
-
-def first_sum_body(near, far, videos, *refs):
-    own_far, own_line, line_got, refs = refs[0], refs[1], refs[2], refs[3:]
+        put_pair(send, (far - 2) * piece, small)
+
+
+def first_sum_body(near, far, entries, *refs):
+    own_far, own_line, small, line_got, refs = *refs[:4], refs[4:]
     plane_got, refs = refs[:near - 1][::-1], refs[near - 1:]
-    smalls, lat_far, refs = refs[:videos], refs[videos], refs[videos + 1:]
-    kept, small_out, refs = refs[0], refs[1], refs[2:]
+    kept, small_out, small_send, refs = *refs[:3], refs[3:]
     plane_sends, line_sends, total = refs[:near - 1], refs[near - 1:-1], refs[-1]
     piece = own_line.shape[1]
-    count = smalls[0].shape[0]
+    count = small.shape[0]
     place = lax.axis_index("ctx") % near
+    got = [take_pair(ref, (far - 2) * piece, count) for ref in plane_got]
+    row = lax.broadcasted_iota(jnp.int32, small.shape, 0)
+    summed = jnp.where(row < entries, functools.reduce(lambda a, b: a + b, got, small[...]), got[0])
+    small_out[...] = summed
+    put_pair(small_send, 0, summed)
     for k, send in enumerate(line_sends):
-        send[...] = functools.reduce(
+        send[0:piece] = functools.reduce(
             lambda a, b: a + b[k * piece:(k + 1) * piece].astype(f32), plane_got, own_far[k]).astype(bf16)
+        put_pair(send, piece, summed)
     for k in range(near):
         total[k] = own_line[k] + line_got[k * piece:(k + 1) * piece].astype(f32)
     kept[...] = total[place]
-    summed = functools.reduce(lambda a, b: a + b, [ref[...] for ref in smalls])
-    small_out[...] = summed
-    top, rest = halves(summed)
-    lat_top, lat_rest = halves(lat_far[...])
-    cells, depth = lat_top.shape
-    at = piece + 2 * count
     for turn, send in enumerate(plane_sends, 1):
-        send[0:piece] = total[place ^ turn].astype(bf16)
-        send[piece:piece + count] = top
-        send[piece + count:at] = rest
-        send[at:at + cells, :depth] = lat_top
-        send[at + cells:at + 2 * cells, :depth] = lat_rest
-
-
-def last_sum_body(near, far, *refs):
-    kept, small, lat_own, refs = refs[0], refs[1], refs[2], refs[3:]
-    line_got, plane_got, refs = refs[:far - 2], refs[far - 2:near + far - 3][::-1], refs[near + far - 3:]
+        send[...] = total[place ^ turn].astype(bf16)
+
+
+def last_sum_body(near, far, entries, *refs):
+    kept, small, small_got, lat_own, refs = *refs[:4], refs[4:]
+    line_got, plane_got, refs = refs[:far - 2], refs[far - 2:near + far - 3], refs[near + far - 3:]
     filter_grad, mod_grads, vector_grads, latent_grad = refs
     piece, lanes = kept.shape
     count = small.shape[0]
-
-    def joined(ref, start, length):
-        return ref[start:start + length].astype(f32) + ref[start + length:start + 2 * length].astype(f32)
-
-    total = functools.reduce(lambda a, b: a + b[0:piece].astype(f32), plane_got + line_got, kept[...])
+    total = functools.reduce(lambda a, b: a + b[0:piece].astype(f32), line_got + plane_got, kept[...])
     cols, rows = filter_grad.shape
     turned = total.T
     for part in range(lanes // cols):
         first, last = part * piece, min(rows, (part + 1) * piece)
         if first < last:
             filter_grad[:, first:last] = turned[part * cols:(part + 1) * cols, :last - first]
-    summed = functools.reduce(lambda a, b: a + joined(b, piece, count), plane_got, small[...])
+    got = [take_pair(ref, piece, count) for ref in line_got] + [take_pair(small_got, 0, count)]
+    summed = functools.reduce(lambda a, b: a + b, got, small[...])
     split, length = mod_grads.shape[0], mod_grads.shape[0] + vector_grads.shape[0]
     for k in range(mod_grads.shape[1] // lanes):
         mod_grads[:, k * lanes:(k + 1) * lanes] = summed[k * length:k * length + split]
         vector_grads[:, k * lanes:(k + 1) * lanes] = summed[k * length + split:(k + 1) * length]
     cells, depth = lat_own.shape
-    latent_grad[...] = lat_own[...] + joined(plane_got[0], piece + 2 * count, cells)[:, :depth]
+    here = lax.axis_index("vid")
+    for video in range(lanes // depth):
+        @pl.when(here == video)
+        def _(video=video):
+            latent_grad[...] = lat_own[...] + small[entries:entries + cells, video * depth:(video + 1) * depth]
 
 
 def local(features, grad_out, mean, rstd, latent, gamma, beta, ws, bs, wt, bt, kernel):
@@ -424,14 +439,15 @@
     grads_all = others(grads_near)
     beyond_all = others(beyond)
     cells = length // 2
-    count_small = -(-(2 * depth + 4) * (chans // outs) // TILE) * TILE
-    feats_grad, small, lat_own, lat_far = call(
+    entries = (2 * depth + 4) * (chans // outs)
+    count_small = -(-(entries + cells) // TILE) * TILE
+    feats_grad, small, lat_own = call(
         functools.partial(input_grad_body, frames, height, width),
-        (shaped((size, chans), bf16), shaped((count_small, outs)), shaped((cells, depth)), shaped((cells, depth))),
+        (shaped((size, chans), bf16), shaped((count_small, outs)), shaped((cells, depth))),
         (shifts, pltpu.VMEM((size, chans), f32)),
         name="input_grad",
-        work=2 * size * TAPS**3 * chans * outs,
     )(beyond, kernel, partial, slope, normed, gain, tab, latent, ws, wt, gamma, beta)
+    smalls = others(small)
     banks = -(-TAPS // min(videos, TAPS))
     packs = pltpu.VMEM((videos, banks, frames, (height + 2) * width, outs), bf16)
     blocks, = call(
@@ -439,41 +455,31 @@
         (shaped((far, near, piece, outs)),),
         (packs,),
         name="filter_own",
-    )(*acts_all, *grads_all, lat_far)
-    got, blocks = lax.optimization_barrier((along_ctx(small, lambda s: s ^ near), blocks))
-    small = small + got
-    blocks, own_far, own_line, line_send, *plane_sends = call(
+    )(*acts_all, *grads_all, lat_own)
+    own_far, own_line, small, line_send, *plane_sends = call(
         functools.partial(filter_grad_body, frames, height, width, videos, near, piece),
-        [shaped(blocks.shape), shaped((far - 2, piece, outs)), shaped((near, piece, outs)),
-         shaped((near * piece, outs), bf16)]
-        + [shaped(((far - 2) * piece, outs), bf16)] * (near - 1),
-        (packs,),
+        [shaped((far - 2, piece, outs)), shaped((near, piece, outs)),
+         shaped((count_small, outs)), shaped((near * piece, outs), bf16)]
+        + [shaped(((far - 2) * piece + 2 * count_small, outs), bf16)] * (near - 1),
+        (packs, pltpu.VMEM(blocks.shape, f32)),
         name="filter_grad",
-        aliases={(frames + 1) * videos: 0},
-    )(*acts_all, *beyond_all, blocks, small)
-    step = 2
-    while step < far:
-        got = along_ctx(small, lambda s: s ^ (step * near))
-        got, line_send, *plane_sends = lax.optimization_barrier((got, line_send, *plane_sends))
-        small = small + got
-        step *= 2
-    extra = 2 * count_small + -(-2 * cells // TILE) * TILE
+    )(*acts_all, *beyond_all, *smalls, blocks)
     line_in = line_got([line_send], 1)
     plane_in = plane_got(plane_sends)
-    kept, small, *sends = call(
-        functools.partial(first_sum_body, near, far, videos),
-        [shaped((piece, outs)), shaped((count_small, outs))]
-        + [shaped((piece + extra, outs), bf16)] * (near - 1) + [shaped((piece, outs), bf16)] * (far - 2),
+    kept, small, small_send, *sends = call(
+        functools.partial(first_sum_body, near, far, entries),
+        [shaped((piece, outs)), shaped((count_small, outs)), shaped((2 * count_small, outs), bf16)]
+        + [shaped((piece, outs), bf16)] * (near - 1) + [shaped((piece + 2 * count_small, outs), bf16)] * (far - 2),
         (pltpu.VMEM((near, piece, outs), f32),),
         name="first_sum",
-    )(own_far, own_line, *line_in, *plane_in[::-1], *others(small), lat_far)
+    )(own_far, own_line, small, *line_in, *plane_in[::-1])
     line_in = line_got(sends[near - 1:], 2)
     plane_in = plane_got(sends[:near - 1])
     filter_grad, mod_grads, vector_grads, latent_grad = call(
-        functools.partial(last_sum_body, near, far),
+        functools.partial(last_sum_body, near, far, entries),
         (shaped((cols, rows)), shaped((2 * depth, chans)), shaped((4, chans)), shaped((cells, depth))),
         name="last_sum",
-    )(kept, small, lat_own, *line_in[::-1], *plane_in[::-1])
+    )(kept, small, *line_got([small_send], 1), lat_own, *line_in[::-1], *plane_in[::-1])
     return (
         feats_grad.reshape(features.shape),
         filter_grad.T,

time: 44.4 us -> 42 us (0.946)
  starting transfers between devices: 18.9 us -> 15.8 us
    ppermute x11 -> x10, starting transfers between devices: 16.6 us -> 12.9 us  [along_ctx(): return lax.ppermute(value, 'ctx', [(s, target(s)) for s in range(count)])]
    ppermute x11 -> x10, waiting for transfers between devices: 10 us -> 11.6 us  [along_ctx(): return lax.ppermute(value, 'ctx', [(s, target(s)) for s in range(count)])]
    ppermute x5, waiting for transfers between devices: 1.22 us -> 0.01 us  [others(): lax.ppermute(value, 'vid', [(s, (s + turn) % videos) for s in range(video...]
    ppermute x5, starting transfers between devices: 1.03 us -> 1.6 us  [others(): lax.ppermute(value, 'vid', [(s, (s + turn) % videos) for s in range(video...]
  transfers between devices with their start and end apart: 17 -> 16, of which waited for: 8 -> 7; matrix products, arithmetic and copies ran while one was open for 0% -> 0% of each run, Pallas kernels for 23% -> 22%
where the time goes in v2:
time: 42 us; the launch traced here: 41.9 us
  starting transfers between devices  15.8 us (38%)
  waiting for transfers between devices  13.7 us (33%)
  Pallas kernels  11.7 us (28%)
  between operations  0.71 us (2%)
    ppermute x10, starting transfers between devices, along_ctx(): return lax.ppermute(value, 'ctx', [(s, target(s)) for s in range(count)])  12.9 us
    pallas_call x6, Pallas kernels, run(): pl.pallas_call(full if far_args else body, out_shape=outs + [shaped(args[...  11.7 us
    ppermute x10, waiting for transfers between devices, along_ctx(): return lax.ppermute(value, 'ctx', [(s, target(s)) for s in range(count)])  11.6 us
    ppermute x1, waiting for transfers between devices, local(): beyond = lax.ppermute(grads, 'ctx', [(s, s - 1) for s in range(1, count)])  2.08 us
    ppermute x5, starting transfers between devices, others(): lax.ppermute(value, 'vid', [(s, (s + turn) % videos) for s in range(video...  1.6 us
    ppermute x1, starting transfers between devices, local(): beyond = lax.ppermute(grads, 'ctx', [(s, s - 1) for s in range(1, count)])  1.29 us
  transfers between devices with their start and end apart: 16, of which 7 were waited for; matrix products, arithmetic and copies ran while one was open for 0% of the time, Pallas kernels for 22%

profile of v2, /device:TPU:0, one launch (start us, length us, event | category | flops | bytes accessed | tf_op | source)
XLA Modules:
  0.0 41.9 jit_solution(10468795044064802233)
XLA Ops:
  0.6 1.3 %collective-permute-start = (bf16[512,128]{1,0:T(8,128)(2,1)}, bf16[512,128]{1,0:T(8,128)(2,1)S(1)}, u32[]{:S(2)}, u32[]{:S(2)}) collective-permute-start(bf16[512,128]{1,0:T(8,128)(2,1)} %bitcast.13), channel_id=1, source_target_pairs={{2,0},{4,2},{6,4},{8,6},{10,8},{12,10},{14,12},{16,14},{18,16},{20... | collective-permute-start | bytes 393224 | tf_op jit(solution)/shard_map/ppermute | solution.py:426
  1.9 4.1 %modulate.1 = (bf16[256,256]{1,0:T(8,128)(2,1)S(1)}, bf16[256,256]{1,0:T(8,128)(2,1)S(1)}, f32[512,256]{1,0:T(8,128)S(1)}, f32[512,256]{1,0:T(8,128)S(1)}, f32[2...) custom-call(bf16[512,256]{1,0:T(8,128)(2,1)} %bitcast.12, ...), custom_call_target="tpu_custom_call" | custom-call | flops 1000 | bytes 1000 | tf_op jit(solution)/shard_map/modulate/pallas_call | solution.py:48
  6.1 0.5 %collective-permute-start.1 = (bf16[256,256]{1,0:T(8,128)(2,1)S(1)}, bf16[256,256]{1,0:T(8,128)(2,1)S(1)}, u32[]{:S(2)}, u32[]{:S(2)}) collective-permute-start(bf16[256,256]{1,0:T(8,128)(2,1)S(1)} %get-tuple-element.53.refs_0_), channel_id=1, source_target_pairs={{0,1},{1,0},{2,3},{3,2},{4,5},{5,4},{6,7},{7,6},{8,9},{9,8},{10,11... | collective-permute-start | bytes 393224 | tf_op jit(solution)/shard_map/ppermute | solution.py:414
  6.6 0.1 collective-permute-start.2
  6.7 0.4 %collective-permute-start.5 = (bf16[512,128]{1,0:T(8,128)(2,1)S(1)}, bf16[512,128]{1,0:T(8,128)(2,1)S(1)}, u32[]{:S(2)}, u32[]{:S(2)}) collective-permute-start(bf16[512,128]{1,0:T(8,128)(2,1)S(1)} %get-tuple-element.56.refs_4_), channel_id=1, source_target_pairs={{0,1},{1,0},{2,3},{3,2},{4,5},{5,4},{6,7},{7,6},{8,9},{9,8},{10,11... | collective-permute-start | bytes 393224 | tf_op jit(solution)/shard_map/ppermute | solution.py:414
  7.1 2.1 %collective-permute-done.beyond.refs_4_ = bf16[512,128]{1,0:T(8,128)(2,1)S(1)} collective-permute-done((bf16[512,128]{1,0:T(8,128)(2,1)}, bf16[512,128]{1,0:T(8,128)(2,1)S(1)}, u32[]{:S(2)}, u32[]{:S(2)}) %collective-permute-start) | collective-permute-done | bytes 131104 | tf_op jit(solution)/shard_map/ppermute | solution.py:426
  9.2 0.0 collective-permute-start.3
  9.2 2.6 %input_grad.1 = (bf16[512,256]{1,0:T(8,128)(2,1)}, f32[80,128]{1,0:T(8,128)S(1)}, f32[8,16]{1,0:T(8,128)S(1)}) custom-call(bf16[512,128]{1,0:T(8,128)(2,1)S(1)} %collective-permute-done.beyond.refs_4_, bf16[6912,128]{1,0:T(8,128)(2,1)S(1)} %get-tuple-element.41.weights, f32[512,256]{1,0:T(8,128)S(1)} %get-tuple-element.42.partial, ...), custom_call_target="tpu_custom_call" | custom-call | flops 1000 | bytes 1000 | tf_op jit(solution)/shard_map/input_grad/pallas_call | solution.py:48
  11.7 0.6 %collective-permute-start.4 = (f32[80,128]{1,0:T(8,128)S(1)}, f32[80,128]{1,0:T(8,128)S(1)}, u32[]{:S(2)}, u32[]{:S(2)}) collective-permute-start(f32[80,128]{1,0:T(8,128)S(1)} %get-tuple-element.55.refs_6_), channel_id=1, source_target_pairs={{0,1},{1,0},{2,3},{3,2},{4,5},{5,4},{6,7},{7,6},{8,9},{9,8},{10,11... | collective-permute-start | bytes 122888 | tf_op jit(solution)/shard_map/ppermute | solution.py:414
  12.3 0.0 collective-permute-done.1.refs_1_
  12.3 2.7 %filter_own.1.refs_8_ = f32[4,4,224,128]{3,2,1,0:T(8,128)S(1)} custom-call(bf16[256,256]{1,0:T(8,128)(2,1)S(1)} %get-tuple-element.53.refs_0_, bf16[256,256]{1,0:T(8,128)(2,1)S(1)} %collective-permute-done.1.refs_1_, bf16[256,256]{1,0:T(8,128)(2,1)S(1)} %get-tuple-element.54.refs_2_, bf16[256,256]{1,0:T(8,128)(2,1)S(1)} %collective-permute-done.2.refs_3_, ...), custom_call_target="tpu_custom_call" | custom-call | flops 1000 | bytes 1000 | tf_op jit(solution)/shard_map/filter_own/pallas_call | solution.py:48
  15.0 0.0 collective-permute-done.3.refs_5_
  15.0 1.3 %filter_grad.1 = (f32[2,224,128]{2,1,0:T(8,128)S(1)}, f32[4,224,128]{2,1,0:T(8,128)S(1)}, f32[80,128]{1,0:T(8,128)S(1)}, bf16[896,128]{1,0:T(8,128)(2,1)S(1)}, b...) custom-call(bf16[256,256]{1,0:T(8,128)(2,1)S(1)} %get-tuple-element.53.refs_0_, ...), custom_call_target="tpu_custom_call" | custom-call | flops 1000 | bytes 1000 | tf_op jit(solution)/shard_map/filter_grad/pallas_call | solution.py:48
  16.3 1.7 %collective-permute-start.6 = (bf16[896,128]{1,0:T(8,128)(2,1)S(1)}, bf16[896,128]{1,0:T(8,128)(2,1)S(1)}, u32[]{:S(2)}, u32[]{:S(2)}) collective-permute-start(bf16[896,128]{1,0:T(8,128)(2,1)S(1)} %get-tuple-element.61), channel_id=1, source_target_pairs={{0,8},{2,10},{4,12},{6,14},{8,0},{10,2},{12,4},{14,6},{16,24},{18,... | collective-permute-start | bytes 688136 | tf_op jit(solution)/shard_map/ppermute | solution.py:410
  18.1 3.2 %collective-permute-start.7 = (bf16[608,128]{1,0:T(8,128)(2,1)S(1)}, bf16[608,128]{1,0:T(8,128)(2,1)S(1)}, u32[]{:S(2)}, u32[]{:S(2)}) collective-permute-start(bf16[608,128]{1,0:T(8,128)(2,1)S(1)} %get-tuple-element.62), channel_id=1, source_target_pairs={{0,6},{2,4},{4,2},{6,0},{8,14},{10,12},{12,10},{14,8},{16,22},{18,... | collective-permute-start | bytes 466952 | tf_op jit(solution)/shard_map/ppermute | solution.py:410
  21.3 0.6 %collective-permute-start.9 = (bf16[608,128]{1,0:T(8,128)(2,1)S(1)}, bf16[608,128]{1,0:T(8,128)(2,1)S(1)}, u32[]{:S(2)}, u32[]{:S(2)}) collective-permute-start(bf16[608,128]{1,0:T(8,128)(2,1)S(1)} %get-tuple-element.64), channel_id=1, source_target_pairs={{0,2},{2,0},{4,6},{6,4},{8,10},{10,8},{12,14},{14,12},{16,18},{18,... | collective-permute-start | bytes 466952 | tf_op jit(solution)/shard_map/ppermute | solution.py:410
  21.9 4.0 %collective-permute-done.7.refs_4_ = bf16[608,128]{1,0:T(8,128)(2,1)S(1)} collective-permute-done((bf16[608,128]{1,0:T(8,128)(2,1)S(1)}, bf16[608,128]{1,0:T(8,128)(2,1)S(1)}, u32[]{:S(2)}, u32[]{:S(2)}) %collective-permute-start.7) | collective-permute-done | bytes 155680 | tf_op jit(solution)/shard_map/ppermute | solution.py:410
  25.8 2.7 %collective-permute-done.8.refs_5_ = bf16[608,128]{1,0:T(8,128)(2,1)S(1)} collective-permute-done((bf16[608,128]{1,0:T(8,128)(2,1)S(1)}, bf16[608,128]{1,0:T(8,128)(2,1)S(1)}, u32[]{:S(2)}, u32[]{:S(2)}) %collective-permute-start.8) | collective-permute-done | bytes 155680 | tf_op jit(solution)/shard_map/ppermute | solution.py:410
  28.5 0.1 first_sum.1
  28.7 0.5 %collective-permute-start.10 = (bf16[160,128]{1,0:T(8,128)(2,1)S(1)}, bf16[160,128]{1,0:T(8,128)(2,1)S(1)}, u32[]{:S(2)}, u32[]{:S(2)}) collective-permute-start(bf16[160,128]{1,0:T(8,128)(2,1)S(1)} %get-tuple-element.67), channel_id=1, source_target_pairs={{0,8},{2,10},{4,12},{6,14},{8,0},{10,2},{12,4},{14,6},{16,24},{18,... | collective-permute-start | bytes 122888 | tf_op jit(solution)/shard_map/ppermute | solution.py:410
  29.2 3.4 %collective-permute-start.11 = (bf16[384,128]{1,0:T(8,128)(2,1)S(1)}, bf16[384,128]{1,0:T(8,128)(2,1)S(1)}, u32[]{:S(2)}, u32[]{:S(2)}) collective-permute-start(bf16[384,128]{1,0:T(8,128)(2,1)S(1)} %get-tuple-element.68), channel_id=1, source_target_pairs={{0,24},{2,26},{4,28},{6,30},{8,16},{10,18},{12,20},{14,22},{16,8},... | collective-permute-start | bytes 294920 | tf_op jit(solution)/shard_map/ppermute | solution.py:410
  32.6 0.0 collective-permute-start.12
  32.6 1.7 %collective-permute-start.13 = (bf16[224,128]{1,0:T(8,128)(2,1)S(1)}, bf16[224,128]{1,0:T(8,128)(2,1)S(1)}, u32[]{:S(2)}, u32[]{:S(2)}) collective-permute-start(bf16[224,128]{1,0:T(8,128)(2,1)S(1)} %get-tuple-element.70), channel_id=1, source_target_pairs={{0,6},{2,4},{4,2},{6,0},{8,14},{10,12},{12,10},{14,8},{16,22},{18,... | collective-permute-start | bytes 172040 | tf_op jit(solution)/shard_map/ppermute | solution.py:410
  34.2 1.3 %collective-permute-start.14 = (bf16[224,128]{1,0:T(8,128)(2,1)S(1)}, bf16[224,128]{1,0:T(8,128)(2,1)S(1)}, u32[]{:S(2)}, u32[]{:S(2)}) collective-permute-start(bf16[224,128]{1,0:T(8,128)(2,1)S(1)} %get-tuple-element.71), channel_id=1, source_target_pairs={{0,4},{2,6},{4,0},{6,2},{8,12},{10,14},{12,8},{14,10},{16,20},{18,... | collective-permute-start | bytes 172040 | tf_op jit(solution)/shard_map/ppermute | solution.py:410
  35.5 0.0 collective-permute-done.10.refs_2_
  35.5 0.6 %collective-permute-start.15 = (bf16[224,128]{1,0:T(8,128)(2,1)S(1)}, bf16[224,128]{1,0:T(8,128)(2,1)S(1)}, u32[]{:S(2)}, u32[]{:S(2)}) collective-permute-start(bf16[224,128]{1,0:T(8,128)(2,1)S(1)} %get-tuple-element.72), channel_id=1, source_target_pairs={{0,2},{2,0},{4,6},{6,4},{8,10},{10,8},{12,14},{14,12},{16,18},{18,... | collective-permute-start | bytes 172040 | tf_op jit(solution)/shard_map/ppermute | solution.py:410
  36.1 2.0 %collective-permute-done.13.refs_6_ = bf16[224,128]{1,0:T(8,128)(2,1)S(1)} collective-permute-done((bf16[224,128]{1,0:T(8,128)(2,1)S(1)}, bf16[224,128]{1,0:T(8,128)(2,1)S(1)}, u32[]{:S(2)}, u32[]{:S(2)}) %collective-permute-start.13) | collective-permute-done | bytes 57376 | tf_op jit(solution)/shard_map/ppermute | solution.py:410
  38.1 0.5 %collective-permute-done.14.refs_7_ = bf16[224,128]{1,0:T(8,128)(2,1)S(1)} collective-permute-done((bf16[224,128]{1,0:T(8,128)(2,1)S(1)}, bf16[224,128]{1,0:T(8,128)(2,1)S(1)}, u32[]{:S(2)}, u32[]{:S(2)}) %collective-permute-start.14) | collective-permute-done | bytes 57376 | tf_op jit(solution)/shard_map/ppermute | solution.py:410
  38.6 1.1 %collective-permute-done.15.refs_8_ = bf16[224,128]{1,0:T(8,128)(2,1)S(1)} collective-permute-done((bf16[224,128]{1,0:T(8,128)(2,1)S(1)}, bf16[224,128]{1,0:T(8,128)(2,1)S(1)}, u32[]{:S(2)}, u32[]{:S(2)}) %collective-permute-start.15) | collective-permute-done | bytes 57376 | tf_op jit(solution)/shard_map/ppermute | solution.py:410
  39.7 0.0 collective-permute-done.11.refs_4_
  39.7 1.3 %collective-permute-done.12.refs_5_ = bf16[384,128]{1,0:T(8,128)(2,1)S(1)} collective-permute-done((bf16[384,128]{1,0:T(8,128)(2,1)S(1)}, bf16[384,128]{1,0:T(8,128)(2,1)S(1)}, u32[]{:S(2)}, u32[]{:S(2)}) %collective-permute-start.12) | collective-permute-done | bytes 98336 | tf_op jit(solution)/shard_map/ppermute | solution.py:410
  41.0 0.9 %last_sum.1 = (f32[64,432]{1,0:T(8,128)}, f32[32,256]{1,0:T(8,128)}, f32[4,256]{1,0:T(4,128)}, f32[8,16]{1,0:T(8,128)}) custom-call(f32[224,128]{1,0:T(8,128)S(1)} %get-tuple-element.65.refs_0_, f32[80,128]{1,0:T(8,128)S(1)} %get-tuple-element.66.refs_1_, bf16[160,128]{1,0:T(8,128)(2,1)S(1)} %collective-permute-done.10.refs_2_, ...), custom_call_target="tpu_custom_call" | custom-call | flops 1000 | bytes 1000 | tf_op jit(solution)/shard_map/last_sum/pallas_call | solution.py:48
  (6 shorter events, 0.0 us)
Async XLA Ops:
  0.6 8.5 %collective-permute-start = (bf16[512,128]{1,0:T(8,128)(2,1)}, bf16[512,128]{1,0:T(8,128)(2,1)S(1)}, u32[]{:S(2)}, u32[]{:S(2)}) collective-permute-start(bf16[512,128]{1,0:T(8,128)(2,1)} %bitcast.13), channel_id=1, source_target_pairs={{2,0},{4,2},{6,4},{8,6},{10,8},{12,10},{14,12},{16,14},{18,16},{20... | collective-permute-start | bytes 393224 | tf_op jit(solution)/shard_map/ppermute | solution.py:426
  6.1 6.3 %collective-permute-start.1 = (bf16[256,256]{1,0:T(8,128)(2,1)S(1)}, bf16[256,256]{1,0:T(8,128)(2,1)S(1)}, u32[]{:S(2)}, u32[]{:S(2)}) collective-permute-start(bf16[256,256]{1,0:T(8,128)(2,1)S(1)} %get-tuple-element.53.refs_0_), channel_id=1, source_target_pairs={{0,1},{1,0},{2,3},{3,2},{4,5},{5,4},{6,7},{7,6},{8,9},{9,8},{10,11... | collective-permute-start | bytes 393224 | tf_op jit(solution)/shard_map/ppermute | solution.py:414
  6.6 5.7 %collective-permute-start.2 = (bf16[256,256]{1,0:T(8,128)(2,1)S(1)}, bf16[256,256]{1,0:T(8,128)(2,1)S(1)}, u32[]{:S(2)}, u32[]{:S(2)}) collective-permute-start(bf16[256,256]{1,0:T(8,128)(2,1)S(1)} %get-tuple-element.54.refs_2_), channel_id=1, source_target_pairs={{0,1},{1,0},{2,3},{3,2},{4,5},{5,4},{6,7},{7,6},{8,9},{9,8},{10,11... | collective-permute-start | bytes 393224 | tf_op jit(solution)/shard_map/ppermute | solution.py:414
  6.7 5.7 %collective-permute-start.5 = (bf16[512,128]{1,0:T(8,128)(2,1)S(1)}, bf16[512,128]{1,0:T(8,128)(2,1)S(1)}, u32[]{:S(2)}, u32[]{:S(2)}) collective-permute-start(bf16[512,128]{1,0:T(8,128)(2,1)S(1)} %get-tuple-element.56.refs_4_), channel_id=1, source_target_pairs={{0,1},{1,0},{2,3},{3,2},{4,5},{5,4},{6,7},{7,6},{8,9},{9,8},{10,11... | collective-permute-start | bytes 393224 | tf_op jit(solution)/shard_map/ppermute | solution.py:414
  9.2 5.8 %collective-permute-start.3 = (bf16[512,128]{1,0:T(8,128)(2,1)S(1)}, bf16[512,128]{1,0:T(8,128)(2,1)S(1)}, u32[]{:S(2)}, u32[]{:S(2)}) collective-permute-start(bf16[512,128]{1,0:T(8,128)(2,1)S(1)} %collective-permute-done.beyond.refs_4_), channel_id=1, source_target_pairs={{0,1},{1,0},{2,3},{3,2},{4,5},{5,4},{6,7},{7,6},{8,9},{9,8},{10,11... | collective-permute-start | bytes 393224 | tf_op jit(solution)/shard_map/ppermute | solution.py:414
  11.7 3.3 %collective-permute-start.4 = (f32[80,128]{1,0:T(8,128)S(1)}, f32[80,128]{1,0:T(8,128)S(1)}, u32[]{:S(2)}, u32[]{:S(2)}) collective-permute-start(f32[80,128]{1,0:T(8,128)S(1)} %get-tuple-element.55.refs_6_), channel_id=1, source_target_pairs={{0,1},{1,0},{2,3},{3,2},{4,5},{5,4},{6,7},{7,6},{8,9},{9,8},{10,11... | collective-permute-start | bytes 122888 | tf_op jit(solution)/shard_map/ppermute | solution.py:414
  16.3 12.2 %collective-permute-start.6 = (bf16[896,128]{1,0:T(8,128)(2,1)S(1)}, bf16[896,128]{1,0:T(8,128)(2,1)S(1)}, u32[]{:S(2)}, u32[]{:S(2)}) collective-permute-start(bf16[896,128]{1,0:T(8,128)(2,1)S(1)} %get-tuple-element.61), channel_id=1, source_target_pairs={{0,8},{2,10},{4,12},{6,14},{8,0},{10,2},{12,4},{14,6},{16,24},{18,... | collective-permute-start | bytes 688136 | tf_op jit(solution)/shard_map/ppermute | solution.py:410
  18.1 7.8 %collective-permute-start.7 = (bf16[608,128]{1,0:T(8,128)(2,1)S(1)}, bf16[608,128]{1,0:T(8,128)(2,1)S(1)}, u32[]{:S(2)}, u32[]{:S(2)}) collective-permute-start(bf16[608,128]{1,0:T(8,128)(2,1)S(1)} %get-tuple-element.62), channel_id=1, source_target_pairs={{0,6},{2,4},{4,2},{6,0},{8,14},{10,12},{12,10},{14,8},{16,22},{18,... | collective-permute-start | bytes 466952 | tf_op jit(solution)/shard_map/ppermute | solution.py:410
  21.3 7.3 %collective-permute-start.8 = (bf16[608,128]{1,0:T(8,128)(2,1)S(1)}, bf16[608,128]{1,0:T(8,128)(2,1)S(1)}, u32[]{:S(2)}, u32[]{:S(2)}) collective-permute-start(bf16[608,128]{1,0:T(8,128)(2,1)S(1)} %get-tuple-element.63), channel_id=1, source_target_pairs={{0,4},{2,6},{4,0},{6,2},{8,12},{10,14},{12,8},{14,10},{16,20},{18,... | collective-permute-start | bytes 466952 | tf_op jit(solution)/shard_map/ppermute | solution.py:410
  21.3 7.3 %collective-permute-start.9 = (bf16[608,128]{1,0:T(8,128)(2,1)S(1)}, bf16[608,128]{1,0:T(8,128)(2,1)S(1)}, u32[]{:S(2)}, u32[]{:S(2)}) collective-permute-start(bf16[608,128]{1,0:T(8,128)(2,1)S(1)} %get-tuple-element.64), channel_id=1, source_target_pairs={{0,2},{2,0},{4,6},{6,4},{8,10},{10,8},{12,14},{14,12},{16,18},{18,... | collective-permute-start | bytes 466952 | tf_op jit(solution)/shard_map/ppermute | solution.py:410
  28.7 6.8 %collective-permute-start.10 = (bf16[160,128]{1,0:T(8,128)(2,1)S(1)}, bf16[160,128]{1,0:T(8,128)(2,1)S(1)}, u32[]{:S(2)}, u32[]{:S(2)}) collective-permute-start(bf16[160,128]{1,0:T(8,128)(2,1)S(1)} %get-tuple-element.67), channel_id=1, source_target_pairs={{0,8},{2,10},{4,12},{6,14},{8,0},{10,2},{12,4},{14,6},{16,24},{18,... | collective-permute-start | bytes 122888 | tf_op jit(solution)/shard_map/ppermute | solution.py:410
  29.2 10.5 %collective-permute-start.11 = (bf16[384,128]{1,0:T(8,128)(2,1)S(1)}, bf16[384,128]{1,0:T(8,128)(2,1)S(1)}, u32[]{:S(2)}, u32[]{:S(2)}) collective-permute-start(bf16[384,128]{1,0:T(8,128)(2,1)S(1)} %get-tuple-element.68), channel_id=1, source_target_pairs={{0,24},{2,26},{4,28},{6,30},{8,16},{10,18},{12,20},{14,22},{16,8},... | collective-permute-start | bytes 294920 | tf_op jit(solution)/shard_map/ppermute | solution.py:410
  32.6 8.4 %collective-permute-start.12 = (bf16[384,128]{1,0:T(8,128)(2,1)S(1)}, bf16[384,128]{1,0:T(8,128)(2,1)S(1)}, u32[]{:S(2)}, u32[]{:S(2)}) collective-permute-start(bf16[384,128]{1,0:T(8,128)(2,1)S(1)} %get-tuple-element.69), channel_id=1, source_target_pairs={{0,16},{2,18},{4,20},{6,22},{8,24},{10,26},{12,28},{14,30},{16,0},... | collective-permute-start | bytes 294920 | tf_op jit(solution)/shard_map/ppermute | solution.py:410
  32.6 5.5 %collective-permute-start.13 = (bf16[224,128]{1,0:T(8,128)(2,1)S(1)}, bf16[224,128]{1,0:T(8,128)(2,1)S(1)}, u32[]{:S(2)}, u32[]{:S(2)}) collective-permute-start(bf16[224,128]{1,0:T(8,128)(2,1)S(1)} %get-tuple-element.70), channel_id=1, source_target_pairs={{0,6},{2,4},{4,2},{6,0},{8,14},{10,12},{12,10},{14,8},{16,22},{18,... | collective-permute-start | bytes 172040 | tf_op jit(solution)/shard_map/ppermute | solution.py:410
  34.2 4.3 %collective-permute-start.14 = (bf16[224,128]{1,0:T(8,128)(2,1)S(1)}, bf16[224,128]{1,0:T(8,128)(2,1)S(1)}, u32[]{:S(2)}, u32[]{:S(2)}) collective-permute-start(bf16[224,128]{1,0:T(8,128)(2,1)S(1)} %get-tuple-element.71), channel_id=1, source_target_pairs={{0,4},{2,6},{4,0},{6,2},{8,12},{10,14},{12,8},{14,10},{16,20},{18,... | collective-permute-start | bytes 172040 | tf_op jit(solution)/shard_map/ppermute | solution.py:410
  35.5 4.2 %collective-permute-start.15 = (bf16[224,128]{1,0:T(8,128)(2,1)S(1)}, bf16[224,128]{1,0:T(8,128)(2,1)S(1)}, u32[]{:S(2)}, u32[]{:S(2)}) collective-permute-start(bf16[224,128]{1,0:T(8,128)(2,1)S(1)} %get-tuple-element.72), channel_id=1, source_target_pairs={{0,2},{2,0},{4,6},{6,4},{8,10},{10,8},{12,14},{14,12},{16,18},{18,... | collective-permute-start | bytes 172040 | tf_op jit(solution)/shard_map/ppermute | solution.py:410

commit v3 on v2

--- a/solution.py
+++ b/solution.py
@@ -57,11 +57,6 @@
         )(*args)
 
     return run
-
-
-def halves(value):
-    top = value.astype(bf16)
-    return top, (value - top.astype(f32)).astype(bf16)
 
 
 def shaped(shape, kind=f32):
@@ -302,16 +297,6 @@
                 parts.put(step, functools.reduce(lambda a, b: a + b, extra), blocks)
 
 
-def put_pair(ref, at, value):
-    top, rest = halves(value)
-    ref[at:at + value.shape[0]] = top
-    ref[at + value.shape[0]:at + 2 * value.shape[0]] = rest
-
-
-def take_pair(ref, at, length):
-    return ref[at:at + length].astype(f32) + ref[at + length:at + 2 * length].astype(f32)
-
-
 def filter_grad_body(frames, height, width, videos, near, piece, *refs):
     acts, refs = refs[:frames * videos], refs[frames * videos:]
     beyond, refs = refs[:videos], refs[videos:]
@@ -332,40 +317,42 @@
     own_line[...] = blocks[line]
     for k in range(near):
         line_send[k * piece:(k + 1) * piece] = blocks[line ^ 1, k].astype(bf16)
+    line_send[near * piece:near * piece + small.shape[0]] = small.astype(bf16)
     for k in range(far - 2):
         own_far[k] = blocks[line ^ (k + 2), place]
     for turn, send in enumerate(sends, 1):
         for k in range(far - 2):
             send[k * piece:(k + 1) * piece] = blocks[line ^ (k + 2), place ^ turn].astype(bf16)
-        put_pair(send, (far - 2) * piece, small)
+        send[(far - 2) * piece:(far - 2) * piece + small.shape[0]] = small.astype(bf16)
 
 
 def first_sum_body(near, far, entries, *refs):
     own_far, own_line, small, line_got, refs = *refs[:4], refs[4:]
     plane_got, refs = refs[:near - 1][::-1], refs[near - 1:]
-    kept, small_out, small_send, refs = *refs[:3], refs[3:]
+    kept, small_out, refs = *refs[:2], refs[2:]
     plane_sends, line_sends, total = refs[:near - 1], refs[near - 1:-1], refs[-1]
     piece = own_line.shape[1]
     count = small.shape[0]
     place = lax.axis_index("ctx") % near
-    got = [take_pair(ref, (far - 2) * piece, count) for ref in plane_got]
+    got = [ref[(far - 2) * piece:(far - 2) * piece + count].astype(f32) for ref in plane_got]
     row = lax.broadcasted_iota(jnp.int32, small.shape, 0)
     summed = jnp.where(row < entries, functools.reduce(lambda a, b: a + b, got, small[...]), got[0])
-    small_out[...] = summed
-    put_pair(small_send, 0, summed)
+    next_line = line_got[near * piece:near * piece + count]
+    small_out[...] = jnp.where(row < entries, summed + next_line.astype(f32), summed)
     for k, send in enumerate(line_sends):
         send[0:piece] = functools.reduce(
             lambda a, b: a + b[k * piece:(k + 1) * piece].astype(f32), plane_got, own_far[k]).astype(bf16)
-        put_pair(send, piece, summed)
+        send[piece:piece + count] = summed.astype(bf16)
     for k in range(near):
         total[k] = own_line[k] + line_got[k * piece:(k + 1) * piece].astype(f32)
     kept[...] = total[place]
     for turn, send in enumerate(plane_sends, 1):
-        send[...] = total[place ^ turn].astype(bf16)
+        send[0:piece] = total[place ^ turn].astype(bf16)
+        send[piece:piece + count] = next_line
 
 
 def last_sum_body(near, far, entries, *refs):
-    kept, small, small_got, lat_own, refs = *refs[:4], refs[4:]
+    kept, small, lat_own, refs = *refs[:3], refs[3:]
     line_got, plane_got, refs = refs[:far - 2], refs[far - 2:near + far - 3], refs[near + far - 3:]
     filter_grad, mod_grads, vector_grads, latent_grad = refs
     piece, lanes = kept.shape
@@ -377,7 +364,7 @@
         first, last = part * piece, min(rows, (part + 1) * piece)
         if first < last:
             filter_grad[:, first:last] = turned[part * cols:(part + 1) * cols, :last - first]
-    got = [take_pair(ref, piece, count) for ref in line_got] + [take_pair(small_got, 0, count)]
+    got = [ref[piece:piece + count].astype(f32) for ref in line_got + plane_got]
     summed = functools.reduce(lambda a, b: a + b, got, small[...])
     split, length = mod_grads.shape[0], mod_grads.shape[0] + vector_grads.shape[0]
     for k in range(mod_grads.shape[1] // lanes):
@@ -459,17 +446,17 @@
     own_far, own_line, small, line_send, *plane_sends = call(
         functools.partial(filter_grad_body, frames, height, width, videos, near, piece),
         [shaped((far - 2, piece, outs)), shaped((near, piece, outs)),
-         shaped((count_small, outs)), shaped((near * piece, outs), bf16)]
-        + [shaped(((far - 2) * piece + 2 * count_small, outs), bf16)] * (near - 1),
+         shaped((count_small, outs)), shaped((near * piece + count_small, outs), bf16)]
+        + [shaped(((far - 2) * piece + count_small, outs), bf16)] * (near - 1),
         (packs, pltpu.VMEM(blocks.shape, f32)),
         name="filter_grad",
     )(*acts_all, *beyond_all, *smalls, blocks)
     line_in = line_got([line_send], 1)
     plane_in = plane_got(plane_sends)
-    kept, small, small_send, *sends = call(
+    kept, small, *sends = call(
         functools.partial(first_sum_body, near, far, entries),
-        [shaped((piece, outs)), shaped((count_small, outs)), shaped((2 * count_small, outs), bf16)]
-        + [shaped((piece, outs), bf16)] * (near - 1) + [shaped((piece + 2 * count_small, outs), bf16)] * (far - 2),
+        [shaped((piece, outs)), shaped((count_small, outs))]
+        + [shaped((piece + count_small, outs), bf16)] * (near + far - 3),
         (pltpu.VMEM((near, piece, outs), f32),),
         name="first_sum",
     )(own_far, own_line, small, *line_in, *plane_in[::-1])
@@ -479,7 +466,7 @@
         functools.partial(last_sum_body, near, far, entries),
         (shaped((cols, rows)), shaped((2 * depth, chans)), shaped((4, chans)), shaped((cells, depth))),
         name="last_sum",
-    )(kept, small, *line_got([small_send], 1), lat_own, *line_in[::-1], *plane_in[::-1])
+    )(kept, small, lat_own, *line_in[::-1], *plane_in[::-1])
     return (
         feats_grad.reshape(features.shape),
         filter_grad.T,

time: 42 us -> 39.1 us (0.931)
  waiting for transfers between devices: 13.7 us -> 12.1 us
  starting transfers between devices: 15.8 us -> 14.4 us
    ppermute x10 -> x9, waiting for transfers between devices: 11.6 us -> 9.97 us  [along_ctx(): return lax.ppermute(value, 'ctx', [(s, target(s)) for s in range(count)])]
    ppermute x10 -> x9, starting transfers between devices: 12.9 us -> 11.5 us  [along_ctx(): return lax.ppermute(value, 'ctx', [(s, target(s)) for s in range(count)])]
  transfers between devices with their start and end apart: 16 -> 15, of which waited for: 7 -> 6; matrix products, arithmetic and copies ran while one was open for 0% -> 0% of each run, Pallas kernels for 22% -> 24%
where the time goes in v3:
time: 39.1 us; the launch traced here: 38.9 us
  starting transfers between devices  14.4 us (37%)
  waiting for transfers between devices  12.1 us (31%)
  Pallas kernels  11.7 us (30%)
  between operations  0.7 us (2%)
    pallas_call x6, Pallas kernels, run(): pl.pallas_call(full if far_args else body, out_shape=outs + [shaped(args[...  11.7 us
    ppermute x9, starting transfers between devices, along_ctx(): return lax.ppermute(value, 'ctx', [(s, target(s)) for s in range(count)])  11.5 us
    ppermute x9, waiting for transfers between devices, along_ctx(): return lax.ppermute(value, 'ctx', [(s, target(s)) for s in range(count)])  9.97 us
    ppermute x1, waiting for transfers between devices, local(): beyond = lax.ppermute(grads, 'ctx', [(s, s - 1) for s in range(1, count)])  2.08 us
    ppermute x5, starting transfers between devices, others(): lax.ppermute(value, 'vid', [(s, (s + turn) % videos) for s in range(video...  1.6 us
    ppermute x1, starting transfers between devices, local(): beyond = lax.ppermute(grads, 'ctx', [(s, s - 1) for s in range(1, count)])  1.29 us
  transfers between devices with their start and end apart: 15, of which 6 were waited for; matrix products, arithmetic and copies ran while one was open for 0% of the time, Pallas kernels for 24%

profile of v3, /device:TPU:0, one launch (start us, length us, event | category | flops | bytes accessed | tf_op | source)
XLA Modules:
  0.0 38.9 jit_solution(8844112587040788911)
XLA Ops:
  0.6 1.3 %collective-permute-start = (bf16[512,128]{1,0:T(8,128)(2,1)}, bf16[512,128]{1,0:T(8,128)(2,1)S(1)}, u32[]{:S(2)}, u32[]{:S(2)}) collective-permute-start(bf16[512,128]{1,0:T(8,128)(2,1)} %bitcast.13), channel_id=1, source_target_pairs={{2,0},{4,2},{6,4},{8,6},{10,8},{12,10},{14,12},{16,14},{18,16},{20... | collective-permute-start | bytes 393224 | tf_op jit(solution)/shard_map/ppermute | solution.py:413
  1.9 4.1 %modulate.1 = (bf16[256,256]{1,0:T(8,128)(2,1)S(1)}, bf16[256,256]{1,0:T(8,128)(2,1)S(1)}, f32[512,256]{1,0:T(8,128)S(1)}, f32[512,256]{1,0:T(8,128)S(1)}, f32[2...) custom-call(bf16[512,256]{1,0:T(8,128)(2,1)} %bitcast.12, ...), custom_call_target="tpu_custom_call" | custom-call | flops 1000 | bytes 1000 | tf_op jit(solution)/shard_map/modulate/pallas_call | solution.py:48
  6.1 0.5 %collective-permute-start.1 = (bf16[256,256]{1,0:T(8,128)(2,1)S(1)}, bf16[256,256]{1,0:T(8,128)(2,1)S(1)}, u32[]{:S(2)}, u32[]{:S(2)}) collective-permute-start(bf16[256,256]{1,0:T(8,128)(2,1)S(1)} %get-tuple-element.52.refs_0_), channel_id=1, source_target_pairs={{0,1},{1,0},{2,3},{3,2},{4,5},{5,4},{6,7},{7,6},{8,9},{9,8},{10,11... | collective-permute-start | bytes 393224 | tf_op jit(solution)/shard_map/ppermute | solution.py:401
  6.6 0.1 collective-permute-start.2
  6.7 0.4 %collective-permute-start.5 = (bf16[512,128]{1,0:T(8,128)(2,1)S(1)}, bf16[512,128]{1,0:T(8,128)(2,1)S(1)}, u32[]{:S(2)}, u32[]{:S(2)}) collective-permute-start(bf16[512,128]{1,0:T(8,128)(2,1)S(1)} %get-tuple-element.55.refs_4_), channel_id=1, source_target_pairs={{0,1},{1,0},{2,3},{3,2},{4,5},{5,4},{6,7},{7,6},{8,9},{9,8},{10,11... | collective-permute-start | bytes 393224 | tf_op jit(solution)/shard_map/ppermute | solution.py:401
  7.1 2.1 %collective-permute-done.beyond.refs_4_ = bf16[512,128]{1,0:T(8,128)(2,1)S(1)} collective-permute-done((bf16[512,128]{1,0:T(8,128)(2,1)}, bf16[512,128]{1,0:T(8,128)(2,1)S(1)}, u32[]{:S(2)}, u32[]{:S(2)}) %collective-permute-start) | collective-permute-done | bytes 131104 | tf_op jit(solution)/shard_map/ppermute | solution.py:413
  9.2 0.0 collective-permute-start.3
  9.2 2.6 %input_grad.1 = (bf16[512,256]{1,0:T(8,128)(2,1)}, f32[80,128]{1,0:T(8,128)S(1)}, f32[8,16]{1,0:T(8,128)S(1)}) custom-call(bf16[512,128]{1,0:T(8,128)(2,1)S(1)} %collective-permute-done.beyond.refs_4_, bf16[6912,128]{1,0:T(8,128)(2,1)S(1)} %get-tuple-element.40.weights, f32[512,256]{1,0:T(8,128)S(1)} %get-tuple-element.41.partial, ...), custom_call_target="tpu_custom_call" | custom-call | flops 1000 | bytes 1000 | tf_op jit(solution)/shard_map/input_grad/pallas_call | solution.py:48
  11.7 0.6 %collective-permute-start.4 = (f32[80,128]{1,0:T(8,128)S(1)}, f32[80,128]{1,0:T(8,128)S(1)}, u32[]{:S(2)}, u32[]{:S(2)}) collective-permute-start(f32[80,128]{1,0:T(8,128)S(1)} %get-tuple-element.54.refs_6_), channel_id=1, source_target_pairs={{0,1},{1,0},{2,3},{3,2},{4,5},{5,4},{6,7},{7,6},{8,9},{9,8},{10,11... | collective-permute-start | bytes 122888 | tf_op jit(solution)/shard_map/ppermute | solution.py:401
  12.3 0.0 collective-permute-done.1.refs_1_
  12.3 0.0 collective-permute-done.2.refs_3_
  12.3 0.0 collective-permute-done.5.refs_5_
  12.3 2.7 %filter_own.1.refs_8_ = f32[4,4,224,128]{3,2,1,0:T(8,128)S(1)} custom-call(bf16[256,256]{1,0:T(8,128)(2,1)S(1)} %get-tuple-element.52.refs_0_, bf16[256,256]{1,0:T(8,128)(2,1)S(1)} %collective-permute-done.1.refs_1_, bf16[256,256]{1,0:T(8,128)(2,1)S(1)} %get-tuple-element.53.refs_2_, bf16[256,256]{1,0:T(8,128)(2,1)S(1)} %collective-permute-done.2.refs_3_, ...), custom_call_target="tpu_custom_call" | custom-call | flops 1000 | bytes 1000 | tf_op jit(solution)/shard_map/filter_own/pallas_call | solution.py:48
  15.0 0.0 collective-permute-done.4.refs_7_
  15.0 0.0 collective-permute-done.3.refs_5_
  15.0 1.3 %filter_grad.1 = (f32[2,224,128]{2,1,0:T(8,128)S(1)}, f32[4,224,128]{2,1,0:T(8,128)S(1)}, f32[80,128]{1,0:T(8,128)S(1)}, bf16[976,128]{1,0:T(8,128)(2,1)S(1)}, b...) custom-call(bf16[256,256]{1,0:T(8,128)(2,1)S(1)} %get-tuple-element.52.refs_0_, ...), custom_call_target="tpu_custom_call" | custom-call | flops 1000 | bytes 1000 | tf_op jit(solution)/shard_map/filter_grad/pallas_call | solution.py:48
  16.3 1.7 %collective-permute-start.6 = (bf16[976,128]{1,0:T(8,128)(2,1)S(1)}, bf16[976,128]{1,0:T(8,128)(2,1)S(1)}, u32[]{:S(2)}, u32[]{:S(2)}) collective-permute-start(bf16[976,128]{1,0:T(8,128)(2,1)S(1)} %get-tuple-element.60), channel_id=1, source_target_pairs={{0,8},{2,10},{4,12},{6,14},{8,0},{10,2},{12,4},{14,6},{16,24},{18,... | collective-permute-start | bytes 749576 | tf_op jit(solution)/shard_map/ppermute | solution.py:397
  18.1 3.2 %collective-permute-start.7 = (bf16[528,128]{1,0:T(8,128)(2,1)S(1)}, bf16[528,128]{1,0:T(8,128)(2,1)S(1)}, u32[]{:S(2)}, u32[]{:S(2)}) collective-permute-start(bf16[528,128]{1,0:T(8,128)(2,1)S(1)} %get-tuple-element.61), channel_id=1, source_target_pairs={{0,6},{2,4},{4,2},{6,0},{8,14},{10,12},{12,10},{14,8},{16,22},{18,... | collective-permute-start | bytes 405512 | tf_op jit(solution)/shard_map/ppermute | solution.py:397
  21.3 0.0 collective-permute-start.8
  21.3 0.6 %collective-permute-start.9 = (bf16[528,128]{1,0:T(8,128)(2,1)S(1)}, bf16[528,128]{1,0:T(8,128)(2,1)S(1)}, u32[]{:S(2)}, u32[]{:S(2)}) collective-permute-start(bf16[528,128]{1,0:T(8,128)(2,1)S(1)} %get-tuple-element.63), channel_id=1, source_target_pairs={{0,2},{2,0},{4,6},{6,4},{8,10},{10,8},{12,14},{14,12},{16,18},{18,... | collective-permute-start | bytes 405512 | tf_op jit(solution)/shard_map/ppermute | solution.py:397
  21.9 3.4 %collective-permute-done.7.refs_4_ = bf16[528,128]{1,0:T(8,128)(2,1)S(1)} collective-permute-done((bf16[528,128]{1,0:T(8,128)(2,1)S(1)}, bf16[528,128]{1,0:T(8,128)(2,1)S(1)}, u32[]{:S(2)}, u32[]{:S(2)}) %collective-permute-start.7) | collective-permute-done | bytes 135200 | tf_op jit(solution)/shard_map/ppermute | solution.py:397
  25.3 2.4 %collective-permute-done.8.refs_5_ = bf16[528,128]{1,0:T(8,128)(2,1)S(1)} collective-permute-done((bf16[528,128]{1,0:T(8,128)(2,1)S(1)}, bf16[528,128]{1,0:T(8,128)(2,1)S(1)}, u32[]{:S(2)}, u32[]{:S(2)}) %collective-permute-start.8) | collective-permute-done | bytes 135200 | tf_op jit(solution)/shard_map/ppermute | solution.py:397
  27.7 0.1 first_sum.1
  27.8 2.5 %collective-permute-start.10 = (bf16[304,128]{1,0:T(8,128)(2,1)S(1)}, bf16[304,128]{1,0:T(8,128)(2,1)S(1)}, u32[]{:S(2)}, u32[]{:S(2)}) collective-permute-start(bf16[304,128]{1,0:T(8,128)(2,1)S(1)} %get-tuple-element.66), channel_id=1, source_target_pairs={{0,24},{2,26},{4,28},{6,30},{8,16},{10,18},{12,20},{14,22},{16,8},... | collective-permute-start | bytes 233480 | tf_op jit(solution)/shard_map/ppermute | solution.py:397
  30.4 0.0 collective-permute-start.11
  30.4 1.7 %collective-permute-start.12 = (bf16[304,128]{1,0:T(8,128)(2,1)S(1)}, bf16[304,128]{1,0:T(8,128)(2,1)S(1)}, u32[]{:S(2)}, u32[]{:S(2)}) collective-permute-start(bf16[304,128]{1,0:T(8,128)(2,1)S(1)} %get-tuple-element.68), channel_id=1, source_target_pairs={{0,6},{2,4},{4,2},{6,0},{8,14},{10,12},{12,10},{14,8},{16,22},{18,... | collective-permute-start | bytes 233480 | tf_op jit(solution)/shard_map/ppermute | solution.py:397
  32.1 1.5 %collective-permute-start.13 = (bf16[304,128]{1,0:T(8,128)(2,1)S(1)}, bf16[304,128]{1,0:T(8,128)(2,1)S(1)}, u32[]{:S(2)}, u32[]{:S(2)}) collective-permute-start(bf16[304,128]{1,0:T(8,128)(2,1)S(1)} %get-tuple-element.69), channel_id=1, source_target_pairs={{0,4},{2,6},{4,0},{6,2},{8,12},{10,14},{12,8},{14,10},{16,20},{18,... | collective-permute-start | bytes 233480 | tf_op jit(solution)/shard_map/ppermute | solution.py:397
  33.6 0.2 collective-permute-start.14
  33.8 0.9 %collective-permute-done.10.refs_3_ = bf16[304,128]{1,0:T(8,128)(2,1)S(1)} collective-permute-done((bf16[304,128]{1,0:T(8,128)(2,1)S(1)}, bf16[304,128]{1,0:T(8,128)(2,1)S(1)}, u32[]{:S(2)}, u32[]{:S(2)}) %collective-permute-start.10) | collective-permute-done | bytes 77856 | tf_op jit(solution)/shard_map/ppermute | solution.py:397
  34.7 3.0 %collective-permute-done.11.refs_4_ = bf16[304,128]{1,0:T(8,128)(2,1)S(1)} collective-permute-done((bf16[304,128]{1,0:T(8,128)(2,1)S(1)}, bf16[304,128]{1,0:T(8,128)(2,1)S(1)}, u32[]{:S(2)}, u32[]{:S(2)}) %collective-permute-start.11) | collective-permute-done | bytes 77856 | tf_op jit(solution)/shard_map/ppermute | solution.py:397
  37.8 0.2 collective-permute-done.14.refs_7_
  38.0 0.9 %last_sum.1 = (f32[64,432]{1,0:T(8,128)}, f32[32,256]{1,0:T(8,128)}, f32[4,256]{1,0:T(4,128)}, f32[8,16]{1,0:T(8,128)}) custom-call(f32[224,128]{1,0:T(8,128)S(1)} %get-tuple-element.64.refs_0_, f32[80,128]{1,0:T(8,128)S(1)} %get-tuple-element.65.refs_1_, f32[8,16]{1,0:T(8,128)S(1)} %get-tuple-element.56.refs_6_.refs_2_, ...), custom_call_target="tpu_custom_call" | custom-call | flops 1000 | bytes 1000 | tf_op jit(solution)/shard_map/last_sum/pallas_call | solution.py:48
  (4 shorter events, 0.0 us)
Async XLA Ops:
  0.6 8.5 %collective-permute-start = (bf16[512,128]{1,0:T(8,128)(2,1)}, bf16[512,128]{1,0:T(8,128)(2,1)S(1)}, u32[]{:S(2)}, u32[]{:S(2)}) collective-permute-start(bf16[512,128]{1,0:T(8,128)(2,1)} %bitcast.13), channel_id=1, source_target_pairs={{2,0},{4,2},{6,4},{8,6},{10,8},{12,10},{14,12},{16,14},{18,16},{20... | collective-permute-start | bytes 393224 | tf_op jit(solution)/shard_map/ppermute | solution.py:413
  6.1 6.3 %collective-permute-start.1 = (bf16[256,256]{1,0:T(8,128)(2,1)S(1)}, bf16[256,256]{1,0:T(8,128)(2,1)S(1)}, u32[]{:S(2)}, u32[]{:S(2)}) collective-permute-start(bf16[256,256]{1,0:T(8,128)(2,1)S(1)} %get-tuple-element.52.refs_0_), channel_id=1, source_target_pairs={{0,1},{1,0},{2,3},{3,2},{4,5},{5,4},{6,7},{7,6},{8,9},{9,8},{10,11... | collective-permute-start | bytes 393224 | tf_op jit(solution)/shard_map/ppermute | solution.py:401
  6.6 5.7 %collective-permute-start.2 = (bf16[256,256]{1,0:T(8,128)(2,1)S(1)}, bf16[256,256]{1,0:T(8,128)(2,1)S(1)}, u32[]{:S(2)}, u32[]{:S(2)}) collective-permute-start(bf16[256,256]{1,0:T(8,128)(2,1)S(1)} %get-tuple-element.53.refs_2_), channel_id=1, source_target_pairs={{0,1},{1,0},{2,3},{3,2},{4,5},{5,4},{6,7},{7,6},{8,9},{9,8},{10,11... | collective-permute-start | bytes 393224 | tf_op jit(solution)/shard_map/ppermute | solution.py:401
  6.7 5.7 %collective-permute-start.5 = (bf16[512,128]{1,0:T(8,128)(2,1)S(1)}, bf16[512,128]{1,0:T(8,128)(2,1)S(1)}, u32[]{:S(2)}, u32[]{:S(2)}) collective-permute-start(bf16[512,128]{1,0:T(8,128)(2,1)S(1)} %get-tuple-element.55.refs_4_), channel_id=1, source_target_pairs={{0,1},{1,0},{2,3},{3,2},{4,5},{5,4},{6,7},{7,6},{8,9},{9,8},{10,11... | collective-permute-start | bytes 393224 | tf_op jit(solution)/shard_map/ppermute | solution.py:401
  9.2 5.8 %collective-permute-start.3 = (bf16[512,128]{1,0:T(8,128)(2,1)S(1)}, bf16[512,128]{1,0:T(8,128)(2,1)S(1)}, u32[]{:S(2)}, u32[]{:S(2)}) collective-permute-start(bf16[512,128]{1,0:T(8,128)(2,1)S(1)} %collective-permute-done.beyond.refs_4_), channel_id=1, source_target_pairs={{0,1},{1,0},{2,3},{3,2},{4,5},{5,4},{6,7},{7,6},{8,9},{9,8},{10,11... | collective-permute-start | bytes 393224 | tf_op jit(solution)/shard_map/ppermute | solution.py:401
  11.7 3.3 %collective-permute-start.4 = (f32[80,128]{1,0:T(8,128)S(1)}, f32[80,128]{1,0:T(8,128)S(1)}, u32[]{:S(2)}, u32[]{:S(2)}) collective-permute-start(f32[80,128]{1,0:T(8,128)S(1)} %get-tuple-element.54.refs_6_), channel_id=1, source_target_pairs={{0,1},{1,0},{2,3},{3,2},{4,5},{5,4},{6,7},{7,6},{8,9},{9,8},{10,11... | collective-permute-start | bytes 122888 | tf_op jit(solution)/shard_map/ppermute | solution.py:401
  16.3 11.3 %collective-permute-start.6 = (bf16[976,128]{1,0:T(8,128)(2,1)S(1)}, bf16[976,128]{1,0:T(8,128)(2,1)S(1)}, u32[]{:S(2)}, u32[]{:S(2)}) collective-permute-start(bf16[976,128]{1,0:T(8,128)(2,1)S(1)} %get-tuple-element.60), channel_id=1, source_target_pairs={{0,8},{2,10},{4,12},{6,14},{8,0},{10,2},{12,4},{14,6},{16,24},{18,... | collective-permute-start | bytes 749576 | tf_op jit(solution)/shard_map/ppermute | solution.py:397
  18.1 7.2 %collective-permute-start.7 = (bf16[528,128]{1,0:T(8,128)(2,1)S(1)}, bf16[528,128]{1,0:T(8,128)(2,1)S(1)}, u32[]{:S(2)}, u32[]{:S(2)}) collective-permute-start(bf16[528,128]{1,0:T(8,128)(2,1)S(1)} %get-tuple-element.61), channel_id=1, source_target_pairs={{0,6},{2,4},{4,2},{6,0},{8,14},{10,12},{12,10},{14,8},{16,22},{18,... | collective-permute-start | bytes 405512 | tf_op jit(solution)/shard_map/ppermute | solution.py:397
  21.3 6.4 %collective-permute-start.8 = (bf16[528,128]{1,0:T(8,128)(2,1)S(1)}, bf16[528,128]{1,0:T(8,128)(2,1)S(1)}, u32[]{:S(2)}, u32[]{:S(2)}) collective-permute-start(bf16[528,128]{1,0:T(8,128)(2,1)S(1)} %get-tuple-element.62), channel_id=1, source_target_pairs={{0,4},{2,6},{4,0},{6,2},{8,12},{10,14},{12,8},{14,10},{16,20},{18,... | collective-permute-start | bytes 405512 | tf_op jit(solution)/shard_map/ppermute | solution.py:397
  21.3 6.4 %collective-permute-start.9 = (bf16[528,128]{1,0:T(8,128)(2,1)S(1)}, bf16[528,128]{1,0:T(8,128)(2,1)S(1)}, u32[]{:S(2)}, u32[]{:S(2)}) collective-permute-start(bf16[528,128]{1,0:T(8,128)(2,1)S(1)} %get-tuple-element.63), channel_id=1, source_target_pairs={{0,2},{2,0},{4,6},{6,4},{8,10},{10,8},{12,14},{14,12},{16,18},{18,... | collective-permute-start | bytes 405512 | tf_op jit(solution)/shard_map/ppermute | solution.py:397
  27.8 6.9 %collective-permute-start.10 = (bf16[304,128]{1,0:T(8,128)(2,1)S(1)}, bf16[304,128]{1,0:T(8,128)(2,1)S(1)}, u32[]{:S(2)}, u32[]{:S(2)}) collective-permute-start(bf16[304,128]{1,0:T(8,128)(2,1)S(1)} %get-tuple-element.66), channel_id=1, source_target_pairs={{0,24},{2,26},{4,28},{6,30},{8,16},{10,18},{12,20},{14,22},{16,8},... | collective-permute-start | bytes 233480 | tf_op jit(solution)/shard_map/ppermute | solution.py:397
  30.4 7.4 %collective-permute-start.11 = (bf16[304,128]{1,0:T(8,128)(2,1)S(1)}, bf16[304,128]{1,0:T(8,128)(2,1)S(1)}, u32[]{:S(2)}, u32[]{:S(2)}) collective-permute-start(bf16[304,128]{1,0:T(8,128)(2,1)S(1)} %get-tuple-element.67), channel_id=1, source_target_pairs={{0,16},{2,18},{4,20},{6,22},{8,24},{10,26},{12,28},{14,30},{16,0},... | collective-permute-start | bytes 233480 | tf_op jit(solution)/shard_map/ppermute | solution.py:397
  30.4 7.4 %collective-permute-start.12 = (bf16[304,128]{1,0:T(8,128)(2,1)S(1)}, bf16[304,128]{1,0:T(8,128)(2,1)S(1)}, u32[]{:S(2)}, u32[]{:S(2)}) collective-permute-start(bf16[304,128]{1,0:T(8,128)(2,1)S(1)} %get-tuple-element.68), channel_id=1, source_target_pairs={{0,6},{2,4},{4,2},{6,0},{8,14},{10,12},{12,10},{14,8},{16,22},{18,... | collective-permute-start | bytes 233480 | tf_op jit(solution)/shard_map/ppermute | solution.py:397
  32.1 5.7 %collective-permute-start.13 = (bf16[304,128]{1,0:T(8,128)(2,1)S(1)}, bf16[304,128]{1,0:T(8,128)(2,1)S(1)}, u32[]{:S(2)}, u32[]{:S(2)}) collective-permute-start(bf16[304,128]{1,0:T(8,128)(2,1)S(1)} %get-tuple-element.69), channel_id=1, source_target_pairs={{0,4},{2,6},{4,0},{6,2},{8,12},{10,14},{12,8},{14,10},{16,20},{18,... | collective-permute-start | bytes 233480 | tf_op jit(solution)/shard_map/ppermute | solution.py:397
  33.6 4.4 %collective-permute-start.14 = (bf16[304,128]{1,0:T(8,128)(2,1)S(1)}, bf16[304,128]{1,0:T(8,128)(2,1)S(1)}, u32[]{:S(2)}, u32[]{:S(2)}) collective-permute-start(bf16[304,128]{1,0:T(8,128)(2,1)S(1)} %get-tuple-element.70), channel_id=1, source_target_pairs={{0,2},{2,0},{4,6},{6,4},{8,10},{10,8},{12,14},{14,12},{16,18},{18,... | collective-permute-start | bytes 233480 | tf_op jit(solution)/shard_map/ppermute | solution.py:397

commit v4 on v3

--- a/solution.py
+++ b/solution.py
@@ -210,7 +210,7 @@
     lat_own[...] = jnp.where(even, first, second)
     lat_far = jnp.where(even, second, first)
     here = lax.axis_index("vid")
-    for video in range(lanes // depth):
+    for video in range(lax.axis_size("vid")):
         @pl.when(here == video)
         def _(video=video):
             small[at:at + length // 2, video * depth:(video + 1) * depth] = lat_far
@@ -328,7 +328,7 @@
 
 def first_sum_body(near, far, entries, *refs):
     own_far, own_line, small, line_got, refs = *refs[:4], refs[4:]
-    plane_got, refs = refs[:near - 1][::-1], refs[near - 1:]
+    plane_got, refs = refs[:near - 1], refs[near - 1:]
     kept, small_out, refs = *refs[:2], refs[2:]
     plane_sends, line_sends, total = refs[:near - 1], refs[near - 1:-1], refs[-1]
     piece = own_line.shape[1]
@@ -372,7 +372,7 @@
         vector_grads[:, k * lanes:(k + 1) * lanes] = summed[k * length + split:(k + 1) * length]
     cells, depth = lat_own.shape
     here = lax.axis_index("vid")
-    for video in range(lanes // depth):
+    for video in range(lax.axis_size("vid")):
         @pl.when(here == video)
         def _(video=video):
             latent_grad[...] = lat_own[...] + small[entries:entries + cells, video * depth:(video + 1) * depth]
@@ -402,8 +402,7 @@
             for turn in range(1, videos)]
 
     def plane_got(values):
-        got = {turn: along_ctx(values[turn - 1], lambda s: s ^ turn) for turn in range(near - 1, 0, -1)}
-        return [got[turn] for turn in range(1, near)]
+        return [along_ctx(value, lambda s: s ^ turn) for turn, value in enumerate(values, 1)]
 
     def line_got(values, first):
         turns = range(first, first + len(values))
@@ -459,14 +458,14 @@
         + [shaped((piece + count_small, outs), bf16)] * (near + far - 3),
         (pltpu.VMEM((near, piece, outs), f32),),
         name="first_sum",
-    )(own_far, own_line, small, *line_in, *plane_in[::-1])
+    )(own_far, own_line, small, *line_in, *plane_in)
     line_in = line_got(sends[near - 1:], 2)
     plane_in = plane_got(sends[:near - 1])
     filter_grad, mod_grads, vector_grads, latent_grad = call(
         functools.partial(last_sum_body, near, far, entries),
         (shaped((cols, rows)), shaped((2 * depth, chans)), shaped((4, chans)), shaped((cells, depth))),
         name="last_sum",
-    )(kept, small, lat_own, *line_in[::-1], *plane_in[::-1])
+    )(kept, small, lat_own, *line_in[::-1], *plane_in)
     return (
         feats_grad.reshape(features.shape),
         filter_grad.T,

time: 39.1 us -> 39 us (level)
  no operation moved by 1% of the time
where the time goes in v4:
time: 39 us; the launch traced here: 38.8 us
  starting transfers between devices  14.4 us (37%)
  waiting for transfers between devices  12 us (31%)
  Pallas kernels  11.7 us (30%)
  between operations  0.7 us (2%)
    pallas_call x6, Pallas kernels, run(): pl.pallas_call(full if far_args else body, out_shape=outs + [shaped(args[...  11.7 us
    ppermute x9, starting transfers between devices, along_ctx(): return lax.ppermute(value, 'ctx', [(s, target(s)) for s in range(count)])  11.5 us
    ppermute x9, waiting for transfers between devices, along_ctx(): return lax.ppermute(value, 'ctx', [(s, target(s)) for s in range(count)])  9.93 us
    ppermute x1, waiting for transfers between devices, local(): beyond = lax.ppermute(grads, 'ctx', [(s, s - 1) for s in range(1, count)])  2.08 us
    ppermute x5, starting transfers between devices, others(): lax.ppermute(value, 'vid', [(s, (s + turn) % videos) for s in range(video...  1.6 us
    ppermute x1, starting transfers between devices, local(): beyond = lax.ppermute(grads, 'ctx', [(s, s - 1) for s in range(1, count)])  1.29 us
  transfers between devices with their start and end apart: 15, of which 6 were waited for; matrix products, arithmetic and copies ran while one was open for 0% of the time, Pallas kernels for 24%

profile of v4, /device:TPU:0, one launch (start us, length us, event | category | flops | bytes accessed | tf_op | source)
XLA Modules:
  0.0 38.8 jit_solution(7925044027857019041)
XLA Ops:
  0.6 1.3 %collective-permute-start = (bf16[512,128]{1,0:T(8,128)(2,1)}, bf16[512,128]{1,0:T(8,128)(2,1)S(1)}, u32[]{:S(2)}, u32[]{:S(2)}) collective-permute-start(bf16[512,128]{1,0:T(8,128)(2,1)} %bitcast.13), channel_id=1, source_target_pairs={{2,0},{4,2},{6,4},{8,6},{10,8},{12,10},{14,12},{16,14},{18,16},{20... | collective-permute-start | bytes 393224 | tf_op jit(solution)/shard_map/ppermute | solution.py:412
  1.9 4.1 %modulate.1 = (bf16[256,256]{1,0:T(8,128)(2,1)S(1)}, bf16[256,256]{1,0:T(8,128)(2,1)S(1)}, f32[512,256]{1,0:T(8,128)S(1)}, f32[512,256]{1,0:T(8,128)S(1)}, f32[2...) custom-call(bf16[512,256]{1,0:T(8,128)(2,1)} %bitcast.12, ...), custom_call_target="tpu_custom_call" | custom-call | flops 1000 | bytes 1000 | tf_op jit(solution)/shard_map/modulate/pallas_call | solution.py:48
  6.1 0.5 %collective-permute-start.1 = (bf16[256,256]{1,0:T(8,128)(2,1)S(1)}, bf16[256,256]{1,0:T(8,128)(2,1)S(1)}, u32[]{:S(2)}, u32[]{:S(2)}) collective-permute-start(bf16[256,256]{1,0:T(8,128)(2,1)S(1)} %get-tuple-element.52.refs_0_), channel_id=1, source_target_pairs={{0,1},{1,0},{2,3},{3,2},{4,5},{5,4},{6,7},{7,6},{8,9},{9,8},{10,11... | collective-permute-start | bytes 393224 | tf_op jit(solution)/shard_map/ppermute | solution.py:401
  6.6 0.1 collective-permute-start.2
  6.7 0.4 %collective-permute-start.5 = (bf16[512,128]{1,0:T(8,128)(2,1)S(1)}, bf16[512,128]{1,0:T(8,128)(2,1)S(1)}, u32[]{:S(2)}, u32[]{:S(2)}) collective-permute-start(bf16[512,128]{1,0:T(8,128)(2,1)S(1)} %get-tuple-element.55.refs_4_), channel_id=1, source_target_pairs={{0,1},{1,0},{2,3},{3,2},{4,5},{5,4},{6,7},{7,6},{8,9},{9,8},{10,11... | collective-permute-start | bytes 393224 | tf_op jit(solution)/shard_map/ppermute | solution.py:401
  7.1 2.1 %collective-permute-done.beyond.refs_4_ = bf16[512,128]{1,0:T(8,128)(2,1)S(1)} collective-permute-done((bf16[512,128]{1,0:T(8,128)(2,1)}, bf16[512,128]{1,0:T(8,128)(2,1)S(1)}, u32[]{:S(2)}, u32[]{:S(2)}) %collective-permute-start) | collective-permute-done | bytes 131104 | tf_op jit(solution)/shard_map/ppermute | solution.py:412
  9.2 0.0 collective-permute-start.3
  9.2 2.6 %input_grad.1 = (bf16[512,256]{1,0:T(8,128)(2,1)}, f32[80,128]{1,0:T(8,128)S(1)}, f32[8,16]{1,0:T(8,128)S(1)}) custom-call(bf16[512,128]{1,0:T(8,128)(2,1)S(1)} %collective-permute-done.beyond.refs_4_, bf16[6912,128]{1,0:T(8,128)(2,1)S(1)} %get-tuple-element.40.weights, f32[512,256]{1,0:T(8,128)S(1)} %get-tuple-element.41.partial, ...), custom_call_target="tpu_custom_call" | custom-call | flops 1000 | bytes 1000 | tf_op jit(solution)/shard_map/input_grad/pallas_call | solution.py:48
  11.7 0.6 %collective-permute-start.4 = (f32[80,128]{1,0:T(8,128)S(1)}, f32[80,128]{1,0:T(8,128)S(1)}, u32[]{:S(2)}, u32[]{:S(2)}) collective-permute-start(f32[80,128]{1,0:T(8,128)S(1)} %get-tuple-element.54.refs_6_), channel_id=1, source_target_pairs={{0,1},{1,0},{2,3},{3,2},{4,5},{5,4},{6,7},{7,6},{8,9},{9,8},{10,11... | collective-permute-start | bytes 122888 | tf_op jit(solution)/shard_map/ppermute | solution.py:401
  12.3 0.0 collective-permute-done.1.refs_1_
  12.3 0.0 collective-permute-done.2.refs_3_
  12.3 0.0 collective-permute-done.5.refs_5_
  12.3 2.7 %filter_own.1.refs_8_ = f32[4,4,224,128]{3,2,1,0:T(8,128)S(1)} custom-call(bf16[256,256]{1,0:T(8,128)(2,1)S(1)} %get-tuple-element.52.refs_0_, bf16[256,256]{1,0:T(8,128)(2,1)S(1)} %collective-permute-done.1.refs_1_, bf16[256,256]{1,0:T(8,128)(2,1)S(1)} %get-tuple-element.53.refs_2_, bf16[256,256]{1,0:T(8,128)(2,1)S(1)} %collective-permute-done.2.refs_3_, ...), custom_call_target="tpu_custom_call" | custom-call | flops 1000 | bytes 1000 | tf_op jit(solution)/shard_map/filter_own/pallas_call | solution.py:48
  15.0 0.0 collective-permute-done.4.refs_7_
  15.0 0.0 collective-permute-done.3.refs_5_
  15.0 1.3 %filter_grad.1 = (f32[2,224,128]{2,1,0:T(8,128)S(1)}, f32[4,224,128]{2,1,0:T(8,128)S(1)}, f32[80,128]{1,0:T(8,128)S(1)}, bf16[976,128]{1,0:T(8,128)(2,1)S(1)}, b...) custom-call(bf16[256,256]{1,0:T(8,128)(2,1)S(1)} %get-tuple-element.52.refs_0_, ...), custom_call_target="tpu_custom_call" | custom-call | flops 1000 | bytes 1000 | tf_op jit(solution)/shard_map/filter_grad/pallas_call | solution.py:48
  16.3 1.7 %collective-permute-start.6 = (bf16[976,128]{1,0:T(8,128)(2,1)S(1)}, bf16[976,128]{1,0:T(8,128)(2,1)S(1)}, u32[]{:S(2)}, u32[]{:S(2)}) collective-permute-start(bf16[976,128]{1,0:T(8,128)(2,1)S(1)} %get-tuple-element.60), channel_id=1, source_target_pairs={{0,8},{2,10},{4,12},{6,14},{8,0},{10,2},{12,4},{14,6},{16,24},{18,... | collective-permute-start | bytes 749576 | tf_op jit(solution)/shard_map/ppermute | solution.py:397
  18.1 1.4 %collective-permute-start.7 = (bf16[528,128]{1,0:T(8,128)(2,1)S(1)}, bf16[528,128]{1,0:T(8,128)(2,1)S(1)}, u32[]{:S(2)}, u32[]{:S(2)}) collective-permute-start(bf16[528,128]{1,0:T(8,128)(2,1)S(1)} %get-tuple-element.61), channel_id=1, source_target_pairs={{0,2},{2,0},{4,6},{6,4},{8,10},{10,8},{12,14},{14,12},{16,18},{18,... | collective-permute-start | bytes 405512 | tf_op jit(solution)/shard_map/ppermute | solution.py:397
  19.4 2.4 %collective-permute-start.8 = (bf16[528,128]{1,0:T(8,128)(2,1)S(1)}, bf16[528,128]{1,0:T(8,128)(2,1)S(1)}, u32[]{:S(2)}, u32[]{:S(2)}) collective-permute-start(bf16[528,128]{1,0:T(8,128)(2,1)S(1)} %get-tuple-element.62), channel_id=1, source_target_pairs={{0,4},{2,6},{4,0},{6,2},{8,12},{10,14},{12,8},{14,10},{16,20},{18,... | collective-permute-start | bytes 405512 | tf_op jit(solution)/shard_map/ppermute | solution.py:397
  21.9 2.0 %collective-permute-done.7.refs_4_ = bf16[528,128]{1,0:T(8,128)(2,1)S(1)} collective-permute-done((bf16[528,128]{1,0:T(8,128)(2,1)S(1)}, bf16[528,128]{1,0:T(8,128)(2,1)S(1)}, u32[]{:S(2)}, u32[]{:S(2)}) %collective-permute-start.7) | collective-permute-done | bytes 135200 | tf_op jit(solution)/shard_map/ppermute | solution.py:397
  23.8 4.1 %collective-permute-done.8.refs_5_ = bf16[528,128]{1,0:T(8,128)(2,1)S(1)} collective-permute-done((bf16[528,128]{1,0:T(8,128)(2,1)S(1)}, bf16[528,128]{1,0:T(8,128)(2,1)S(1)}, u32[]{:S(2)}, u32[]{:S(2)}) %collective-permute-start.8) | collective-permute-done | bytes 135200 | tf_op jit(solution)/shard_map/ppermute | solution.py:397
  28.0 0.0 collective-permute-done.9.refs_6_
  28.0 0.0 collective-permute-done.6.refs_3_
  28.0 0.1 first_sum.1
  28.1 2.5 %collective-permute-start.10 = (bf16[304,128]{1,0:T(8,128)(2,1)S(1)}, bf16[304,128]{1,0:T(8,128)(2,1)S(1)}, u32[]{:S(2)}, u32[]{:S(2)}) collective-permute-start(bf16[304,128]{1,0:T(8,128)(2,1)S(1)} %get-tuple-element.66), channel_id=1, source_target_pairs={{0,24},{2,26},{4,28},{6,30},{8,16},{10,18},{12,20},{14,22},{16,8},... | collective-permute-start | bytes 233480 | tf_op jit(solution)/shard_map/ppermute | solution.py:397
  30.6 1.5 %collective-permute-start.12 = (bf16[304,128]{1,0:T(8,128)(2,1)S(1)}, bf16[304,128]{1,0:T(8,128)(2,1)S(1)}, u32[]{:S(2)}, u32[]{:S(2)}) collective-permute-start(bf16[304,128]{1,0:T(8,128)(2,1)S(1)} %get-tuple-element.68), channel_id=1, source_target_pairs={{0,2},{2,0},{4,6},{6,4},{8,10},{10,8},{12,14},{14,12},{16,18},{18,... | collective-permute-start | bytes 233480 | tf_op jit(solution)/shard_map/ppermute | solution.py:397
  32.1 0.6 %collective-permute-start.13 = (bf16[304,128]{1,0:T(8,128)(2,1)S(1)}, bf16[304,128]{1,0:T(8,128)(2,1)S(1)}, u32[]{:S(2)}, u32[]{:S(2)}) collective-permute-start(bf16[304,128]{1,0:T(8,128)(2,1)S(1)} %get-tuple-element.69), channel_id=1, source_target_pairs={{0,4},{2,6},{4,0},{6,2},{8,12},{10,14},{12,8},{14,10},{16,20},{18,... | collective-permute-start | bytes 233480 | tf_op jit(solution)/shard_map/ppermute | solution.py:397
  32.7 1.5 %collective-permute-start.14 = (bf16[304,128]{1,0:T(8,128)(2,1)S(1)}, bf16[304,128]{1,0:T(8,128)(2,1)S(1)}, u32[]{:S(2)}, u32[]{:S(2)}) collective-permute-start(bf16[304,128]{1,0:T(8,128)(2,1)S(1)} %get-tuple-element.70), channel_id=1, source_target_pairs={{0,6},{2,4},{4,2},{6,0},{8,14},{10,12},{12,10},{14,8},{16,22},{18,... | collective-permute-start | bytes 233480 | tf_op jit(solution)/shard_map/ppermute | solution.py:397
  34.1 0.3 collective-permute-done.10.refs_3_
  34.5 2.1 %collective-permute-done.11.refs_4_ = bf16[304,128]{1,0:T(8,128)(2,1)S(1)} collective-permute-done((bf16[304,128]{1,0:T(8,128)(2,1)S(1)}, bf16[304,128]{1,0:T(8,128)(2,1)S(1)}, u32[]{:S(2)}, u32[]{:S(2)}) %collective-permute-start.11) | collective-permute-done | bytes 77856 | tf_op jit(solution)/shard_map/ppermute | solution.py:397
  36.6 1.4 %collective-permute-done.14.refs_7_ = bf16[304,128]{1,0:T(8,128)(2,1)S(1)} collective-permute-done((bf16[304,128]{1,0:T(8,128)(2,1)S(1)}, bf16[304,128]{1,0:T(8,128)(2,1)S(1)}, u32[]{:S(2)}, u32[]{:S(2)}) %collective-permute-start.14) | collective-permute-done | bytes 77856 | tf_op jit(solution)/shard_map/ppermute | solution.py:397
  38.0 0.9 %last_sum.1 = (f32[64,432]{1,0:T(8,128)}, f32[32,256]{1,0:T(8,128)}, f32[4,256]{1,0:T(4,128)}, f32[8,16]{1,0:T(8,128)}) custom-call(f32[224,128]{1,0:T(8,128)S(1)} %get-tuple-element.64.refs_0_, f32[80,128]{1,0:T(8,128)S(1)} %get-tuple-element.65.refs_1_, f32[8,16]{1,0:T(8,128)S(1)} %get-tuple-element.56.refs_6_.refs_2_, ...), custom_call_target="tpu_custom_call" | custom-call | flops 1000 | bytes 1000 | tf_op jit(solution)/shard_map/last_sum/pallas_call | solution.py:48
  (4 shorter events, 0.0 us)
Async XLA Ops:
  0.6 8.5 %collective-permute-start = (bf16[512,128]{1,0:T(8,128)(2,1)}, bf16[512,128]{1,0:T(8,128)(2,1)S(1)}, u32[]{:S(2)}, u32[]{:S(2)}) collective-permute-start(bf16[512,128]{1,0:T(8,128)(2,1)} %bitcast.13), channel_id=1, source_target_pairs={{2,0},{4,2},{6,4},{8,6},{10,8},{12,10},{14,12},{16,14},{18,16},{20... | collective-permute-start | bytes 393224 | tf_op jit(solution)/shard_map/ppermute | solution.py:412
  6.1 6.3 %collective-permute-start.1 = (bf16[256,256]{1,0:T(8,128)(2,1)S(1)}, bf16[256,256]{1,0:T(8,128)(2,1)S(1)}, u32[]{:S(2)}, u32[]{:S(2)}) collective-permute-start(bf16[256,256]{1,0:T(8,128)(2,1)S(1)} %get-tuple-element.52.refs_0_), channel_id=1, source_target_pairs={{0,1},{1,0},{2,3},{3,2},{4,5},{5,4},{6,7},{7,6},{8,9},{9,8},{10,11... | collective-permute-start | bytes 393224 | tf_op jit(solution)/shard_map/ppermute | solution.py:401
  6.6 5.7 %collective-permute-start.2 = (bf16[256,256]{1,0:T(8,128)(2,1)S(1)}, bf16[256,256]{1,0:T(8,128)(2,1)S(1)}, u32[]{:S(2)}, u32[]{:S(2)}) collective-permute-start(bf16[256,256]{1,0:T(8,128)(2,1)S(1)} %get-tuple-element.53.refs_2_), channel_id=1, source_target_pairs={{0,1},{1,0},{2,3},{3,2},{4,5},{5,4},{6,7},{7,6},{8,9},{9,8},{10,11... | collective-permute-start | bytes 393224 | tf_op jit(solution)/shard_map/ppermute | solution.py:401
  6.7 5.7 %collective-permute-start.5 = (bf16[512,128]{1,0:T(8,128)(2,1)S(1)}, bf16[512,128]{1,0:T(8,128)(2,1)S(1)}, u32[]{:S(2)}, u32[]{:S(2)}) collective-permute-start(bf16[512,128]{1,0:T(8,128)(2,1)S(1)} %get-tuple-element.55.refs_4_), channel_id=1, source_target_pairs={{0,1},{1,0},{2,3},{3,2},{4,5},{5,4},{6,7},{7,6},{8,9},{9,8},{10,11... | collective-permute-start | bytes 393224 | tf_op jit(solution)/shard_map/ppermute | solution.py:401
  9.2 5.8 %collective-permute-start.3 = (bf16[512,128]{1,0:T(8,128)(2,1)S(1)}, bf16[512,128]{1,0:T(8,128)(2,1)S(1)}, u32[]{:S(2)}, u32[]{:S(2)}) collective-permute-start(bf16[512,128]{1,0:T(8,128)(2,1)S(1)} %collective-permute-done.beyond.refs_4_), channel_id=1, source_target_pairs={{0,1},{1,0},{2,3},{3,2},{4,5},{5,4},{6,7},{7,6},{8,9},{9,8},{10,11... | collective-permute-start | bytes 393224 | tf_op jit(solution)/shard_map/ppermute | solution.py:401
  11.7 3.3 %collective-permute-start.4 = (f32[80,128]{1,0:T(8,128)S(1)}, f32[80,128]{1,0:T(8,128)S(1)}, u32[]{:S(2)}, u32[]{:S(2)}) collective-permute-start(f32[80,128]{1,0:T(8,128)S(1)} %get-tuple-element.54.refs_6_), channel_id=1, source_target_pairs={{0,1},{1,0},{2,3},{3,2},{4,5},{5,4},{6,7},{7,6},{8,9},{9,8},{10,11... | collective-permute-start | bytes 122888 | tf_op jit(solution)/shard_map/ppermute | solution.py:401
  16.3 11.6 %collective-permute-start.6 = (bf16[976,128]{1,0:T(8,128)(2,1)S(1)}, bf16[976,128]{1,0:T(8,128)(2,1)S(1)}, u32[]{:S(2)}, u32[]{:S(2)}) collective-permute-start(bf16[976,128]{1,0:T(8,128)(2,1)S(1)} %get-tuple-element.60), channel_id=1, source_target_pairs={{0,8},{2,10},{4,12},{6,14},{8,0},{10,2},{12,4},{14,6},{16,24},{18,... | collective-permute-start | bytes 749576 | tf_op jit(solution)/shard_map/ppermute | solution.py:397
  18.1 5.8 %collective-permute-start.7 = (bf16[528,128]{1,0:T(8,128)(2,1)S(1)}, bf16[528,128]{1,0:T(8,128)(2,1)S(1)}, u32[]{:S(2)}, u32[]{:S(2)}) collective-permute-start(bf16[528,128]{1,0:T(8,128)(2,1)S(1)} %get-tuple-element.61), channel_id=1, source_target_pairs={{0,2},{2,0},{4,6},{6,4},{8,10},{10,8},{12,14},{14,12},{16,18},{18,... | collective-permute-start | bytes 405512 | tf_op jit(solution)/shard_map/ppermute | solution.py:397
  19.4 8.5 %collective-permute-start.8 = (bf16[528,128]{1,0:T(8,128)(2,1)S(1)}, bf16[528,128]{1,0:T(8,128)(2,1)S(1)}, u32[]{:S(2)}, u32[]{:S(2)}) collective-permute-start(bf16[528,128]{1,0:T(8,128)(2,1)S(1)} %get-tuple-element.62), channel_id=1, source_target_pairs={{0,4},{2,6},{4,0},{6,2},{8,12},{10,14},{12,8},{14,10},{16,20},{18,... | collective-permute-start | bytes 405512 | tf_op jit(solution)/shard_map/ppermute | solution.py:397
  21.8 6.1 %collective-permute-start.9 = (bf16[528,128]{1,0:T(8,128)(2,1)S(1)}, bf16[528,128]{1,0:T(8,128)(2,1)S(1)}, u32[]{:S(2)}, u32[]{:S(2)}) collective-permute-start(bf16[528,128]{1,0:T(8,128)(2,1)S(1)} %get-tuple-element.63), channel_id=1, source_target_pairs={{0,6},{2,4},{4,2},{6,0},{8,14},{10,12},{12,10},{14,8},{16,22},{18,... | collective-permute-start | bytes 405512 | tf_op jit(solution)/shard_map/ppermute | solution.py:397
  28.1 6.4 %collective-permute-start.10 = (bf16[304,128]{1,0:T(8,128)(2,1)S(1)}, bf16[304,128]{1,0:T(8,128)(2,1)S(1)}, u32[]{:S(2)}, u32[]{:S(2)}) collective-permute-start(bf16[304,128]{1,0:T(8,128)(2,1)S(1)} %get-tuple-element.66), channel_id=1, source_target_pairs={{0,24},{2,26},{4,28},{6,30},{8,16},{10,18},{12,20},{14,22},{16,8},... | collective-permute-start | bytes 233480 | tf_op jit(solution)/shard_map/ppermute | solution.py:397
  30.6 5.9 %collective-permute-start.11 = (bf16[304,128]{1,0:T(8,128)(2,1)S(1)}, bf16[304,128]{1,0:T(8,128)(2,1)S(1)}, u32[]{:S(2)}, u32[]{:S(2)}) collective-permute-start(bf16[304,128]{1,0:T(8,128)(2,1)S(1)} %get-tuple-element.67), channel_id=1, source_target_pairs={{0,16},{2,18},{4,20},{6,22},{8,24},{10,26},{12,28},{14,30},{16,0},... | collective-permute-start | bytes 233480 | tf_op jit(solution)/shard_map/ppermute | solution.py:397
  30.6 5.9 %collective-permute-start.12 = (bf16[304,128]{1,0:T(8,128)(2,1)S(1)}, bf16[304,128]{1,0:T(8,128)(2,1)S(1)}, u32[]{:S(2)}, u32[]{:S(2)}) collective-permute-start(bf16[304,128]{1,0:T(8,128)(2,1)S(1)} %get-tuple-element.68), channel_id=1, source_target_pairs={{0,2},{2,0},{4,6},{6,4},{8,10},{10,8},{12,14},{14,12},{16,18},{18,... | collective-permute-start | bytes 233480 | tf_op jit(solution)/shard_map/ppermute | solution.py:397
  32.1 4.5 %collective-permute-start.13 = (bf16[304,128]{1,0:T(8,128)(2,1)S(1)}, bf16[304,128]{1,0:T(8,128)(2,1)S(1)}, u32[]{:S(2)}, u32[]{:S(2)}) collective-permute-start(bf16[304,128]{1,0:T(8,128)(2,1)S(1)} %get-tuple-element.69), channel_id=1, source_target_pairs={{0,4},{2,6},{4,0},{6,2},{8,12},{10,14},{12,8},{14,10},{16,20},{18,... | collective-permute-start | bytes 233480 | tf_op jit(solution)/shard_map/ppermute | solution.py:397
  32.7 5.3 %collective-permute-start.14 = (bf16[304,128]{1,0:T(8,128)(2,1)S(1)}, bf16[304,128]{1,0:T(8,128)(2,1)S(1)}, u32[]{:S(2)}, u32[]{:S(2)}) collective-permute-start(bf16[304,128]{1,0:T(8,128)(2,1)S(1)} %get-tuple-element.70), channel_id=1, source_target_pairs={{0,6},{2,4},{4,2},{6,0},{8,14},{10,12},{12,10},{14,8},{16,22},{18,... | collective-permute-start | bytes 233480 | tf_op jit(solution)/shard_map/ppermute | solution.py:397

commit v5 on v4

--- a/solution.py
+++ b/solution.py
@@ -190,11 +190,20 @@
         pooled_norm += pre * normed[at, :]
     lat = latent[0, device * frames // CELL]
     depth, length = lat.shape
-    cells = cell_matrix(height, width, length)
-    shift_pool = exact(cells, pooled_shift, COLS_COLS)
-    norm_pool = exact(cells, pooled_norm, COLS_COLS)
+    bands = []
+    for field in (pooled_norm, pooled_shift):
+        for top in range(0, height, CELL):
+            rows = [field[(top + k) * width:(top + k + 1) * width] for k in range(CELL)]
+            bands.append(functools.reduce(lambda a, b: a + b, rows))
+    across = cell_matrix(1, width, width // CELL)
+    pooled = exact(across, jnp.concatenate(bands, axis=1), COLS_COLS)
+    pools = [pooled[:, k * chans:(k + 1) * chans] for k in range(len(bands))]
+    norm_pool = jnp.concatenate(pools[:len(pools) // 2], axis=0)
+    shift_pool = jnp.concatenate(pools[len(pools) // 2:], axis=0)
     scale_pool = norm_pool * gamma[...] + shift_pool * beta[...]
-    parts = [exact(lat, scale_pool, ROWS_COLS), exact(lat, shift_pool, ROWS_COLS)]
+    both = jnp.concatenate([scale_pool, shift_pool], axis=1)
+    mods = exact(lat, both, ROWS_COLS)
+    parts = [mods[:, :chans], mods[:, chans:]]
     for field in (norm_pool * tab[...], shift_pool * tab[...], scale_pool, shift_pool):
         parts.append(jnp.sum(field, axis=0, keepdims=True))
     lanes = small.shape[1]
@@ -204,7 +213,7 @@
         for part in parts:
             small[at:at + part.shape[0]] = part[:, k * lanes:(k + 1) * lanes]
             at += part.shape[0]
-    latent_sum = exact(scale_pool, ws[...], ROWS_ROWS) + exact(shift_pool, wt[...], ROWS_ROWS)
+    latent_sum = exact(both, jnp.concatenate([ws[...], wt[...]], axis=1), ROWS_ROWS)
     first, second = latent_sum[:length // 2], latent_sum[length // 2:]
     even = device % 2 == 0
     lat_own[...] = jnp.where(even, first, second)
@@ -465,7 +474,7 @@
         functools.partial(last_sum_body, near, far, entries),
         (shaped((cols, rows)), shaped((2 * depth, chans)), shaped((4, chans)), shaped((cells, depth))),
         name="last_sum",
-    )(kept, small, lat_own, *line_in[::-1], *plane_in)
+    )(kept, small, lat_own, *line_in[::-1], *plane_in[::-1])
     return (
         feats_grad.reshape(features.shape),
         filter_grad.T,

time: 39 us -> 38.5 us (0.987)
  Pallas kernels: 11.7 us -> 11.2 us
    pallas_call x6, Pallas kernels: 11.7 us -> 11.2 us  [run(): pl.pallas_call(full if far_args else body, out_shape=outs + [shaped(args[...]
  transfers between devices with their start and end apart: 15 -> 15, of which waited for: 6 -> 7; matrix products, arithmetic and copies ran while one was open for 0% -> 0% of each run, Pallas kernels for 24% -> 23%
where the time goes in v5:
time: 38.5 us; the launch traced here: 38.3 us
  starting transfers between devices  14.4 us (37%)
  waiting for transfers between devices  12 us (31%)
  Pallas kernels  11.2 us (29%)
  between operations  0.7 us (2%)
    ppermute x9, starting transfers between devices, along_ctx(): return lax.ppermute(value, 'ctx', [(s, target(s)) for s in range(count)])  11.5 us
    pallas_call x6, Pallas kernels, run(): pl.pallas_call(full if far_args else body, out_shape=outs + [shaped(args[...  11.2 us
    ppermute x9, waiting for transfers between devices, along_ctx(): return lax.ppermute(value, 'ctx', [(s, target(s)) for s in range(count)])  9.92 us
    ppermute x1, waiting for transfers between devices, local(): beyond = lax.ppermute(grads, 'ctx', [(s, s - 1) for s in range(1, count)])  2.08 us
    ppermute x5, starting transfers between devices, others(): lax.ppermute(value, 'vid', [(s, (s + turn) % videos) for s in range(video...  1.6 us
    ppermute x1, starting transfers between devices, local(): beyond = lax.ppermute(grads, 'ctx', [(s, s - 1) for s in range(1, count)])  1.29 us
  transfers between devices with their start and end apart: 15, of which 7 were waited for; matrix products, arithmetic and copies ran while one was open for 0% of the time, Pallas kernels for 23%

profile of v5, /device:TPU:0, one launch (start us, length us, event | category | flops | bytes accessed | tf_op | source)
XLA Modules:
  0.0 38.3 jit_solution(17314738929829958883)
XLA Ops:
  0.6 1.3 %collective-permute-start = (bf16[512,128]{1,0:T(8,128)(2,1)}, bf16[512,128]{1,0:T(8,128)(2,1)S(1)}, u32[]{:S(2)}, u32[]{:S(2)}) collective-permute-start(bf16[512,128]{1,0:T(8,128)(2,1)} %bitcast.13), channel_id=1, source_target_pairs={{2,0},{4,2},{6,4},{8,6},{10,8},{12,10},{14,12},{16,14},{18,16},{20... | collective-permute-start | bytes 393224 | tf_op jit(solution)/shard_map/ppermute | solution.py:421
  1.9 4.1 %modulate.1 = (bf16[256,256]{1,0:T(8,128)(2,1)S(1)}, bf16[256,256]{1,0:T(8,128)(2,1)S(1)}, f32[512,256]{1,0:T(8,128)S(1)}, f32[512,256]{1,0:T(8,128)S(1)}, f32[2...) custom-call(bf16[512,256]{1,0:T(8,128)(2,1)} %bitcast.12, ...), custom_call_target="tpu_custom_call" | custom-call | flops 1000 | bytes 1000 | tf_op jit(solution)/shard_map/modulate/pallas_call | solution.py:48
  6.1 0.5 %collective-permute-start.1 = (bf16[256,256]{1,0:T(8,128)(2,1)S(1)}, bf16[256,256]{1,0:T(8,128)(2,1)S(1)}, u32[]{:S(2)}, u32[]{:S(2)}) collective-permute-start(bf16[256,256]{1,0:T(8,128)(2,1)S(1)} %get-tuple-element.52.refs_0_), channel_id=1, source_target_pairs={{0,1},{1,0},{2,3},{3,2},{4,5},{5,4},{6,7},{7,6},{8,9},{9,8},{10,11... | collective-permute-start | bytes 393224 | tf_op jit(solution)/shard_map/ppermute | solution.py:410
  6.6 0.1 collective-permute-start.2
  6.7 0.4 %collective-permute-start.5 = (bf16[512,128]{1,0:T(8,128)(2,1)S(1)}, bf16[512,128]{1,0:T(8,128)(2,1)S(1)}, u32[]{:S(2)}, u32[]{:S(2)}) collective-permute-start(bf16[512,128]{1,0:T(8,128)(2,1)S(1)} %get-tuple-element.55.refs_4_), channel_id=1, source_target_pairs={{0,1},{1,0},{2,3},{3,2},{4,5},{5,4},{6,7},{7,6},{8,9},{9,8},{10,11... | collective-permute-start | bytes 393224 | tf_op jit(solution)/shard_map/ppermute | solution.py:410
  7.1 2.1 %collective-permute-done.beyond.refs_4_ = bf16[512,128]{1,0:T(8,128)(2,1)S(1)} collective-permute-done((bf16[512,128]{1,0:T(8,128)(2,1)}, bf16[512,128]{1,0:T(8,128)(2,1)S(1)}, u32[]{:S(2)}, u32[]{:S(2)}) %collective-permute-start) | collective-permute-done | bytes 131104 | tf_op jit(solution)/shard_map/ppermute | solution.py:421
  9.2 0.0 collective-permute-start.3
  9.2 2.1 %input_grad.1 = (bf16[512,256]{1,0:T(8,128)(2,1)}, f32[80,128]{1,0:T(8,128)S(1)}, f32[8,16]{1,0:T(8,128)S(1)}) custom-call(bf16[512,128]{1,0:T(8,128)(2,1)S(1)} %collective-permute-done.beyond.refs_4_, bf16[6912,128]{1,0:T(8,128)(2,1)S(1)} %get-tuple-element.40.weights, f32[512,256]{1,0:T(8,128)S(1)} %get-tuple-element.41.partial, ...), custom_call_target="tpu_custom_call" | custom-call | flops 1000 | bytes 1000 | tf_op jit(solution)/shard_map/input_grad/pallas_call | solution.py:48
  11.3 0.6 %collective-permute-start.4 = (f32[80,128]{1,0:T(8,128)S(1)}, f32[80,128]{1,0:T(8,128)S(1)}, u32[]{:S(2)}, u32[]{:S(2)}) collective-permute-start(f32[80,128]{1,0:T(8,128)S(1)} %get-tuple-element.54.refs_6_), channel_id=1, source_target_pairs={{0,1},{1,0},{2,3},{3,2},{4,5},{5,4},{6,7},{7,6},{8,9},{9,8},{10,11... | collective-permute-start | bytes 122888 | tf_op jit(solution)/shard_map/ppermute | solution.py:410
  11.9 0.0 collective-permute-done.1.refs_1_
  11.9 0.0 collective-permute-done.2.refs_3_
  11.9 0.0 collective-permute-done.5.refs_5_
  11.9 2.7 %filter_own.1.refs_8_ = f32[4,4,224,128]{3,2,1,0:T(8,128)S(1)} custom-call(bf16[256,256]{1,0:T(8,128)(2,1)S(1)} %get-tuple-element.52.refs_0_, bf16[256,256]{1,0:T(8,128)(2,1)S(1)} %collective-permute-done.1.refs_1_, bf16[256,256]{1,0:T(8,128)(2,1)S(1)} %get-tuple-element.53.refs_2_, bf16[256,256]{1,0:T(8,128)(2,1)S(1)} %collective-permute-done.2.refs_3_, ...), custom_call_target="tpu_custom_call" | custom-call | flops 1000 | bytes 1000 | tf_op jit(solution)/shard_map/filter_own/pallas_call | solution.py:48
  14.5 0.0 collective-permute-done.4.refs_7_
  14.6 0.0 collective-permute-done.3.refs_5_
  14.6 1.3 %filter_grad.1 = (f32[2,224,128]{2,1,0:T(8,128)S(1)}, f32[4,224,128]{2,1,0:T(8,128)S(1)}, f32[80,128]{1,0:T(8,128)S(1)}, bf16[976,128]{1,0:T(8,128)(2,1)S(1)}, b...) custom-call(bf16[256,256]{1,0:T(8,128)(2,1)S(1)} %get-tuple-element.52.refs_0_, ...), custom_call_target="tpu_custom_call" | custom-call | flops 1000 | bytes 1000 | tf_op jit(solution)/shard_map/filter_grad/pallas_call | solution.py:48
  15.9 1.7 %collective-permute-start.6 = (bf16[976,128]{1,0:T(8,128)(2,1)S(1)}, bf16[976,128]{1,0:T(8,128)(2,1)S(1)}, u32[]{:S(2)}, u32[]{:S(2)}) collective-permute-start(bf16[976,128]{1,0:T(8,128)(2,1)S(1)} %get-tuple-element.60), channel_id=1, source_target_pairs={{0,8},{2,10},{4,12},{6,14},{8,0},{10,2},{12,4},{14,6},{16,24},{18,... | collective-permute-start | bytes 749576 | tf_op jit(solution)/shard_map/ppermute | solution.py:406
  17.6 1.4 %collective-permute-start.7 = (bf16[528,128]{1,0:T(8,128)(2,1)S(1)}, bf16[528,128]{1,0:T(8,128)(2,1)S(1)}, u32[]{:S(2)}, u32[]{:S(2)}) collective-permute-start(bf16[528,128]{1,0:T(8,128)(2,1)S(1)} %get-tuple-element.61), channel_id=1, source_target_pairs={{0,2},{2,0},{4,6},{6,4},{8,10},{10,8},{12,14},{14,12},{16,18},{18,... | collective-permute-start | bytes 405512 | tf_op jit(solution)/shard_map/ppermute | solution.py:406
  19.0 2.4 %collective-permute-start.8 = (bf16[528,128]{1,0:T(8,128)(2,1)S(1)}, bf16[528,128]{1,0:T(8,128)(2,1)S(1)}, u32[]{:S(2)}, u32[]{:S(2)}) collective-permute-start(bf16[528,128]{1,0:T(8,128)(2,1)S(1)} %get-tuple-element.62), channel_id=1, source_target_pairs={{0,4},{2,6},{4,0},{6,2},{8,12},{10,14},{12,8},{14,10},{16,20},{18,... | collective-permute-start | bytes 405512 | tf_op jit(solution)/shard_map/ppermute | solution.py:406
  21.4 2.0 %collective-permute-done.7.refs_4_ = bf16[528,128]{1,0:T(8,128)(2,1)S(1)} collective-permute-done((bf16[528,128]{1,0:T(8,128)(2,1)S(1)}, bf16[528,128]{1,0:T(8,128)(2,1)S(1)}, u32[]{:S(2)}, u32[]{:S(2)}) %collective-permute-start.7) | collective-permute-done | bytes 135200 | tf_op jit(solution)/shard_map/ppermute | solution.py:406
  23.4 4.1 %collective-permute-done.8.refs_5_ = bf16[528,128]{1,0:T(8,128)(2,1)S(1)} collective-permute-done((bf16[528,128]{1,0:T(8,128)(2,1)S(1)}, bf16[528,128]{1,0:T(8,128)(2,1)S(1)}, u32[]{:S(2)}, u32[]{:S(2)}) %collective-permute-start.8) | collective-permute-done | bytes 135200 | tf_op jit(solution)/shard_map/ppermute | solution.py:406
  27.5 0.0 collective-permute-done.9.refs_6_
  27.5 0.1 first_sum.1
  27.6 2.5 %collective-permute-start.10 = (bf16[304,128]{1,0:T(8,128)(2,1)S(1)}, bf16[304,128]{1,0:T(8,128)(2,1)S(1)}, u32[]{:S(2)}, u32[]{:S(2)}) collective-permute-start(bf16[304,128]{1,0:T(8,128)(2,1)S(1)} %get-tuple-element.66), channel_id=1, source_target_pairs={{0,24},{2,26},{4,28},{6,30},{8,16},{10,18},{12,20},{14,22},{16,8},... | collective-permute-start | bytes 233480 | tf_op jit(solution)/shard_map/ppermute | solution.py:406
  30.2 1.5 %collective-permute-start.12 = (bf16[304,128]{1,0:T(8,128)(2,1)S(1)}, bf16[304,128]{1,0:T(8,128)(2,1)S(1)}, u32[]{:S(2)}, u32[]{:S(2)}) collective-permute-start(bf16[304,128]{1,0:T(8,128)(2,1)S(1)} %get-tuple-element.68), channel_id=1, source_target_pairs={{0,6},{2,4},{4,2},{6,0},{8,14},{10,12},{12,10},{14,8},{16,22},{18,... | collective-permute-start | bytes 233480 | tf_op jit(solution)/shard_map/ppermute | solution.py:406
  31.6 1.5 %collective-permute-start.13 = (bf16[304,128]{1,0:T(8,128)(2,1)S(1)}, bf16[304,128]{1,0:T(8,128)(2,1)S(1)}, u32[]{:S(2)}, u32[]{:S(2)}) collective-permute-start(bf16[304,128]{1,0:T(8,128)(2,1)S(1)} %get-tuple-element.69), channel_id=1, source_target_pairs={{0,4},{2,6},{4,0},{6,2},{8,12},{10,14},{12,8},{14,10},{16,20},{18,... | collective-permute-start | bytes 233480 | tf_op jit(solution)/shard_map/ppermute | solution.py:406
  33.1 0.6 %collective-permute-start.14 = (bf16[304,128]{1,0:T(8,128)(2,1)S(1)}, bf16[304,128]{1,0:T(8,128)(2,1)S(1)}, u32[]{:S(2)}, u32[]{:S(2)}) collective-permute-start(bf16[304,128]{1,0:T(8,128)(2,1)S(1)} %get-tuple-element.70), channel_id=1, source_target_pairs={{0,2},{2,0},{4,6},{6,4},{8,10},{10,8},{12,14},{14,12},{16,18},{18,... | collective-permute-start | bytes 233480 | tf_op jit(solution)/shard_map/ppermute | solution.py:406
  33.7 0.3 collective-permute-done.10.refs_3_
  34.0 2.1 %collective-permute-done.11.refs_4_ = bf16[304,128]{1,0:T(8,128)(2,1)S(1)} collective-permute-done((bf16[304,128]{1,0:T(8,128)(2,1)S(1)}, bf16[304,128]{1,0:T(8,128)(2,1)S(1)}, u32[]{:S(2)}, u32[]{:S(2)}) %collective-permute-start.11) | collective-permute-done | bytes 77856 | tf_op jit(solution)/shard_map/ppermute | solution.py:406
  36.1 0.2 collective-permute-done.13.refs_6_
  36.3 1.2 %collective-permute-done.14.refs_7_ = bf16[304,128]{1,0:T(8,128)(2,1)S(1)} collective-permute-done((bf16[304,128]{1,0:T(8,128)(2,1)S(1)}, bf16[304,128]{1,0:T(8,128)(2,1)S(1)}, u32[]{:S(2)}, u32[]{:S(2)}) %collective-permute-start.14) | collective-permute-done | bytes 77856 | tf_op jit(solution)/shard_map/ppermute | solution.py:406
  37.5 0.9 %last_sum.1 = (f32[64,432]{1,0:T(8,128)}, f32[32,256]{1,0:T(8,128)}, f32[4,256]{1,0:T(4,128)}, f32[8,16]{1,0:T(8,128)}) custom-call(f32[224,128]{1,0:T(8,128)S(1)} %get-tuple-element.64.refs_0_, f32[80,128]{1,0:T(8,128)S(1)} %get-tuple-element.65.refs_1_, f32[8,16]{1,0:T(8,128)S(1)} %get-tuple-element.56.refs_6_.refs_2_, ...), custom_call_target="tpu_custom_call" | custom-call | flops 1000 | bytes 1000 | tf_op jit(solution)/shard_map/last_sum/pallas_call | solution.py:48
  (4 shorter events, 0.0 us)
Async XLA Ops:
  0.6 8.5 %collective-permute-start = (bf16[512,128]{1,0:T(8,128)(2,1)}, bf16[512,128]{1,0:T(8,128)(2,1)S(1)}, u32[]{:S(2)}, u32[]{:S(2)}) collective-permute-start(bf16[512,128]{1,0:T(8,128)(2,1)} %bitcast.13), channel_id=1, source_target_pairs={{2,0},{4,2},{6,4},{8,6},{10,8},{12,10},{14,12},{16,14},{18,16},{20... | collective-permute-start | bytes 393224 | tf_op jit(solution)/shard_map/ppermute | solution.py:421
  6.1 5.8 %collective-permute-start.1 = (bf16[256,256]{1,0:T(8,128)(2,1)S(1)}, bf16[256,256]{1,0:T(8,128)(2,1)S(1)}, u32[]{:S(2)}, u32[]{:S(2)}) collective-permute-start(bf16[256,256]{1,0:T(8,128)(2,1)S(1)} %get-tuple-element.52.refs_0_), channel_id=1, source_target_pairs={{0,1},{1,0},{2,3},{3,2},{4,5},{5,4},{6,7},{7,6},{8,9},{9,8},{10,11... | collective-permute-start | bytes 393224 | tf_op jit(solution)/shard_map/ppermute | solution.py:410
  6.6 5.3 %collective-permute-start.2 = (bf16[256,256]{1,0:T(8,128)(2,1)S(1)}, bf16[256,256]{1,0:T(8,128)(2,1)S(1)}, u32[]{:S(2)}, u32[]{:S(2)}) collective-permute-start(bf16[256,256]{1,0:T(8,128)(2,1)S(1)} %get-tuple-element.53.refs_2_), channel_id=1, source_target_pairs={{0,1},{1,0},{2,3},{3,2},{4,5},{5,4},{6,7},{7,6},{8,9},{9,8},{10,11... | collective-permute-start | bytes 393224 | tf_op jit(solution)/shard_map/ppermute | solution.py:410
  6.7 5.2 %collective-permute-start.5 = (bf16[512,128]{1,0:T(8,128)(2,1)S(1)}, bf16[512,128]{1,0:T(8,128)(2,1)S(1)}, u32[]{:S(2)}, u32[]{:S(2)}) collective-permute-start(bf16[512,128]{1,0:T(8,128)(2,1)S(1)} %get-tuple-element.55.refs_4_), channel_id=1, source_target_pairs={{0,1},{1,0},{2,3},{3,2},{4,5},{5,4},{6,7},{7,6},{8,9},{9,8},{10,11... | collective-permute-start | bytes 393224 | tf_op jit(solution)/shard_map/ppermute | solution.py:410
  9.2 5.4 %collective-permute-start.3 = (bf16[512,128]{1,0:T(8,128)(2,1)S(1)}, bf16[512,128]{1,0:T(8,128)(2,1)S(1)}, u32[]{:S(2)}, u32[]{:S(2)}) collective-permute-start(bf16[512,128]{1,0:T(8,128)(2,1)S(1)} %collective-permute-done.beyond.refs_4_), channel_id=1, source_target_pairs={{0,1},{1,0},{2,3},{3,2},{4,5},{5,4},{6,7},{7,6},{8,9},{9,8},{10,11... | collective-permute-start | bytes 393224 | tf_op jit(solution)/shard_map/ppermute | solution.py:410
  11.3 3.3 %collective-permute-start.4 = (f32[80,128]{1,0:T(8,128)S(1)}, f32[80,128]{1,0:T(8,128)S(1)}, u32[]{:S(2)}, u32[]{:S(2)}) collective-permute-start(f32[80,128]{1,0:T(8,128)S(1)} %get-tuple-element.54.refs_6_), channel_id=1, source_target_pairs={{0,1},{1,0},{2,3},{3,2},{4,5},{5,4},{6,7},{7,6},{8,9},{9,8},{10,11... | collective-permute-start | bytes 122888 | tf_op jit(solution)/shard_map/ppermute | solution.py:410
  15.9 11.6 %collective-permute-start.6 = (bf16[976,128]{1,0:T(8,128)(2,1)S(1)}, bf16[976,128]{1,0:T(8,128)(2,1)S(1)}, u32[]{:S(2)}, u32[]{:S(2)}) collective-permute-start(bf16[976,128]{1,0:T(8,128)(2,1)S(1)} %get-tuple-element.60), channel_id=1, source_target_pairs={{0,8},{2,10},{4,12},{6,14},{8,0},{10,2},{12,4},{14,6},{16,24},{18,... | collective-permute-start | bytes 749576 | tf_op jit(solution)/shard_map/ppermute | solution.py:406
  17.6 5.8 %collective-permute-start.7 = (bf16[528,128]{1,0:T(8,128)(2,1)S(1)}, bf16[528,128]{1,0:T(8,128)(2,1)S(1)}, u32[]{:S(2)}, u32[]{:S(2)}) collective-permute-start(bf16[528,128]{1,0:T(8,128)(2,1)S(1)} %get-tuple-element.61), channel_id=1, source_target_pairs={{0,2},{2,0},{4,6},{6,4},{8,10},{10,8},{12,14},{14,12},{16,18},{18,... | collective-permute-start | bytes 405512 | tf_op jit(solution)/shard_map/ppermute | solution.py:406
  19.0 8.5 %collective-permute-start.8 = (bf16[528,128]{1,0:T(8,128)(2,1)S(1)}, bf16[528,128]{1,0:T(8,128)(2,1)S(1)}, u32[]{:S(2)}, u32[]{:S(2)}) collective-permute-start(bf16[528,128]{1,0:T(8,128)(2,1)S(1)} %get-tuple-element.62), channel_id=1, source_target_pairs={{0,4},{2,6},{4,0},{6,2},{8,12},{10,14},{12,8},{14,10},{16,20},{18,... | collective-permute-start | bytes 405512 | tf_op jit(solution)/shard_map/ppermute | solution.py:406
  21.4 6.1 %collective-permute-start.9 = (bf16[528,128]{1,0:T(8,128)(2,1)S(1)}, bf16[528,128]{1,0:T(8,128)(2,1)S(1)}, u32[]{:S(2)}, u32[]{:S(2)}) collective-permute-start(bf16[528,128]{1,0:T(8,128)(2,1)S(1)} %get-tuple-element.63), channel_id=1, source_target_pairs={{0,6},{2,4},{4,2},{6,0},{8,14},{10,12},{12,10},{14,8},{16,22},{18,... | collective-permute-start | bytes 405512 | tf_op jit(solution)/shard_map/ppermute | solution.py:406
  27.6 6.4 %collective-permute-start.10 = (bf16[304,128]{1,0:T(8,128)(2,1)S(1)}, bf16[304,128]{1,0:T(8,128)(2,1)S(1)}, u32[]{:S(2)}, u32[]{:S(2)}) collective-permute-start(bf16[304,128]{1,0:T(8,128)(2,1)S(1)} %get-tuple-element.66), channel_id=1, source_target_pairs={{0,24},{2,26},{4,28},{6,30},{8,16},{10,18},{12,20},{14,22},{16,8},... | collective-permute-start | bytes 233480 | tf_op jit(solution)/shard_map/ppermute | solution.py:406
  30.2 6.0 %collective-permute-start.11 = (bf16[304,128]{1,0:T(8,128)(2,1)S(1)}, bf16[304,128]{1,0:T(8,128)(2,1)S(1)}, u32[]{:S(2)}, u32[]{:S(2)}) collective-permute-start(bf16[304,128]{1,0:T(8,128)(2,1)S(1)} %get-tuple-element.67), channel_id=1, source_target_pairs={{0,16},{2,18},{4,20},{6,22},{8,24},{10,26},{12,28},{14,30},{16,0},... | collective-permute-start | bytes 233480 | tf_op jit(solution)/shard_map/ppermute | solution.py:406
  30.2 6.0 %collective-permute-start.12 = (bf16[304,128]{1,0:T(8,128)(2,1)S(1)}, bf16[304,128]{1,0:T(8,128)(2,1)S(1)}, u32[]{:S(2)}, u32[]{:S(2)}) collective-permute-start(bf16[304,128]{1,0:T(8,128)(2,1)S(1)} %get-tuple-element.68), channel_id=1, source_target_pairs={{0,6},{2,4},{4,2},{6,0},{8,14},{10,12},{12,10},{14,8},{16,22},{18,... | collective-permute-start | bytes 233480 | tf_op jit(solution)/shard_map/ppermute | solution.py:406
  31.6 4.7 %collective-permute-start.13 = (bf16[304,128]{1,0:T(8,128)(2,1)S(1)}, bf16[304,128]{1,0:T(8,128)(2,1)S(1)}, u32[]{:S(2)}, u32[]{:S(2)}) collective-permute-start(bf16[304,128]{1,0:T(8,128)(2,1)S(1)} %get-tuple-element.69), channel_id=1, source_target_pairs={{0,4},{2,6},{4,0},{6,2},{8,12},{10,14},{12,8},{14,10},{16,20},{18,... | collective-permute-start | bytes 233480 | tf_op jit(solution)/shard_map/ppermute | solution.py:406
  33.1 4.4 %collective-permute-start.14 = (bf16[304,128]{1,0:T(8,128)(2,1)S(1)}, bf16[304,128]{1,0:T(8,128)(2,1)S(1)}, u32[]{:S(2)}, u32[]{:S(2)}) collective-permute-start(bf16[304,128]{1,0:T(8,128)(2,1)S(1)} %get-tuple-element.70), channel_id=1, source_target_pairs={{0,2},{2,0},{4,6},{6,4},{8,10},{10,8},{12,14},{14,12},{16,18},{18,... | collective-permute-start | bytes 233480 | tf_op jit(solution)/shard_map/ppermute | solution.py:406

commit v6 on v5

--- a/solution.py
+++ b/solution.py
@@ -362,19 +362,17 @@
 
 def last_sum_body(near, far, entries, *refs):
     kept, small, lat_own, refs = *refs[:3], refs[3:]
-    line_got, plane_got, refs = refs[:far - 2], refs[far - 2:near + far - 3], refs[near + far - 3:]
-    filter_grad, mod_grads, vector_grads, latent_grad = refs
+    got, (filter_grad, mod_grads, vector_grads, latent_grad) = refs[:near + far - 3], refs[near + far - 3:]
     piece, lanes = kept.shape
     count = small.shape[0]
-    total = functools.reduce(lambda a, b: a + b[0:piece].astype(f32), line_got + plane_got, kept[...])
+    total = functools.reduce(lambda a, b: a + b[0:piece].astype(f32), got, kept[...])
     cols, rows = filter_grad.shape
     turned = total.T
     for part in range(lanes // cols):
         first, last = part * piece, min(rows, (part + 1) * piece)
         if first < last:
             filter_grad[:, first:last] = turned[part * cols:(part + 1) * cols, :last - first]
-    got = [ref[piece:piece + count].astype(f32) for ref in line_got + plane_got]
-    summed = functools.reduce(lambda a, b: a + b, got, small[...])
+    summed = functools.reduce(lambda a, b: a + b[piece:piece + count].astype(f32), got, small[...])
     split, length = mod_grads.shape[0], mod_grads.shape[0] + vector_grads.shape[0]
     for k in range(mod_grads.shape[1] // lanes):
         mod_grads[:, k * lanes:(k + 1) * lanes] = summed[k * length:k * length + split]
@@ -474,7 +472,7 @@
         functools.partial(last_sum_body, near, far, entries),
         (shaped((cols, rows)), shaped((2 * depth, chans)), shaped((4, chans)), shaped((cells, depth))),
         name="last_sum",
-    )(kept, small, lat_own, *line_in[::-1], *plane_in[::-1])
+    )(kept, small, lat_own, *line_in[:1], *plane_in[:2], *line_in[1:], *plane_in[2:])
     return (
         feats_grad.reshape(features.shape),
         filter_grad.T,

time: 38.5 us -> 38.9 us (1.010)
  starting transfers between devices: 14.4 us -> 14.8 us
where the time goes in v6:
time: 38.9 us; the launch traced here: 38.7 us
  starting transfers between devices  14.8 us (38%)
  waiting for transfers between devices  12 us (31%)
  Pallas kernels  11.2 us (29%)
  between operations  0.7 us (2%)
    ppermute x9, starting transfers between devices, along_ctx(): return lax.ppermute(value, 'ctx', [(s, target(s)) for s in range(count)])  11.9 us
    pallas_call x6, Pallas kernels, run(): pl.pallas_call(full if far_args else body, out_shape=outs + [shaped(args[...  11.2 us
    ppermute x9, waiting for transfers between devices, along_ctx(): return lax.ppermute(value, 'ctx', [(s, target(s)) for s in range(count)])  9.93 us
    ppermute x1, waiting for transfers between devices, local(): beyond = lax.ppermute(grads, 'ctx', [(s, s - 1) for s in range(1, count)])  2.08 us
    ppermute x5, starting transfers between devices, others(): lax.ppermute(value, 'vid', [(s, (s + turn) % videos) for s in range(video...  1.6 us
    ppermute x1, starting transfers between devices, local(): beyond = lax.ppermute(grads, 'ctx', [(s, s - 1) for s in range(1, count)])  1.29 us
  transfers between devices with their start and end apart: 15, of which 7 were waited for; matrix products, arithmetic and copies ran while one was open for 0% of the time, Pallas kernels for 23%

profile of v6, /device:TPU:0, one launch (start us, length us, event | category | flops | bytes accessed | tf_op | source)
XLA Modules:
  0.0 38.7 jit_solution(813271258930020456)
XLA Ops:
  0.6 1.3 %collective-permute-start = (bf16[512,128]{1,0:T(8,128)(2,1)}, bf16[512,128]{1,0:T(8,128)(2,1)S(1)}, u32[]{:S(2)}, u32[]{:S(2)}) collective-permute-start(bf16[512,128]{1,0:T(8,128)(2,1)} %bitcast.13), channel_id=1, source_target_pairs={{2,0},{4,2},{6,4},{8,6},{10,8},{12,10},{14,12},{16,14},{18,16},{20... | collective-permute-start | bytes 393224 | tf_op jit(solution)/shard_map/ppermute | solution.py:419
  1.9 4.1 %modulate.1 = (bf16[256,256]{1,0:T(8,128)(2,1)S(1)}, bf16[256,256]{1,0:T(8,128)(2,1)S(1)}, f32[512,256]{1,0:T(8,128)S(1)}, f32[512,256]{1,0:T(8,128)S(1)}, f32[2...) custom-call(bf16[512,256]{1,0:T(8,128)(2,1)} %bitcast.12, ...), custom_call_target="tpu_custom_call" | custom-call | flops 1000 | bytes 1000 | tf_op jit(solution)/shard_map/modulate/pallas_call | solution.py:48
  6.1 0.5 %collective-permute-start.1 = (bf16[256,256]{1,0:T(8,128)(2,1)S(1)}, bf16[256,256]{1,0:T(8,128)(2,1)S(1)}, u32[]{:S(2)}, u32[]{:S(2)}) collective-permute-start(bf16[256,256]{1,0:T(8,128)(2,1)S(1)} %get-tuple-element.52.refs_0_), channel_id=1, source_target_pairs={{0,1},{1,0},{2,3},{3,2},{4,5},{5,4},{6,7},{7,6},{8,9},{9,8},{10,11... | collective-permute-start | bytes 393224 | tf_op jit(solution)/shard_map/ppermute | solution.py:408
  6.6 0.1 collective-permute-start.2
  6.7 0.4 %collective-permute-start.5 = (bf16[512,128]{1,0:T(8,128)(2,1)S(1)}, bf16[512,128]{1,0:T(8,128)(2,1)S(1)}, u32[]{:S(2)}, u32[]{:S(2)}) collective-permute-start(bf16[512,128]{1,0:T(8,128)(2,1)S(1)} %get-tuple-element.55.refs_4_), channel_id=1, source_target_pairs={{0,1},{1,0},{2,3},{3,2},{4,5},{5,4},{6,7},{7,6},{8,9},{9,8},{10,11... | collective-permute-start | bytes 393224 | tf_op jit(solution)/shard_map/ppermute | solution.py:408
  7.1 2.1 %collective-permute-done.beyond.refs_4_ = bf16[512,128]{1,0:T(8,128)(2,1)S(1)} collective-permute-done((bf16[512,128]{1,0:T(8,128)(2,1)}, bf16[512,128]{1,0:T(8,128)(2,1)S(1)}, u32[]{:S(2)}, u32[]{:S(2)}) %collective-permute-start) | collective-permute-done | bytes 131104 | tf_op jit(solution)/shard_map/ppermute | solution.py:419
  9.2 0.0 collective-permute-start.3
  9.2 2.1 %input_grad.1 = (bf16[512,256]{1,0:T(8,128)(2,1)}, f32[80,128]{1,0:T(8,128)S(1)}, f32[8,16]{1,0:T(8,128)S(1)}) custom-call(bf16[512,128]{1,0:T(8,128)(2,1)S(1)} %collective-permute-done.beyond.refs_4_, bf16[6912,128]{1,0:T(8,128)(2,1)S(1)} %get-tuple-element.40.weights, f32[512,256]{1,0:T(8,128)S(1)} %get-tuple-element.41.partial, ...), custom_call_target="tpu_custom_call" | custom-call | flops 1000 | bytes 1000 | tf_op jit(solution)/shard_map/input_grad/pallas_call | solution.py:48
  11.3 0.6 %collective-permute-start.4 = (f32[80,128]{1,0:T(8,128)S(1)}, f32[80,128]{1,0:T(8,128)S(1)}, u32[]{:S(2)}, u32[]{:S(2)}) collective-permute-start(f32[80,128]{1,0:T(8,128)S(1)} %get-tuple-element.54.refs_6_), channel_id=1, source_target_pairs={{0,1},{1,0},{2,3},{3,2},{4,5},{5,4},{6,7},{7,6},{8,9},{9,8},{10,11... | collective-permute-start | bytes 122888 | tf_op jit(solution)/shard_map/ppermute | solution.py:408
  11.9 0.0 collective-permute-done.1.refs_1_
  11.9 0.0 collective-permute-done.2.refs_3_
  11.9 0.0 collective-permute-done.5.refs_5_
  11.9 2.7 %filter_own.1.refs_8_ = f32[4,4,224,128]{3,2,1,0:T(8,128)S(1)} custom-call(bf16[256,256]{1,0:T(8,128)(2,1)S(1)} %get-tuple-element.52.refs_0_, bf16[256,256]{1,0:T(8,128)(2,1)S(1)} %collective-permute-done.1.refs_1_, bf16[256,256]{1,0:T(8,128)(2,1)S(1)} %get-tuple-element.53.refs_2_, bf16[256,256]{1,0:T(8,128)(2,1)S(1)} %collective-permute-done.2.refs_3_, ...), custom_call_target="tpu_custom_call" | custom-call | flops 1000 | bytes 1000 | tf_op jit(solution)/shard_map/filter_own/pallas_call | solution.py:48
  14.5 0.0 collective-permute-done.4.refs_7_
  14.6 1.3 %filter_grad.1 = (f32[2,224,128]{2,1,0:T(8,128)S(1)}, f32[4,224,128]{2,1,0:T(8,128)S(1)}, f32[80,128]{1,0:T(8,128)S(1)}, bf16[976,128]{1,0:T(8,128)(2,1)S(1)}, b...) custom-call(bf16[256,256]{1,0:T(8,128)(2,1)S(1)} %get-tuple-element.52.refs_0_, ...), custom_call_target="tpu_custom_call" | custom-call | flops 1000 | bytes 1000 | tf_op jit(solution)/shard_map/filter_grad/pallas_call | solution.py:48
  15.9 1.7 %collective-permute-start.6 = (bf16[976,128]{1,0:T(8,128)(2,1)S(1)}, bf16[976,128]{1,0:T(8,128)(2,1)S(1)}, u32[]{:S(2)}, u32[]{:S(2)}) collective-permute-start(bf16[976,128]{1,0:T(8,128)(2,1)S(1)} %get-tuple-element.60), channel_id=1, source_target_pairs={{0,8},{2,10},{4,12},{6,14},{8,0},{10,2},{12,4},{14,6},{16,24},{18,... | collective-permute-start | bytes 749576 | tf_op jit(solution)/shard_map/ppermute | solution.py:404
  17.6 1.4 %collective-permute-start.7 = (bf16[528,128]{1,0:T(8,128)(2,1)S(1)}, bf16[528,128]{1,0:T(8,128)(2,1)S(1)}, u32[]{:S(2)}, u32[]{:S(2)}) collective-permute-start(bf16[528,128]{1,0:T(8,128)(2,1)S(1)} %get-tuple-element.61), channel_id=1, source_target_pairs={{0,2},{2,0},{4,6},{6,4},{8,10},{10,8},{12,14},{14,12},{16,18},{18,... | collective-permute-start | bytes 405512 | tf_op jit(solution)/shard_map/ppermute | solution.py:404
  19.0 2.4 %collective-permute-start.8 = (bf16[528,128]{1,0:T(8,128)(2,1)S(1)}, bf16[528,128]{1,0:T(8,128)(2,1)S(1)}, u32[]{:S(2)}, u32[]{:S(2)}) collective-permute-start(bf16[528,128]{1,0:T(8,128)(2,1)S(1)} %get-tuple-element.62), channel_id=1, source_target_pairs={{0,4},{2,6},{4,0},{6,2},{8,12},{10,14},{12,8},{14,10},{16,20},{18,... | collective-permute-start | bytes 405512 | tf_op jit(solution)/shard_map/ppermute | solution.py:404
  21.4 2.0 %collective-permute-done.7.refs_4_ = bf16[528,128]{1,0:T(8,128)(2,1)S(1)} collective-permute-done((bf16[528,128]{1,0:T(8,128)(2,1)S(1)}, bf16[528,128]{1,0:T(8,128)(2,1)S(1)}, u32[]{:S(2)}, u32[]{:S(2)}) %collective-permute-start.7) | collective-permute-done | bytes 135200 | tf_op jit(solution)/shard_map/ppermute | solution.py:404
  23.4 4.1 %collective-permute-done.8.refs_5_ = bf16[528,128]{1,0:T(8,128)(2,1)S(1)} collective-permute-done((bf16[528,128]{1,0:T(8,128)(2,1)S(1)}, bf16[528,128]{1,0:T(8,128)(2,1)S(1)}, u32[]{:S(2)}, u32[]{:S(2)}) %collective-permute-start.8) | collective-permute-done | bytes 135200 | tf_op jit(solution)/shard_map/ppermute | solution.py:404
  27.5 0.0 collective-permute-done.9.refs_6_
  27.5 0.1 first_sum.1
  27.6 2.1 %collective-permute-start.10 = (bf16[304,128]{1,0:T(8,128)(2,1)S(1)}, bf16[304,128]{1,0:T(8,128)(2,1)S(1)}, u32[]{:S(2)}, u32[]{:S(2)}) collective-permute-start(bf16[304,128]{1,0:T(8,128)(2,1)S(1)} %get-tuple-element.66), channel_id=1, source_target_pairs={{0,16},{2,18},{4,20},{6,22},{8,24},{10,26},{12,28},{14,30},{16,0},... | collective-permute-start | bytes 233480 | tf_op jit(solution)/shard_map/ppermute | solution.py:404
  29.7 0.9 %collective-permute-start.11 = (bf16[304,128]{1,0:T(8,128)(2,1)S(1)}, bf16[304,128]{1,0:T(8,128)(2,1)S(1)}, u32[]{:S(2)}, u32[]{:S(2)}) collective-permute-start(bf16[304,128]{1,0:T(8,128)(2,1)S(1)} %get-tuple-element.67), channel_id=1, source_target_pairs={{0,2},{2,0},{4,6},{6,4},{8,10},{10,8},{12,14},{14,12},{16,18},{18,... | collective-permute-start | bytes 233480 | tf_op jit(solution)/shard_map/ppermute | solution.py:404
  30.6 0.7 %collective-permute-start.12 = (bf16[304,128]{1,0:T(8,128)(2,1)S(1)}, bf16[304,128]{1,0:T(8,128)(2,1)S(1)}, u32[]{:S(2)}, u32[]{:S(2)}) collective-permute-start(bf16[304,128]{1,0:T(8,128)(2,1)S(1)} %get-tuple-element.68), channel_id=1, source_target_pairs={{0,4},{2,6},{4,0},{6,2},{8,12},{10,14},{12,8},{14,10},{16,20},{18,... | collective-permute-start | bytes 233480 | tf_op jit(solution)/shard_map/ppermute | solution.py:404
  31.3 1.2 %collective-permute-start.13 = (bf16[304,128]{1,0:T(8,128)(2,1)S(1)}, bf16[304,128]{1,0:T(8,128)(2,1)S(1)}, u32[]{:S(2)}, u32[]{:S(2)}) collective-permute-start(bf16[304,128]{1,0:T(8,128)(2,1)S(1)} %get-tuple-element.69), channel_id=1, source_target_pairs={{0,24},{2,26},{4,28},{6,30},{8,16},{10,18},{12,20},{14,22},{16,8},... | collective-permute-start | bytes 233480 | tf_op jit(solution)/shard_map/ppermute | solution.py:404
  32.5 1.5 %collective-permute-start.14 = (bf16[304,128]{1,0:T(8,128)(2,1)S(1)}, bf16[304,128]{1,0:T(8,128)(2,1)S(1)}, u32[]{:S(2)}, u32[]{:S(2)}) collective-permute-start(bf16[304,128]{1,0:T(8,128)(2,1)S(1)} %get-tuple-element.70), channel_id=1, source_target_pairs={{0,6},{2,4},{4,2},{6,0},{8,14},{10,12},{12,10},{14,8},{16,22},{18,... | collective-permute-start | bytes 233480 | tf_op jit(solution)/shard_map/ppermute | solution.py:404
  34.0 1.3 %collective-permute-done.10.refs_3_ = bf16[304,128]{1,0:T(8,128)(2,1)S(1)} collective-permute-done((bf16[304,128]{1,0:T(8,128)(2,1)S(1)}, bf16[304,128]{1,0:T(8,128)(2,1)S(1)}, u32[]{:S(2)}, u32[]{:S(2)}) %collective-permute-start.10) | collective-permute-done | bytes 77856 | tf_op jit(solution)/shard_map/ppermute | solution.py:404
  35.3 0.3 collective-permute-done.12.refs_5_
  35.6 1.9 %collective-permute-done.13.refs_6_ = bf16[304,128]{1,0:T(8,128)(2,1)S(1)} collective-permute-done((bf16[304,128]{1,0:T(8,128)(2,1)S(1)}, bf16[304,128]{1,0:T(8,128)(2,1)S(1)}, u32[]{:S(2)}, u32[]{:S(2)}) %collective-permute-start.13) | collective-permute-done | bytes 77856 | tf_op jit(solution)/shard_map/ppermute | solution.py:404
  37.5 0.3 collective-permute-done.14.refs_7_
  37.8 0.9 %last_sum.1 = (f32[64,432]{1,0:T(8,128)}, f32[32,256]{1,0:T(8,128)}, f32[4,256]{1,0:T(4,128)}, f32[8,16]{1,0:T(8,128)}) custom-call(f32[224,128]{1,0:T(8,128)S(1)} %get-tuple-element.64.refs_0_, f32[80,128]{1,0:T(8,128)S(1)} %get-tuple-element.65.refs_1_, f32[8,16]{1,0:T(8,128)S(1)} %get-tuple-element.56.refs_6_.refs_2_, ...), custom_call_target="tpu_custom_call" | custom-call | flops 1000 | bytes 1000 | tf_op jit(solution)/shard_map/last_sum/pallas_call | solution.py:48
  (4 shorter events, 0.0 us)
Async XLA Ops:
  0.6 8.5 %collective-permute-start = (bf16[512,128]{1,0:T(8,128)(2,1)}, bf16[512,128]{1,0:T(8,128)(2,1)S(1)}, u32[]{:S(2)}, u32[]{:S(2)}) collective-permute-start(bf16[512,128]{1,0:T(8,128)(2,1)} %bitcast.13), channel_id=1, source_target_pairs={{2,0},{4,2},{6,4},{8,6},{10,8},{12,10},{14,12},{16,14},{18,16},{20... | collective-permute-start | bytes 393224 | tf_op jit(solution)/shard_map/ppermute | solution.py:419
  6.1 5.8 %collective-permute-start.1 = (bf16[256,256]{1,0:T(8,128)(2,1)S(1)}, bf16[256,256]{1,0:T(8,128)(2,1)S(1)}, u32[]{:S(2)}, u32[]{:S(2)}) collective-permute-start(bf16[256,256]{1,0:T(8,128)(2,1)S(1)} %get-tuple-element.52.refs_0_), channel_id=1, source_target_pairs={{0,1},{1,0},{2,3},{3,2},{4,5},{5,4},{6,7},{7,6},{8,9},{9,8},{10,11... | collective-permute-start | bytes 393224 | tf_op jit(solution)/shard_map/ppermute | solution.py:408
  6.6 5.3 %collective-permute-start.2 = (bf16[256,256]{1,0:T(8,128)(2,1)S(1)}, bf16[256,256]{1,0:T(8,128)(2,1)S(1)}, u32[]{:S(2)}, u32[]{:S(2)}) collective-permute-start(bf16[256,256]{1,0:T(8,128)(2,1)S(1)} %get-tuple-element.53.refs_2_), channel_id=1, source_target_pairs={{0,1},{1,0},{2,3},{3,2},{4,5},{5,4},{6,7},{7,6},{8,9},{9,8},{10,11... | collective-permute-start | bytes 393224 | tf_op jit(solution)/shard_map/ppermute | solution.py:408
  6.7 5.2 %collective-permute-start.5 = (bf16[512,128]{1,0:T(8,128)(2,1)S(1)}, bf16[512,128]{1,0:T(8,128)(2,1)S(1)}, u32[]{:S(2)}, u32[]{:S(2)}) collective-permute-start(bf16[512,128]{1,0:T(8,128)(2,1)S(1)} %get-tuple-element.55.refs_4_), channel_id=1, source_target_pairs={{0,1},{1,0},{2,3},{3,2},{4,5},{5,4},{6,7},{7,6},{8,9},{9,8},{10,11... | collective-permute-start | bytes 393224 | tf_op jit(solution)/shard_map/ppermute | solution.py:408
  9.2 5.4 %collective-permute-start.3 = (bf16[512,128]{1,0:T(8,128)(2,1)S(1)}, bf16[512,128]{1,0:T(8,128)(2,1)S(1)}, u32[]{:S(2)}, u32[]{:S(2)}) collective-permute-start(bf16[512,128]{1,0:T(8,128)(2,1)S(1)} %collective-permute-done.beyond.refs_4_), channel_id=1, source_target_pairs={{0,1},{1,0},{2,3},{3,2},{4,5},{5,4},{6,7},{7,6},{8,9},{9,8},{10,11... | collective-permute-start | bytes 393224 | tf_op jit(solution)/shard_map/ppermute | solution.py:408
  11.3 3.3 %collective-permute-start.4 = (f32[80,128]{1,0:T(8,128)S(1)}, f32[80,128]{1,0:T(8,128)S(1)}, u32[]{:S(2)}, u32[]{:S(2)}) collective-permute-start(f32[80,128]{1,0:T(8,128)S(1)} %get-tuple-element.54.refs_6_), channel_id=1, source_target_pairs={{0,1},{1,0},{2,3},{3,2},{4,5},{5,4},{6,7},{7,6},{8,9},{9,8},{10,11... | collective-permute-start | bytes 122888 | tf_op jit(solution)/shard_map/ppermute | solution.py:408
  15.9 11.6 %collective-permute-start.6 = (bf16[976,128]{1,0:T(8,128)(2,1)S(1)}, bf16[976,128]{1,0:T(8,128)(2,1)S(1)}, u32[]{:S(2)}, u32[]{:S(2)}) collective-permute-start(bf16[976,128]{1,0:T(8,128)(2,1)S(1)} %get-tuple-element.60), channel_id=1, source_target_pairs={{0,8},{2,10},{4,12},{6,14},{8,0},{10,2},{12,4},{14,6},{16,24},{18,... | collective-permute-start | bytes 749576 | tf_op jit(solution)/shard_map/ppermute | solution.py:404
  17.6 5.8 %collective-permute-start.7 = (bf16[528,128]{1,0:T(8,128)(2,1)S(1)}, bf16[528,128]{1,0:T(8,128)(2,1)S(1)}, u32[]{:S(2)}, u32[]{:S(2)}) collective-permute-start(bf16[528,128]{1,0:T(8,128)(2,1)S(1)} %get-tuple-element.61), channel_id=1, source_target_pairs={{0,2},{2,0},{4,6},{6,4},{8,10},{10,8},{12,14},{14,12},{16,18},{18,... | collective-permute-start | bytes 405512 | tf_op jit(solution)/shard_map/ppermute | solution.py:404
  19.0 8.5 %collective-permute-start.8 = (bf16[528,128]{1,0:T(8,128)(2,1)S(1)}, bf16[528,128]{1,0:T(8,128)(2,1)S(1)}, u32[]{:S(2)}, u32[]{:S(2)}) collective-permute-start(bf16[528,128]{1,0:T(8,128)(2,1)S(1)} %get-tuple-element.62), channel_id=1, source_target_pairs={{0,4},{2,6},{4,0},{6,2},{8,12},{10,14},{12,8},{14,10},{16,20},{18,... | collective-permute-start | bytes 405512 | tf_op jit(solution)/shard_map/ppermute | solution.py:404
  21.4 6.1 %collective-permute-start.9 = (bf16[528,128]{1,0:T(8,128)(2,1)S(1)}, bf16[528,128]{1,0:T(8,128)(2,1)S(1)}, u32[]{:S(2)}, u32[]{:S(2)}) collective-permute-start(bf16[528,128]{1,0:T(8,128)(2,1)S(1)} %get-tuple-element.63), channel_id=1, source_target_pairs={{0,6},{2,4},{4,2},{6,0},{8,14},{10,12},{12,10},{14,8},{16,22},{18,... | collective-permute-start | bytes 405512 | tf_op jit(solution)/shard_map/ppermute | solution.py:404
  27.6 7.7 %collective-permute-start.10 = (bf16[304,128]{1,0:T(8,128)(2,1)S(1)}, bf16[304,128]{1,0:T(8,128)(2,1)S(1)}, u32[]{:S(2)}, u32[]{:S(2)}) collective-permute-start(bf16[304,128]{1,0:T(8,128)(2,1)S(1)} %get-tuple-element.66), channel_id=1, source_target_pairs={{0,16},{2,18},{4,20},{6,22},{8,24},{10,26},{12,28},{14,30},{16,0},... | collective-permute-start | bytes 233480 | tf_op jit(solution)/shard_map/ppermute | solution.py:404
  29.7 5.7 %collective-permute-start.11 = (bf16[304,128]{1,0:T(8,128)(2,1)S(1)}, bf16[304,128]{1,0:T(8,128)(2,1)S(1)}, u32[]{:S(2)}, u32[]{:S(2)}) collective-permute-start(bf16[304,128]{1,0:T(8,128)(2,1)S(1)} %get-tuple-element.67), channel_id=1, source_target_pairs={{0,2},{2,0},{4,6},{6,4},{8,10},{10,8},{12,14},{14,12},{16,18},{18,... | collective-permute-start | bytes 233480 | tf_op jit(solution)/shard_map/ppermute | solution.py:404
  30.6 5.0 %collective-permute-start.12 = (bf16[304,128]{1,0:T(8,128)(2,1)S(1)}, bf16[304,128]{1,0:T(8,128)(2,1)S(1)}, u32[]{:S(2)}, u32[]{:S(2)}) collective-permute-start(bf16[304,128]{1,0:T(8,128)(2,1)S(1)} %get-tuple-element.68), channel_id=1, source_target_pairs={{0,4},{2,6},{4,0},{6,2},{8,12},{10,14},{12,8},{14,10},{16,20},{18,... | collective-permute-start | bytes 233480 | tf_op jit(solution)/shard_map/ppermute | solution.py:404
  31.3 6.2 %collective-permute-start.13 = (bf16[304,128]{1,0:T(8,128)(2,1)S(1)}, bf16[304,128]{1,0:T(8,128)(2,1)S(1)}, u32[]{:S(2)}, u32[]{:S(2)}) collective-permute-start(bf16[304,128]{1,0:T(8,128)(2,1)S(1)} %get-tuple-element.69), channel_id=1, source_target_pairs={{0,24},{2,26},{4,28},{6,30},{8,16},{10,18},{12,20},{14,22},{16,8},... | collective-permute-start | bytes 233480 | tf_op jit(solution)/shard_map/ppermute | solution.py:404
  32.5 5.3 %collective-permute-start.14 = (bf16[304,128]{1,0:T(8,128)(2,1)S(1)}, bf16[304,128]{1,0:T(8,128)(2,1)S(1)}, u32[]{:S(2)}, u32[]{:S(2)}) collective-permute-start(bf16[304,128]{1,0:T(8,128)(2,1)S(1)} %get-tuple-element.70), channel_id=1, source_target_pairs={{0,6},{2,4},{4,2},{6,0},{8,14},{10,12},{12,10},{14,8},{16,22},{18,... | collective-permute-start | bytes 233480 | tf_op jit(solution)/shard_map/ppermute | solution.py:404
